TPU v7x, 32 devices: a whole 2x2x4 slice. The times are simulated.
32 devices in a mesh: rep: 2 (over core), fsdp: 16 (over z, y, x).
Axes of the slice: x: 2, y: 2, z: 4, core: 2. Of those that a mesh axis runs over, the one named last changes fastest.
Arguments:
- inputs: bfloat16 [32, 1024, 768], P(('rep', 'fsdp')), may hold values from -6 to 6
- cotangent: bfloat16 [32, 1024, 768], P(('rep', 'fsdp')), may hold values from -6 to 6
- seg_sizes: int32 [32, 8], P(('rep', 'fsdp')), may hold values from 0 to 1024, as said below
- seq_lengths: int32 [32, 8], P(('rep', 'fsdp')), may hold values from 0 to 1024, as said below
- timesteps: int32 [32, 8], P(('rep', 'fsdp')), may hold values from 0 to 999
- absorbed: int32 [32, 1024], P(('rep', 'fsdp')), may hold values 0 or 1
- qkv_weight: float32 [768, 2304], P('fsdp'), may hold values from -0.2 to 0.2
- out_weight: float32 [768, 768], P('fsdp'), may hold values from -2.5 to 2.5
- up_weight: float32 [768, 3072], P('fsdp'), may hold values from -0.25 to 0.25
- down_weight: float32 [3072, 768], P('fsdp'), may hold values from -0.7 to 0.7
- mod_weight: float32 [128, 4608], P(None, 'fsdp'), may hold values from -4 to 4
- qkv_first: float32 [768, 2304], P('fsdp'), may hold values from -27.1529 to 27.1529
- out_first: float32 [768, 768], P('fsdp'), may hold values from -2.2627417 to 2.2627417
- up_first: float32 [768, 3072], P('fsdp'), may hold values from -108.6116 to 108.6116
- down_first: float32 [3072, 768], P('fsdp'), may hold values from -43.44464 to 43.44464
- mod_first: float32 [128, 4608], P(None, 'fsdp'), may hold values from -23.532514 to 23.532514
- qkv_second: float32 [768, 2304], P('fsdp'), may hold values from 0 to 18.56
- out_second: float32 [768, 768], P('fsdp'), may hold values from 0 to 0.1312
- up_second: float32 [768, 3072], P('fsdp'), may hold values from 0 to 298.1888
- down_second: float32 [3072, 768], P('fsdp'), may hold values from 0 to 49.152
- mod_second: float32 [128, 4608], P(None, 'fsdp'), may hold values from 0 to 13.1072
- vectors: float32 [9984], P('fsdp'), may hold values from -1.2 to 3.8
- vectors_first: float32 [9984], P('fsdp'), may hold values from -38.01406 to 38.01406
- vectors_second: float32 [9984], P('fsdp'), may hold values from 0 to 36.0448
Outputs:
- out_hidden: bfloat16 [32, 1024, 768], P(('rep', 'fsdp'))
- grad_inputs: float32 [32, 1024, 768], P(('rep', 'fsdp'))
- qkv_updated: float32 [768, 2304], P('fsdp')
- out_updated: float32 [768, 768], P('fsdp')
- up_updated: float32 [768, 3072], P('fsdp')
- down_updated: float32 [3072, 768], P('fsdp')
- mod_updated: float32 [128, 4608], P(None, 'fsdp')
- qkv_moment: float32 [768, 2304], P('fsdp')
- out_moment: float32 [768, 768], P('fsdp')
- up_moment: float32 [768, 3072], P('fsdp')
- down_moment: float32 [3072, 768], P('fsdp')
- mod_moment: float32 [128, 4608], P(None, 'fsdp')
- qkv_variance: float32 [768, 2304], P('fsdp')
- out_variance: float32 [768, 768], P('fsdp')
- up_variance: float32 [768, 3072], P('fsdp')
- down_variance: float32 [3072, 768], P('fsdp')
- mod_variance: float32 [128, 4608], P(None, 'fsdp')
- vectors_updated: float32 [9984], P('fsdp')
- vectors_moment: float32 [9984], P('fsdp')
- vectors_variance: float32 [9984], P('fsdp')
- weight_norms: float32 [2, 5], replicated
Inputs may be any that keep to these rules, and one draw needn't show every extreme that they name: `seg_sizes`: in every row the nonzero entries come first, each is 1024, 512 or 128, and they sum to 1024; the rest are zero. `seq_lengths`: each entry lies between half of the matching seg_sizes entry and all of it; zero where that entry is zero.
All inputs are finite; a program needn't handle non-finite values. No bound on the sum of `absorbed` on one device may be relied on, other than what follows from the above.
Results may differ from a plain program's by a relative error of at most 0.025.
The roundings to bfloat16 on the way count: a program that leaves them out, or rounds other values in their place, can miss the bound.
Values may be sent and summed in bfloat16 or wider, within the bound.
No kernel may reach another device: no remote copies, remote signals or barrier semaphores. Data moves between devices by JAX's collectives and lax.ppermute only.
A program may use at most 320 MiB of HBM per device.

v0:
```python
import functools
import math

import jax
import jax.numpy as jnp
import numpy as np
from jax import lax
from jax.experimental import pallas as pl
from jax.experimental.pallas import tpu as pltpu
from jax.sharding import PartitionSpec as P

D = 768
HEADS = 12
HDIM = 64
FF = 3072
COND = 128
SLOTS = 1024
NSEG = 8
STEP = 10
TILE = 128
BLOCKS = SLOTS // TILE

BETA_ONE = 0.9
BETA_TWO = 0.999
EPSILON = 1e-06
DECAY_RATE = 0.01
MATRIX_RATE = 0.3
VECTOR_RATE = 1.0

PAIR = 128
NT = (((1,), (1,)), ((), ()))
NN = (((1,), (0,)), ((), ()))
TN = (((0,), (0,)), ((), ()))
BF = jnp.bfloat16
F32 = jnp.float32


def mm(a, b, dims=NN):
    return lax.dot_general(a, b, dims, preferred_element_type=F32)


def swap_halves(v):
    lane = lax.broadcasted_iota(jnp.int32, v.shape, 1)
    return jnp.where(lane % 64 < 32, pltpu.roll(v, PAIR - 32, 1), pltpu.roll(v, 32, 1))


def attention_forward_kernel(block, q_ref, k_ref, v_ref, fq_ref, fk_ref, *refs):
    o_ref, fo_ref, ka, kb, va, vb = refs[-6:]
    slots = q_ref.shape[0]
    low_all = lax.broadcasted_iota(jnp.int32, (slots, PAIR), 1) < 64
    k_low = k_ref[...]
    v_low = v_ref[...]
    fk = fk_ref[...]
    one = jnp.ones((slots, PAIR), BF)
    ka[...] = jnp.where(low_all, k_low, fk)
    kb[...] = jnp.where(low_all, fk, k_low)
    va[...] = jnp.where(low_all, v_low, one)
    vb[...] = jnp.where(low_all, one, v_low)
    lane = lax.broadcasted_iota(jnp.int32, (block, PAIR), 1)
    low = lane < 64
    spot = lane % 64

    def step(i, carry):
        at = pl.ds(pl.multiple_of(i * block, block), block)
        q = q_ref[at, :]
        fq = fq_ref[at, :]
        sa = mm(jnp.where(low, q, fq), ka[...], NT)
        sb = mm(jnp.where(low, fq, q), kb[...], NT)
        ma = jnp.max(sa, axis=1, keepdims=True)
        mb = jnp.max(sb, axis=1, keepdims=True)
        pa = jnp.exp(sa - ma).astype(BF)
        pb = jnp.exp(sb - mb).astype(BF)
        oa = mm(pa, va[...])
        ob = mm(pb, vb[...])
        o = jnp.where(low, oa / pltpu.roll(oa, 64, 1), ob / pltpu.roll(ob, 64, 1))
        o_ref[at, :] = o.astype(o_ref.dtype)
        neg = jnp.where(low, -(mb + jnp.log(ob)), -(ma + jnp.log(oa)))
        hi = neg.astype(BF)
        rest = neg - hi.astype(F32)
        mid = rest.astype(BF)
        last = (rest - mid.astype(F32)).astype(BF)
        fo_ref[at, :] = jnp.where(spot == 8, hi, jnp.where(spot == 9, mid, jnp.where(spot == 10, last, fq)))
        return carry

    lax.fori_loop(0, slots // block, step, 0)


def attention_forward(qkv, fq, fk, before, first, count, block=1024):
    slots, width = qkv.shape
    pairs = width // 3 // PAIR
    blk = lambda off: pl.BlockSpec((slots, PAIR), lambda p: (0, off + p))
    fixed = pl.BlockSpec((slots, PAIR), lambda p: (0, 0))
    anywhere = pl.BlockSpec(memory_space=pl.ANY)
    shape = jax.ShapeDtypeStruct((slots, pairs * PAIR), BF)
    extra = () if before is None else before
    elements = 2 * count * slots * slots
    return pl.pallas_call(
        functools.partial(attention_forward_kernel, block),
        grid=(count,),
        in_specs=[blk(first), blk(pairs + first), blk(2 * pairs + first), fixed, fixed] + [anywhere] * len(extra),
        out_specs=[blk(first)] * 2,
        out_shape=[shape, shape],
        scratch_shapes=[pltpu.VMEM((slots, PAIR), BF)] * 4,
        input_output_aliases={5: 0, 6: 1} if extra else {},
        cost_estimate=pl.CostEstimate(flops=elements * 3000, bytes_accessed=10 * slots * count * PAIR, transcendentals=elements),
        compiler_params=pltpu.CompilerParams(vmem_limit_bytes=48 * 2**20),
    )(qkv, qkv, qkv, fq, fk, *extra)


def attention_backward_kernel(block, q_ref, k_ref, v_ref, fo_ref, fk_ref, do_ref, o_ref, cos_ref, sin_ref, *refs):
    g_ref, ka, kb, va, vb, kt, dka, dkb, dva, dvb = refs[-10:]
    slots = q_ref.shape[0]
    lane_all = lax.broadcasted_iota(jnp.int32, (slots, PAIR), 1)
    low_all = lane_all < 64
    fk = fk_ref[...]
    k_low = k_ref[...]
    v_low = v_ref[...]
    one = jnp.where(lane_all % 64 < 2, 1.0, 0.0).astype(BF)
    ka[...] = jnp.where(low_all, k_low, fk)
    kb[...] = jnp.where(low_all, fk, k_low)
    va[...] = jnp.where(low_all, v_low, one)
    vb[...] = jnp.where(low_all, one, v_low)
    kt[...] = k_low.T
    dka[...] = jnp.zeros_like(dka)
    dkb[...] = jnp.zeros_like(dkb)
    dva[...] = jnp.zeros_like(dva)
    dvb[...] = jnp.zeros_like(dvb)
    lane = lax.broadcasted_iota(jnp.int32, (block, PAIR), 1)
    low = lane < 64
    spot = lane % 64
    top = lax.broadcasted_iota(jnp.int32, (PAIR, block), 0) < 64

    def step(i, carry):
        at = pl.ds(pl.multiple_of(i * block, block), block)
        q = q_ref[at, :]
        fq = fo_ref[at, :]
        do = do_ref[at, :]
        both = do.astype(F32) * o_ref[at, :].astype(F32)
        da = jnp.sum(jnp.where(low, both, 0.0), axis=1, keepdims=True)
        db = jnp.sum(jnp.where(low, 0.0, both), axis=1, keepdims=True)
        neg = jnp.where(low, -db, -da)
        hi = neg.astype(BF)
        rest = (neg - hi.astype(F32)).astype(BF)
        fd = jnp.where(spot == 0, hi, jnp.where(spot == 1, rest, jnp.zeros_like(hi)))
        sa = mm(ka[...], jnp.where(low, q, fq), NT)
        sb = mm(kb[...], jnp.where(low, fq, q), NT)
        ea = mm(va[...], jnp.where(low, do, fd), NT)
        eb = mm(vb[...], jnp.where(low, fd, do), NT)
        pa = jnp.exp(sa)
        pb = jnp.exp(sb)
        dsa = (pa * ea).astype(BF)
        dsb = (pb * eb).astype(BF)
        dva[...] += mm(pa.astype(BF), do)
        dvb[...] += mm(pb.astype(BF), do)
        dka[...] += mm(dsa, q)
        dkb[...] += mm(dsb, q)
        dqt = jnp.where(top, mm(kt[...], dsa), mm(kt[...], dsb))
        dq = dqt.T * 0.125
        g_ref[0, at, :] = (dq * cos_ref[at, :] - swap_halves(dq) * sin_ref[at, :]).astype(BF)
        return carry

    lax.fori_loop(0, slots // block, step, 0)
    dk = jnp.where(low_all, dka[...], dkb[...])
    g_ref[1] = (dk * cos_ref[...] - swap_halves(dk) * sin_ref[...]).astype(BF)
    g_ref[2] = jnp.where(low_all, dva[...], dvb[...]).astype(BF)


def attention_backward(qkv, fo, fk, do, o, cos, sin, before, first, count, block=512):
    slots, width = qkv.shape
    pairs = width // 3 // PAIR
    blk = lambda off: pl.BlockSpec((slots, PAIR), lambda p: (0, off + p))
    fixed = pl.BlockSpec((slots, PAIR), lambda p: (0, 0))
    extra = () if before is None else (before,)
    elements = 2 * count * slots * slots
    return pl.pallas_call(
        functools.partial(attention_backward_kernel, block),
        grid=(count,),
        in_specs=[blk(first), blk(pairs + first), blk(2 * pairs + first), blk(first), fixed, blk(first), blk(first),
                  fixed, fixed] + [pl.BlockSpec(memory_space=pl.ANY)] * len(extra),
        out_specs=pl.BlockSpec((3, slots, PAIR), lambda p: (0, 0, first + p)),
        out_shape=jax.ShapeDtypeStruct((3, slots, pairs * PAIR), BF),
        scratch_shapes=[pltpu.VMEM((slots, PAIR), BF)] * 4 + [pltpu.VMEM((PAIR, slots), BF)]
        + [pltpu.VMEM((slots, PAIR), F32)] * 4,
        input_output_aliases={9: 0} if extra else {},
        cost_estimate=pl.CostEstimate(flops=elements * 2000, bytes_accessed=20 * slots * count * PAIR, transcendentals=elements),
        compiler_params=pltpu.CompilerParams(vmem_limit_bytes=48 * 2**20),
    )(qkv, qkv, qkv, fo, fk, do, o, cos, sin, *extra)


def attention_tables(segment, position, valid_slot):
    inverse = jnp.exp(jnp.arange(32, dtype=F32) * (-math.log(10000.0) / 32))
    angles = position.astype(F32)[:, None] * inverse[None, :]
    c, s = jnp.cos(angles), jnp.sin(angles)
    cos = jnp.concatenate([c, c, c, c], axis=1)
    sin = jnp.concatenate([-s, s, -s, s], axis=1)
    spot = jnp.arange(PAIR) % 64
    same = segment[:, None] == spot[None, :]
    fq = same.astype(BF)
    fk = jnp.where((spot < 8)[None, :], jnp.where(same & valid_slot[:, None], 0.0, -1e30),
                   jnp.where((spot < 11)[None, :], 1.0, 0.0)).astype(BF)
    return cos, sin, fq, fk


UNITS = 16
QKV_HALF = 3 * D // 2
SMALL_WIDE = 6 * COND + 128
FIRST_WIDE = QKV_HALF + 3 * COND + 128
UP_AT, DOWN_AT, OUT_AT, SECOND_WIDE = 0, FF // 2, FF // 2 + 2 * D, FF // 2 + 2 * D + D // 2
VECTOR_PART = (9 * D + FF) // UNITS
FLAT_ROWS = 80
HBM = pltpu.HBM
SMALL_VMEM = pl.BlockSpec(memory_space=pltpu.SMEM)


def whole(shape):
    return pl.BlockSpec(shape, lambda *_: (0,) * len(shape))


def line(flat_ref, start, count):
    return jnp.concatenate([flat_ref[start + i : start + i + 1, :] for i in range(count)], axis=1)


def unit_of(units, half, place):
    if len(units) == 8:
        return units[half * 4 + place // 4].at[place % 4]
    return units[half * 8 + place // 4 * 2 + min(place % 4, 1)].at[max(place % 4 - 1, 0)]


def unit_copies(units, order, core, sems, plan, first_sem):
    copies = []
    for half in range(2):
        side = core if half == 0 else 1 - core
        for place in range(UNITS):
            origin = order[half * UNITS + place]
            for target, rows, column, width, by_origin, by_side, row, column_side, both in plan:
                if half == 1 and not both:
                    continue
                to_row = pl.multiple_of(origin * by_origin + side * by_side + row, 16)
                to_column = pl.multiple_of(side * column_side, 128) if column_side else 0
                copies.append(
                    pltpu.make_async_copy(
                        unit_of(units, half, place).at[pl.ds(0, rows), pl.ds(column, width)],
                        target.at[pl.ds(to_row, rows), pl.ds(to_column, width)],
                        sems.at[first_sem + len(copies)],
                    )
                )
    return copies


def layer_norm(values):
    average = jnp.mean(values, axis=-1, keepdims=True)
    centered = values - average
    root = lax.rsqrt(jnp.mean(centered * centered, axis=-1, keepdims=True) + 1e-05)
    return (centered * root, root)


def layer_norm_back(grad, normal, root, gain):
    scaled = grad * gain
    inner = jnp.mean(scaled * normal, axis=-1, keepdims=True)
    return root * (scaled - jnp.mean(scaled, axis=-1, keepdims=True) - normal * inner)


def first_kernel(rows, order_ref, core_ref, tiles_ref, *refs):
    units = refs[:8]
    x_ref, cond_ref, cos_ref, sin_ref, qkv_ref, first_ref, w_ref, mod_ref, flat_ref, modt, vecs, sems = refs[8:]
    step = pl.program_id(0)

    @pl.when(step == 0)
    def _():
        core = core_ref[0]
        small = unit_copies(units, order_ref, core, sems, (
            (vecs, 16, QKV_HALF + 3 * COND, 128, 16, 0, 0, 0, False),
            (modt, 48, QKV_HALF, 128, 288, 144, 0, 0, True),
            (modt, 48, QKV_HALF + 128, 128, 288, 144, 48, 0, True),
            (modt, 48, QKV_HALF + 256, 128, 288, 144, 96, 0, True),
        ), 0)
        large = unit_copies(units, order_ref, core, sems, (
            (w_ref, 48, 0, QKV_HALF, 48, 0, 0, QKV_HALF, True),
        ), len(small))
        for copy in small + large:
            copy.start()
        for copy in small:
            copy.wait()
        flat_ref[...] = jnp.zeros_like(flat_ref)
        lane = lax.broadcasted_iota(jnp.int32, (8, 128), 1)
        for part in range(UNITS):
            row, turn = divmod(VECTOR_PART * part, 128)
            piece = vecs[16 * part : 16 * part + 16, :].astype(F32)[:8]
            if turn:
                piece = pltpu.roll(piece, turn, 1)
                flat_ref[row + 1 : row + 6, :] += jnp.where(lane < turn, piece, 0.0)[:5]
                piece = jnp.where(lane >= turn, piece, 0.0)
            flat_ref[row : row + 5, :] += piece[:5]
        mod_ref[...] = mm(cond_ref[...], modt[...], NT) + line(flat_ref, (3 * D + FF) // 128, 6 * D // 128)
        for copy in large:
            copy.wait()

    gain = line(flat_ref, 0, D // 128)
    for part in range(rows // TILE):
        at = pl.ds(part * TILE, TILE)
        segment = tiles_ref[step * (rows // TILE) + part]
        normal, _ = layer_norm(x_ref[at, :].astype(F32))
        shift = mod_ref[pl.ds(segment, 1), 0:D]
        scale = mod_ref[pl.ds(segment, 1), D : 2 * D]
        first_ref[at, :] = (normal * (gain * (1.0 + scale)) + shift).astype(BF)
    first = first_ref[...]
    cos, sin = cos_ref[...], sin_ref[...]
    for kind in range(3):
        mixed = mm(first, w_ref[:, kind * D : (kind + 1) * D])
        if kind < 2:
            for pair in range(D // PAIR):
                part = mixed[:, pair * PAIR : (pair + 1) * PAIR]
                turned = part * cos + swap_halves(part) * sin
                if kind == 0:
                    turned = turned * HDIM ** (-0.5)
                qkv_ref[:, kind * D + pair * PAIR : kind * D + (pair + 1) * PAIR] = turned.astype(BF)
        else:
            qkv_ref[:, 2 * D :] = mixed.astype(BF)


def first_part(units, order, core, tiles, x, cond, cos, sin, rows=256):
    count = UNITS * (1 + 2 * 3 + 2)
    row = lambda width: pl.BlockSpec((rows, width), lambda i: (i, 0))
    shape = lambda s, t: jax.ShapeDtypeStruct(s, t)
    return pl.pallas_call(
        functools.partial(first_kernel, rows),
        grid=(SLOTS // rows,),
        in_specs=[SMALL_VMEM] * 3 + [pl.BlockSpec(memory_space=HBM)] * 8
        + [row(D), whole((NSEG, COND)), row(PAIR), row(PAIR)],
        out_specs=[row(3 * D), row(D), whole((D, 3 * D)), whole((NSEG, 6 * D)), whole((FLAT_ROWS, 128))],
        out_shape=[shape((SLOTS, 3 * D), BF), shape((SLOTS, D), BF), shape((D, 3 * D), BF),
                   shape((NSEG, 6 * D), F32), shape((FLAT_ROWS, 128), F32)],
        scratch_shapes=[pltpu.VMEM((6 * D, COND), BF), pltpu.VMEM((16 * UNITS, 128), BF), pltpu.SemaphoreType.DMA((count,))],
        cost_estimate=pl.CostEstimate(flops=2 * SLOTS * D * 3 * D, bytes_accessed=20 * 2**20, transcendentals=SLOTS),
        compiler_params=pltpu.CompilerParams(vmem_limit_bytes=56 * 2**20),
    )(order, core, tiles, *units, x, cond, cos, sin)


def middle_kernel(rows, order_ref, core_ref, tiles_ref, *refs):
    units = refs[:16]
    (att_ref, x_ref, cot_ref, mask_ref, mod_ref, flat_ref,
     out_ref, left_ref, right_ref, gmid_ref, gatt_ref, sums_ref, bias_ref,
     wo, wu, wd, slope, branch_s, middle_s, sems) = refs[16:]
    step = pl.program_id(0)
    core = core_ref[0]
    chunks = FF // D
    tiles = rows // TILE
    each = 2 * UNITS
    copies = [
        unit_copies(units, order_ref, core, sems, ((wo, 48, OUT_AT, D // 2, 48, 0, 0, D // 2, True),), 0),
        unit_copies(units, order_ref, core, sems, ((wu, 48, UP_AT, FF // 2, 48, 0, 0, FF // 2, True),), each),
        unit_copies(units, order_ref, core, sems, (
            (wd, 48, DOWN_AT, D, 192, 96, 0, 0, True),
            (wd, 48, DOWN_AT + D, D, 192, 96, 48, 0, True),
        ), 2 * each),
    ]

    @pl.when(step == 0)
    def _():
        for group in copies:
            for copy in group:
                copy.start()
        bias_ref[...] = jnp.zeros_like(bias_ref)
        for copy in copies[0]:
            copy.wait()

    def table(part, kind):
        return mod_ref[pl.ds(tiles_ref[step * tiles + part], 1), kind * D : (kind + 1) * D]

    def mask_column(part):
        row = mask_ref[pl.ds(step * tiles + part, 1), :]
        return jnp.broadcast_to(row, (TILE, TILE)).T[:, :1]

    att = att_ref[...]
    left_ref[:, FF + D :] = att
    branch_s[...] = mm(att, wo[...])
    gain = line(flat_ref, D // 128, D // 128)
    for part in range(tiles):
        at = pl.ds(part * TILE, TILE)
        middle = x_ref[at, :].astype(F32) + table(part, 2) * branch_s[at, :]
        middle_s[at, :] = middle
        normal, _ = layer_norm(middle)
        left_ref[at, FF : FF + D] = (normal * (gain * (1.0 + table(part, 4))) + table(part, 3)).astype(BF)

    @pl.when(step == 0)
    def _():
        for group in copies[1:]:
            for copy in group:
                copy.wait()

    second = left_ref[:, FF : FF + D]
    factor = math.sqrt(2.0 / math.pi)
    feed = None
    for j in range(chunks):
        at = pl.ds(j * D, D)
        u = mm(second, wu[:, at]) + line(flat_ref, 2 * D // 128 + j * (D // 128), D // 128)
        square = u * u
        bent = jnp.tanh(u * (factor + (factor * 0.044715) * square))
        half = 0.5 * u
        bow = half * bent
        hidden = (half + bow).astype(BF)
        left_ref[:, at] = hidden
        slope[:, at] = (0.5 + 0.5 * bent) + (half - bow * bent) * (factor + (3 * factor * 0.044715) * square)
        share = mm(hidden, wd[at, :])
        feed = share if feed is None else feed + share
    bias_down = line(flat_ref, (2 * D + FF) // 128, D // 128)
    for part in range(tiles):
        at = pl.ds(part * TILE, TILE)
        gate = table(part, 5)
        feed_out = feed[part * TILE : (part + 1) * TILE] + bias_down
        out_ref[at, :] = (middle_s[at, :] + gate * feed_out).astype(BF)
        grad_out = cot_ref[at, :].astype(F32) * mask_column(part)
        sums_ref[part, 3:4, :] = jnp.sum(grad_out * feed_out, axis=0, keepdims=True)
        grad_mlp = (grad_out * gate).astype(BF)
        right_ref[at, 0:D] = grad_mlp
        bias_ref[0:1, FF:] += jnp.sum(grad_mlp.astype(F32), axis=0, keepdims=True)
    grad_mlp = right_ref[:, 0:D]
    grad_second = None
    for j in range(chunks):
        at = pl.ds(j * D, D)
        grad_up = (mm(grad_mlp, wd[at, :], NT) * slope[:, at]).astype(BF)
        right_ref[:, D + j * D : 2 * D + j * D] = grad_up
        bias_ref[0:1, at] += jnp.sum(grad_up.astype(F32), axis=0, keepdims=True)
        share = mm(grad_up, wu[:, at], NT)
        grad_second = share if grad_second is None else grad_second + share
    for part in range(tiles):
        at = pl.ds(part * TILE, TILE)
        normal, root = layer_norm(middle_s[at, :])
        grad = grad_second[part * TILE : (part + 1) * TILE]
        sums_ref[part, 1:2, :] = jnp.sum(grad, axis=0, keepdims=True)
        sums_ref[part, 2:3, :] = jnp.sum(grad * normal, axis=0, keepdims=True)
        grad_middle = cot_ref[at, :].astype(F32) * mask_column(part) + layer_norm_back(
            grad, normal, root, gain * (1.0 + table(part, 4))
        )
        gmid_ref[at, :] = grad_middle
        sums_ref[part, 0:1, :] = jnp.sum(grad_middle * branch_s[at, :], axis=0, keepdims=True)
        right_ref[at, FF + D :] = (grad_middle * table(part, 2)).astype(BF)
    gatt_ref[...] = mm(right_ref[:, FF + D :], wo[...], NT).astype(BF)


def middle_part(units, order, core, tiles, att, x, cot, mask, modulation, flat, rows=256):
    row = lambda width: pl.BlockSpec((rows, width), lambda i: (i, 0))
    shape = lambda s, t: jax.ShapeDtypeStruct(s, t)
    return pl.pallas_call(
        functools.partial(middle_kernel, rows),
        grid=(SLOTS // rows,),
        in_specs=[SMALL_VMEM] * 3 + [pl.BlockSpec(memory_space=HBM)] * 16
        + [row(D), row(D), row(D), whole((BLOCKS, TILE)), whole((NSEG, 6 * D)), whole((FLAT_ROWS, 128))],
        out_specs=[row(D), row(FF + 2 * D), row(FF + 2 * D), row(D), row(D),
                   pl.BlockSpec((rows // TILE, 8, D), lambda i: (i, 0, 0)), whole((8, FF + D))],
        out_shape=[shape((SLOTS, D), BF), shape((SLOTS, FF + 2 * D), BF), shape((SLOTS, FF + 2 * D), BF),
                   shape((SLOTS, D), F32), shape((SLOTS, D), BF), shape((BLOCKS, 8, D), F32), shape((8, FF + D), F32)],
        scratch_shapes=[pltpu.VMEM((D, D), BF), pltpu.VMEM((D, FF), BF), pltpu.VMEM((FF, D), BF),
                        pltpu.VMEM((rows, FF), F32), pltpu.VMEM((rows, D), F32), pltpu.VMEM((rows, D), F32),
                        pltpu.SemaphoreType.DMA((8 * UNITS,))],
        cost_estimate=pl.CostEstimate(flops=4 * SLOTS * D * (D + 2 * FF), bytes_accessed=50 * 2**20, transcendentals=SLOTS * FF),
        compiler_params=pltpu.CompilerParams(vmem_limit_bytes=60 * 2**20),
    )(order, core, tiles, *units, att, x, cot, mask, modulation, flat)


def later_grads_kernel(core_ref, left_ref, right_ref, mine_ref, give_ref, buffer, sems):
    step = pl.program_id(0)
    steps = 2 * (FF // D) + 1
    slot = step % 2
    down_steps = FF // D
    core = core_ref[0]

    def wait(at_slot):
        for number in range(16):
            pltpu.make_async_copy(buffer.at[at_slot, number], buffer.at[at_slot, number], sems.at[at_slot, number]).wait()

    @pl.when(step >= 2)
    def _():
        wait(slot)

    product = mm(left_ref[...], right_ref[...], TN).astype(BF)
    buffer[slot] = product.reshape(16, 48, D)

    @pl.when(step < down_steps)
    def _():
        for number in range(16):
            local, side, block = number // 4, (number // 2) % 2, number % 2
            for ref, wanted in ((mine_ref, 0), (give_ref, 1)):
                @pl.when((core ^ side) == wanted)
                def _(ref=ref):
                    pltpu.make_async_copy(
                        buffer.at[slot, number],
                        ref.at[4 * step + local, :, pl.ds(DOWN_AT + block * D, D)],
                        sems.at[slot, number],
                    ).start()

    for j in range(down_steps):
        @pl.when(step == down_steps + j)
        def _():
            for number in range(16):
                for ref, wanted in ((mine_ref, 0), (give_ref, 1)):
                    @pl.when((core ^ (j // 2)) == wanted)
                    def _(ref=ref):
                        pltpu.make_async_copy(
                            buffer.at[slot, number],
                            ref.at[number, :, pl.ds(UP_AT + (j % 2) * D, D)],
                            sems.at[slot, number],
                        ).start()

    @pl.when(step == steps - 1)
    def _():
        for number in range(16):
            for side in range(2):
                for ref, wanted in ((mine_ref, 0), (give_ref, 1)):
                    @pl.when((core ^ side) == wanted)
                    def _(ref=ref):
                        pltpu.make_async_copy(
                            buffer.at[slot, number, :, pl.ds(side * (D // 2), D // 2)],
                            ref.at[number, :, pl.ds(OUT_AT, D // 2)],
                            sems.at[slot, number],
                        ).start()
        wait(1 - slot)
        wait(slot)


def later_grads(core, left, right):
    chunks = FF // D
    left_at = lambda i: (0, jnp.minimum(i, chunks) + jnp.maximum(i - 2 * chunks + 1, 0))
    right_at = lambda i: (0, jnp.maximum(i - chunks + 1, 0))
    shape = jax.ShapeDtypeStruct((UNITS, 48, SECOND_WIDE), BF)
    return pl.pallas_call(
        later_grads_kernel,
        grid=(2 * chunks + 1,),
        in_specs=[SMALL_VMEM, pl.BlockSpec((SLOTS, D), left_at), pl.BlockSpec((SLOTS, D), right_at)],
        out_specs=[pl.BlockSpec(memory_space=HBM)] * 2,
        out_shape=[shape, shape],
        scratch_shapes=[pltpu.VMEM((2, 16, 48, D), BF), pltpu.SemaphoreType.DMA((2, 16))],
        cost_estimate=pl.CostEstimate(flops=2 * SLOTS * D * (2 * FF + D), bytes_accessed=40 * 2**20, transcendentals=0),
        compiler_params=pltpu.CompilerParams(vmem_limit_bytes=48 * 2**20),
    )(core, left, right)


def qkv_grads_kernel(core_ref, first_ref, g_ref, mine_ref, give_ref, units, sems):
    step = pl.program_id(0)
    core = core_ref[0]
    product = mm(first_ref[...], g_ref[0], TN).astype(BF).reshape(UNITS, 48, D)

    @pl.when(step == 0)
    def _():
        units[0, :, :, 0:D] = product

    @pl.when(step == 1)
    def _():
        units[0, :, :, D:] = product[:, :, : D // 2]
        units[1, :, :, 0 : D // 2] = product[:, :, D // 2 :]

    @pl.when(step == 2)
    def _():
        units[1, :, :, D // 2 :] = product
        copies = [
            pltpu.make_async_copy(units.at[core], mine_ref, sems.at[0]),
            pltpu.make_async_copy(units.at[1 - core], give_ref, sems.at[1]),
        ]
        for copy in copies:
            copy.start()
        for copy in copies:
            copy.wait()


def qkv_grads(core, first, g):
    shape = jax.ShapeDtypeStruct((UNITS, 48, QKV_HALF), BF)
    return pl.pallas_call(
        qkv_grads_kernel,
        grid=(3,),
        in_specs=[SMALL_VMEM, whole((SLOTS, D)), pl.BlockSpec((1, SLOTS, D), lambda i: (i, 0, 0))],
        out_specs=[pl.BlockSpec(memory_space=HBM)] * 2,
        out_shape=[shape, shape],
        scratch_shapes=[pltpu.VMEM((2, UNITS, 48, QKV_HALF), BF), pltpu.SemaphoreType.DMA((2,))],
        cost_estimate=pl.CostEstimate(flops=SLOTS * D * D, bytes_accessed=2**20, transcendentals=0),
        compiler_params=pltpu.CompilerParams(vmem_limit_bytes=48 * 2**20),
    )(core, first, g)


def last_kernel(rows, places_ref, tiles_ref, member_ref, g_ref, w_ref, x_ref, gmid_ref, mod_ref, flat_ref, cond_ref,
                sums_in, bias_in, gin_ref, own_ref, first_ref, second_ref, far_ref, sums, units, sems):
    step = pl.program_id(0)
    tiles = rows // TILE
    steps = SLOTS // rows
    gain = line(flat_ref, 0, D // 128)

    grad = None
    for kind in range(3):
        share = mm(g_ref[kind], w_ref[:, kind * D : (kind + 1) * D], NT)
        grad = share if grad is None else grad + share
    for part in range(tiles):
        at = pl.ds(part * TILE, TILE)
        tile = step * tiles + part
        segment = tiles_ref[tile]
        normal, root = layer_norm(x_ref[at, :].astype(F32))
        piece = grad[part * TILE : (part + 1) * TILE]
        scale = mod_ref[pl.ds(segment, 1), D : 2 * D]
        sums[pl.ds(tile, 1), 0:D] = jnp.sum(piece, axis=0, keepdims=True)
        sums[pl.ds(tile, 1), D : 2 * D] = jnp.sum(piece * normal, axis=0, keepdims=True)
        gin_ref[at, :] = gmid_ref[at, :] + layer_norm_back(piece, normal, root, gain * (1.0 + scale))

    @pl.when(step == steps - 1)
    def _():
        gain_two = line(flat_ref, D // 128, D // 128)
        for tile in range(BLOCKS):
            at = pl.ds(tile, 1)
            sums[at, 2 * D : 3 * D] = sums_in[tile, 0:1, :]
            sums[at, 3 * D : 4 * D] = sums_in[tile, 1:2, :]
            sums[at, 4 * D : 5 * D] = sums_in[tile, 2:3, :]
            sums[at, 5 * D : 6 * D] = sums_in[tile, 3:4, :]
        member = member_ref[...]
        scale_one = lax.dot_general(member, mod_ref[:, D : 2 * D], NN, precision=lax.Precision.HIGHEST, preferred_element_type=F32)
        scale_two = lax.dot_general(member, mod_ref[:, 4 * D : 5 * D], NN, precision=lax.Precision.HIGHEST, preferred_element_type=F32)
        grad_gain_one = jnp.sum(sums[:, D : 2 * D] * (1.0 + scale_one), axis=0, keepdims=True)
        grad_gain_two = jnp.sum(sums[:, 4 * D : 5 * D] * (1.0 + scale_two), axis=0, keepdims=True)
        sums[:, D : 2 * D] = sums[:, D : 2 * D] * gain
        sums[:, 4 * D : 5 * D] = sums[:, 4 * D : 5 * D] * gain_two
        by_segment = lax.dot_general(member, sums[...], TN, precision=lax.Precision.HIGHEST, preferred_element_type=F32)
        grad_mod = lax.dot_general(
            by_segment, cond_ref[...].astype(F32), TN, precision=lax.Precision.HIGHEST, preferred_element_type=F32
        ).astype(BF).reshape(4, 4, 6, 48, COND)
        for block in range(6):
            units[:, :, :, block * COND : (block + 1) * COND] = grad_mod[:, :, block]
        row = jnp.concatenate(
            [grad_gain_one, grad_gain_two, bias_in[0:1, :], jnp.sum(by_segment, axis=0, keepdims=True)], axis=1
        )
        lane = lax.broadcasted_iota(jnp.int32, (1, 128), 1)
        blank = jnp.zeros((43, 128), F32)
        for part in range(UNITS):
            start = VECTOR_PART * part
            pieces = []
            for number in range(5):
                first_row, turn = divmod(start + 128 * number, 128)
                piece = row[:, first_row * 128 : (first_row + 1) * 128]
                if turn:
                    following = (
                        row[:, (first_row + 1) * 128 : (first_row + 2) * 128]
                        if (first_row + 2) * 128 <= row.shape[1]
                        else jnp.zeros((1, 128), F32)
                    )
                    piece = jnp.where(
                        lane < 128 - turn, pltpu.roll(piece, 128 - turn, 1), pltpu.roll(following, 128 - turn, 1)
                    )
                if number == 4:
                    piece = jnp.where(lane < VECTOR_PART - 512, piece, 0.0)
                pieces.append(piece)
            stack = jnp.concatenate(pieces + [blank], axis=0).astype(BF)
            units[part // 4, part % 4, :, 6 * COND :] = stack
        copies = [
            pltpu.make_async_copy(units.at[:, places_ref[kind]], ref, sems.at[kind])
            for kind, ref in enumerate((own_ref, first_ref, second_ref, far_ref))
        ]
        for copy in copies:
            copy.start()
        for copy in copies:
            copy.wait()


def last_part(places, tiles, member, g, w, x, gmid, modulation, flat, cond, sums, bias, rows=256):
    row = lambda width: pl.BlockSpec((rows, width), lambda i: (i, 0))
    shape = jax.ShapeDtypeStruct((4, 48, SMALL_WIDE), BF)
    return pl.pallas_call(
        functools.partial(last_kernel, rows),
        grid=(SLOTS // rows,),
        in_specs=[SMALL_VMEM, SMALL_VMEM, whole((BLOCKS, NSEG)), pl.BlockSpec((3, rows, D), lambda i: (0, i, 0)), whole((D, 3 * D)),
                  row(D), row(D), whole((NSEG, 6 * D)), whole((FLAT_ROWS, 128)), whole((NSEG, COND)),
                  whole((BLOCKS, 8, D)), whole((8, FF + D))],
        out_specs=[row(D)] + [pl.BlockSpec(memory_space=HBM)] * 4,
        out_shape=[jax.ShapeDtypeStruct((SLOTS, D), F32)] + [shape] * 4,
        scratch_shapes=[pltpu.VMEM((BLOCKS, 6 * D), F32), pltpu.VMEM((4, 4, 48, SMALL_WIDE), BF),
                        pltpu.SemaphoreType.DMA((4,))],
        cost_estimate=pl.CostEstimate(flops=2 * SLOTS * D * 3 * D, bytes_accessed=30 * 2**20, transcendentals=SLOTS),
        compiler_params=pltpu.CompilerParams(vmem_limit_bytes=60 * 2**20),
    )(places, tiles, member, g, w, x, gmid, modulation, flat, cond, sums, bias)


def moments(weight_ref, first_ref, second_ref, gradient, first_out, second_out, direction_out, decay_rate=DECAY_RATE):
    weight = weight_ref[...]
    first_new = BETA_ONE * first_ref[...] + (1.0 - BETA_ONE) * gradient
    second_new = BETA_TWO * second_ref[...] + (1.0 - BETA_TWO) * gradient * gradient
    direction = (
        first_new
        / (1.0 - BETA_ONE**STEP)
        / (jnp.sqrt(second_new / (1.0 - BETA_TWO**STEP)) + EPSILON)
        + decay_rate * weight
    )
    first_out[...] = first_new
    second_out[...] = second_new
    direction_out[...] = direction
    return [jnp.sum(values * values, axis=(0, 1), keepdims=True) for values in (weight, direction)]


def squares_table(pairs):
    row = lax.broadcasted_iota(jnp.int32, (8, 128), 0)
    lane = lax.broadcasted_iota(jnp.int32, (8, 128), 1)
    table = jnp.zeros((8, 128), F32)
    for number, sums in pairs:
        for kind in range(2):
            table = jnp.where((row == kind) & (lane == number), sums[kind], table)
    return table


def update_later_kernel(side_ref, own_ref, other_ref, *refs):
    outs, table_ref = refs[9:18], refs[18]
    zero = side_ref[0] == 0
    own, other = own_ref[...].astype(F32), other_ref[...].astype(F32)
    halves = (jnp.where(zero, own, other), jnp.where(zero, other, own))
    out_grad = jnp.concatenate([half[:, OUT_AT:] for half in halves], axis=1)
    up_grad = jnp.concatenate([half[:, UP_AT : UP_AT + FF // 2] for half in halves], axis=1)
    down_grad = jnp.concatenate(
        [half[:, DOWN_AT + D * part : DOWN_AT + D * (part + 1)] for half in halves for part in range(2)], axis=0
    )
    table_ref[...] = squares_table(
        [
            (1 + place, moments(*refs[3 * place : 3 * place + 3], gradient, *outs[3 * place : 3 * place + 3]))
            for place, gradient in enumerate((out_grad, up_grad, down_grad))
        ]
    )


def update_sooner_kernel(side_ref, own_ref, other_ref, small_ref, *refs):
    outs, table_ref = refs[6:12], refs[12]
    zero = side_ref[0] == 0
    own, other = own_ref[...].astype(F32), other_ref[...].astype(F32)
    qkv_grad = jnp.concatenate([jnp.where(zero, own, other), jnp.where(zero, other, own)], axis=1)
    mod_grad = jnp.concatenate([small_ref[:, COND * part : COND * (part + 1)] for part in range(6)], axis=0)
    table_ref[...] = squares_table(
        [
            (4 * place, moments(*refs[3 * place : 3 * place + 3], gradient, *outs[3 * place : 3 * place + 3]))
            for place, gradient in enumerate((qkv_grad, mod_grad))
        ]
    )


def update_moments(kernel, side, parts, arrays):
    block = pl.BlockSpec(memory_space=pltpu.VMEM)
    shapes = [jax.ShapeDtypeStruct(arrays[3 * (i // 3)].shape, F32) for i in range(len(arrays))]
    *outs, table = pl.pallas_call(
        kernel,
        in_specs=[SMALL_VMEM] + [block] * (len(parts) + len(arrays)),
        out_specs=[block] * (len(arrays) + 1),
        out_shape=shapes + [jax.ShapeDtypeStruct((8, 128), F32)],
        compiler_params=pltpu.CompilerParams(vmem_limit_bytes=48 * 2**20),
    )(side, *parts, *arrays)
    return [outs[i : i + 3] for i in range(0, len(outs), 3)], table


def renew_kernel(table_ref, *refs):
    norms_ref = refs[15]
    roots = jnp.sqrt(table_ref[...])
    norms_ref[...] = roots[:2, :5]
    for number in range(5):
        trust = roots[0:1, number : number + 1] / (roots[1:2, number : number + 1] + EPSILON)
        refs[10 + number][...] = refs[number][...] - (MATRIX_RATE * trust) * refs[5 + number][...]


def renew(table, matrices, turns):
    block = pl.BlockSpec(memory_space=pltpu.VMEM)
    return pl.pallas_call(
        renew_kernel,
        in_specs=[block] * 11,
        out_specs=[block] * 6,
        out_shape=[jax.ShapeDtypeStruct(matrix.shape, F32) for matrix in matrices] + [jax.ShapeDtypeStruct((2, 5), F32)],
        compiler_params=pltpu.CompilerParams(vmem_limit_bytes=48 * 2**20),
    )(table, *matrices, *turns)


ALONG = ((1, 2), (2, 1))


def column_of(core, chip, kind):
    first, second = ALONG[core]
    return (chip % 4) ^ (0, first, second, first ^ second)[kind]


ORIGIN = np.array(
    [
        [[column_of(core, chip, kind) + 4 * ((chip // 4 - back) % 4) for kind in range(4) for back in range(4)]
         for chip in range(UNITS)]
        for core in range(2)
    ],
    np.int32,
)
PLACES = np.array(
    [
        [[column_of(core, chip, kind) for kind in range(4)] + [(chip // 4 + ahead) % 4 for ahead in range(4)]
         for chip in range(UNITS)]
        for core in range(2)
    ],
    np.int32,
)


def along_z(values, ahead):
    return lax.ppermute(values, "fsdp", [(chip, chip % 4 + 4 * ((chip // 4 + ahead) % 4)) for chip in range(UNITS)])


def along_plane(values, direction):
    moves = [
        (core * UNITS + chip, core * UNITS + (chip ^ ALONG[core][direction]))
        for core in range(2)
        for chip in range(UNITS)
    ]
    return lax.ppermute(values, ("rep", "fsdp"), moves)


def across_plane(values):
    return lax.ppermute(values, "fsdp", [(chip, chip ^ 3) for chip in range(UNITS)])


def swap_core(values):
    return lax.ppermute(values, "rep", [(0, 1), (1, 0)])


def hold_back(later, sooner):
    return lax.optimization_barrier((later, sooner))[0]


def by_rounds():
    return lax.axis_size("fsdp") == UNITS


def far_from(near):
    return along_plane(near[0], 1)


def near_of(piece):
    return [along_plane(piece, 0), along_plane(piece, 1)]


def swapped(values):
    return [swap_core(one) for one in values]


def column_sums_kernel(counts, places_ref, *refs):
    outs = refs[len(refs) - len(counts) :]
    at = 0
    for out_ref, count in zip(outs, counts):
        total = refs[at][...].astype(F32) + refs[at + 1][...].astype(F32)
        for arrived in refs[at + 2 : at + 2 + count]:
            total = total + arrived[...].astype(F32).reshape(total.shape)
        out_ref[...] = total.astype(BF).reshape(out_ref.shape)
        at += 2 + count


def column_sums(places, mine, given, parts, apart=False):
    block = mine.shape[1:]
    pair = [values.reshape((4, 4) + block) for values in (mine, given)]
    specs, operands, counts = [], [], []
    for ahead in range(4) if apart else (None,):
        for kind, arrived in parts:
            if apart:
                pick = pl.BlockSpec((1, 1) + block, lambda i, s, kind=kind, ahead=ahead: (s[4 + ahead], s[kind], 0, 0))
                came = pl.BlockSpec((1,) + block, lambda i, s, ahead=ahead: (s[4 + ahead], 0, 0))
            else:
                pick = pl.BlockSpec((1, 1) + block, lambda i, s, kind=kind: (i, s[kind], 0, 0))
                came = pl.BlockSpec((1,) + block, lambda i, s: (i, 0, 0))
            specs += [pick, pick] + [came] * len(arrived)
            operands += pair + arrived
            counts.append(len(arrived))
    if apart:
        out_spec, out_shape = pl.BlockSpec(block, lambda i, s: (0, 0)), jax.ShapeDtypeStruct(block, BF)
    else:
        out_spec, out_shape = pl.BlockSpec((1,) + block, lambda i, s: (i, 0, 0)), jax.ShapeDtypeStruct((4,) + block, BF)
    return pl.pallas_call(
        functools.partial(column_sums_kernel, counts),
        grid_spec=pltpu.PrefetchScalarGridSpec(
            num_scalar_prefetch=1,
            grid=(1 if apart else 4,),
            in_specs=specs,
            out_specs=[out_spec] * len(counts),
        ),
        out_shape=[out_shape] * len(counts),
        cost_estimate=pl.CostEstimate(flops=0, bytes_accessed=(200 if apart else 12) * 2**20, transcendentals=0),
        compiler_params=pltpu.CompilerParams(vmem_limit_bytes=48 * 2**20),
    )(places, *operands)


class Scatter:
    def __init__(self, mine, give, places):
        self.mine, self.places = mine, places
        self.given = swap_core(give)

    def send_plane(self, sooner=None):
        given = self.given if sooner is None else hold_back(self.given, sooner)
        sums = column_sums(self.places, self.mine, given, [(3, []), (1, []), (2, [])])
        self.arrived = [across_plane(sums[0]), along_plane(sums[1], 0), along_plane(sums[2], 1)]
        return sums[0]

    def send_far(self, sooner=None):
        given = self.given if sooner is None else hold_back(self.given, sooner)
        far, second = column_sums(self.places, self.mine, given, [(3, []), (2, [])])
        self.far_came, self.second_came = along_plane(far, 1), along_plane(second, 1)
        return far

    def send_first(self, sooner=None):
        self.far_came, self.second_came = (
            (self.far_came, self.second_came) if sooner is None else hold_back((self.far_came, self.second_came), sooner)
        )
        (first,) = column_sums(self.places, self.mine, self.given, [(1, [self.far_came])])
        self.arrived = [along_plane(first, 0), self.second_came]
        return first

    def send_column(self, sooner=None):
        arrived = self.arrived if sooner is None else hold_back(self.arrived, sooner)
        units = column_sums(self.places, self.mine, self.given, [(0, arrived)], apart=True)
        self.own = units[0]
        self.came = [along_z(units[ahead], ahead) for ahead in range(1, 4)]
        return self.own

    def finish(self, sooner=None):
        came = self.came if sooner is None else hold_back(self.came, sooner)
        total = self.own.astype(F32)
        for part in came:
            total = total + part.astype(F32)
        own = total.astype(BF)
        return (own, swap_core(own))


def arrivals_kernel(*refs):
    inputs, outs = refs[1 : len(refs) - 4], refs[len(refs) - 4 :]
    each = len(inputs) // 4
    for number, out_ref in enumerate(outs):
        total = inputs[number * each][0].astype(F32)
        for part in inputs[number * each + 1 : (number + 1) * each]:
            total = total + part[0].astype(F32)
        out_ref[...] = total.astype(BF)


class SmallScatter:
    def __init__(self, own, first, second, far, places):
        self.places = places
        self.parts = [own, across_plane(far), along_plane(first, 0), along_plane(second, 1)]

    def send_column(self, sooner=None):
        parts = self.parts if sooner is None else hold_back(self.parts, sooner)
        block = parts[0].shape[1:]
        picks = [
            pl.BlockSpec((1,) + block, lambda i, s, ahead=ahead: (s[4 + ahead], 0, 0)) for ahead in range(4) for _ in parts
        ]
        self.own, *units = pl.pallas_call(
            arrivals_kernel,
            grid_spec=pltpu.PrefetchScalarGridSpec(
                num_scalar_prefetch=1, grid=(1,), in_specs=picks, out_specs=[pl.BlockSpec(block, lambda i, s: (0, 0))] * 4
            ),
            out_shape=[jax.ShapeDtypeStruct(block, BF)] * 4,
        )(self.places, *(parts * 4))
        self.came = [along_z(unit, ahead + 1) for ahead, unit in enumerate(units)]
        return self.own

    def finish(self):
        total = self.own.astype(F32)
        for part in self.came:
            total = total + part.astype(F32)
        own = total.astype(BF)
        return own.astype(F32) + swap_core(own).astype(F32)


def sum_small(values):
    for turn in (1, 2, 4, 8):
        values = values + lax.ppermute(values, "fsdp", [(chip, chip ^ turn) for chip in range(UNITS)])
    return values


def side_columns(matrix, core, width):
    return lax.dynamic_slice_in_dim(matrix, core * width, width, axis=1)


def side_rows(blocks, core):
    return lax.dynamic_index_in_dim(blocks, core, 1, keepdims=False)


def pack_first(qkv, mod_turned, vectors, core):
    count = vectors.shape[0]
    mod_blocks = side_rows(mod_turned.reshape(count, 2, 3, 48, COND), core)
    padded = jnp.pad(vectors, ((0, 0), (0, 640 - VECTOR_PART))).reshape(count, 5, 128)
    return jnp.concatenate(
        [
            side_columns(qkv, core, QKV_HALF).reshape(count, 48, QKV_HALF),
            mod_blocks.transpose(0, 2, 1, 3).reshape(count, 48, 3 * COND),
            jnp.pad(padded, ((0, 0), (0, 43), (0, 0))),
        ],
        axis=2,
    )


def pack_second(out, up, down, core):
    count = out.shape[0] // 48
    down_blocks = side_rows(down.reshape(count, 2, 2, 48, D), core)
    return jnp.concatenate(
        [
            side_columns(up, core, FF // 2).reshape(count, 48, FF // 2),
            down_blocks.transpose(0, 2, 1, 3).reshape(count, 48, 2 * D),
            side_columns(out, core, D // 2).reshape(count, 48, D // 2),
        ],
        axis=2,
    )


def unpack_qkv(sides):
    return jnp.concatenate([side for side in sides], axis=2).reshape(-1, 3 * D)


def unpack_small(own, first, second, far):
    units = jnp.stack([own, first, second, far], axis=1).reshape(UNITS, 48, SMALL_WIDE)
    turned = units[:, :, : 6 * COND].reshape(UNITS, 48, 6, COND).transpose(0, 2, 1, 3).reshape(6 * D, COND)
    vectors = units[:, :5, 6 * COND :].reshape(UNITS, 640)[:, :VECTOR_PART]
    return (turned.T, vectors.reshape(-1))


def unpack_second(sides):
    count = sides[0].shape[0]
    up = jnp.concatenate([side[:, :, UP_AT : UP_AT + FF // 2] for side in sides], axis=2).reshape(count * 48, FF)
    out = jnp.concatenate([side[:, :, OUT_AT:] for side in sides], axis=2).reshape(count * 48, D)
    down = jnp.stack([side[:, :, DOWN_AT : DOWN_AT + 2 * D] for side in sides], axis=1)
    down = down.reshape(count, 2, 48, 2, D).transpose(0, 1, 3, 2, 4).reshape(count * 192, D)
    return (out, up, down)


def gather_plain(parts, axes):
    return [lax.all_gather(part, "fsdp", axis=axis, tiled=True) for part, axis in zip(parts, axes)]


def virtual_units(pack, cuts):
    return [
        packed[4 * part + start : 4 * part + stop] for packed in (pack(0), pack(1)) for part in range(4) for start, stop in cuts
    ]


def reduce_plain(grads, axes):
    parts = [
        lax.psum_scatter(grad.astype(F32), "fsdp", scatter_dimension=axis, tiled=True) for grad, axis in zip(grads, axes)
    ]
    return tuple(lax.psum(part.astype(BF), "rep").astype(F32) for part in parts)


def adam_direction(weight, first_old, second_old, gradient, decay_rate):
    first_new = BETA_ONE * first_old + (1.0 - BETA_ONE) * gradient
    second_new = BETA_TWO * second_old + (1.0 - BETA_TWO) * gradient * gradient
    direction = (
        first_new
        / (1.0 - BETA_ONE**STEP)
        / (jnp.sqrt(second_new / (1.0 - BETA_TWO**STEP)) + EPSILON)
        + decay_rate * weight
    )
    return (first_new, second_new, direction)


def layout_tables(sizes_row, lengths_row):
    slot_ids = jnp.arange(SLOTS, dtype=jnp.int32)
    seg_ends = jnp.cumsum(sizes_row)
    starts = seg_ends - sizes_row
    segment = jnp.sum((slot_ids[:, None] >= seg_ends[None, :]).astype(jnp.int32), axis=1)
    member = segment[:, None] == jnp.arange(NSEG, dtype=jnp.int32)[None, :]
    offset = jnp.sum(jnp.where(member, starts[None, :], 0), axis=1)
    length_of = jnp.sum(jnp.where(member, lengths_row[None, :], 0), axis=1)
    position = slot_ids - offset
    return (segment, member, position, position < length_of)


def condition(steps_row):
    half_cond = COND // 2
    frequency = jnp.exp(jnp.arange(half_cond, dtype=F32) * (-math.log(10000.0) / half_cond))
    angles = steps_row.astype(F32)[:, None] * frequency[None, :]
    return jax.nn.silu(jnp.concatenate([jnp.cos(angles), jnp.sin(angles)], axis=1))


FORWARD_CALLS = (2, 3, 1)
BACKWARD_CALLS = (1, 3, 2)


def on_device(
    inputs, cotangent, seg_sizes, seq_lengths, timesteps, absorbed,
    qkv_weight, out_weight, up_weight, down_weight, mod_weight,
    qkv_first, out_first, up_first, down_first, mod_first,
    qkv_second, out_second, up_second, down_second, mod_second,
    vectors, vectors_first, vectors_second,
):
    rounds = by_rounds()
    chip = lax.axis_index("fsdp")
    core = lax.axis_index("rep")
    matrices = (qkv_weight, out_weight, up_weight, down_weight, mod_weight)
    qkv_low, out_low, up_low, down_low, mod_low = [matrix.astype(BF) for matrix in matrices]
    vector_low = vectors.astype(BF)
    if rounds:
        order = jnp.concatenate([jnp.asarray(ORIGIN)[core, chip], jnp.asarray(ORIGIN)[1 - core, chip]])
        places = jnp.asarray(PLACES)[core, chip]
        side = core[None].astype(jnp.int32)
        unit_first = pack_first(qkv_low, mod_low.T, vector_low[None], core)[0]
        unit_second = pack_second(out_low, up_low, down_low, core)[0]
        second_one = unit_second[None]
        first_back = [along_z(unit_first, back) for back in range(1, 4)]
        second_near = near_of(second_one)
        first_column = jnp.stack([unit_first] + first_back)
        first_near = near_of(first_column)
        second_from = hold_back(unit_second, first_column)
        second_back = [along_z(second_from, back) for back in range(1, 4)]
        second_far = far_from(second_near)
        first_near[0] = hold_back(first_near[0], (second_far, second_near, second_back))
        units_first = [first_column] + first_near + [far_from(first_near)]
        units_first = units_first + swapped(units_first)
    else:
        order = jnp.concatenate([jnp.arange(UNITS, dtype=jnp.int32)] * 2)
        places = jnp.asarray(PLACES)[0, 0]
        side = jnp.zeros((1,), jnp.int32)
        qkv_all, mod_all, vector_all = gather_plain((qkv_low, mod_low, vector_low), (0, 1, 0))
        out_all, up_all, down_all = gather_plain((out_low, up_low, down_low), (0, 0, 0))
        units_first = virtual_units(lambda s: pack_first(qkv_all, mod_all.T, vector_all.reshape(UNITS, -1), s), ((0, 4),))
        units_second = virtual_units(lambda s: pack_second(out_all, up_all, down_all, s), ((0, 1), (1, 4)))

    segment, member, position, valid_slot = layout_tables(seg_sizes[0], seq_lengths[0])
    tiles = segment.reshape(BLOCKS, TILE)[:, 0]
    member_tile = member.reshape(BLOCKS, TILE, NSEG)[:, 0].astype(F32)
    condition_low = condition(timesteps[0]).astype(BF)
    cos, sin, feature_query, feature_key = attention_tables(segment, position, valid_slot)
    weight_mask = (absorbed[0] * valid_slot.astype(jnp.int32)).astype(F32).reshape(BLOCKS, TILE)
    row_in, row_cot = inputs[0], cotangent[0]

    mixed, first_low, qkv_full, modulation, flat = first_part(
        units_first, order, side, tiles, row_in, condition_low, cos, sin
    )
    forward, first_pair = None, 0
    if rounds:
        second_rest = jnp.stack(second_back)
        second_rest_near = near_of(second_rest)
    for number, count in enumerate(FORWARD_CALLS):
        if rounds and number == 1:
            second_rest_far = far_from(hold_back(second_rest_near, forward))
            second_own = [second_one, second_rest, second_near[0], second_rest_near[0], second_near[1], second_rest_near[1]]
            second_own.append(second_far)
            second_other = swapped(hold_back(second_own, forward))
        if rounds and number == 2:
            forward, second_rest_far = hold_back((forward, second_rest_far), second_other)
        forward = attention_forward(mixed, feature_query, feature_key, forward, first_pair, count)
        first_pair += count
    if rounds:
        units_second = second_own + [second_rest_far] + second_other + [swap_core(second_rest_far)]
    attended_low, feature = forward
    out_hidden, left, right, grad_middle, grad_attended, sums, bias_sums = middle_part(
        units_second, order, side, tiles, attended_low, row_in, row_cot, weight_mask, modulation, flat
    )
    mine_later, give_later = later_grads(side, left, right)

    state = [None]

    def backward_part(number, came):
        grad_here = grad_attended if came is None else hold_back(grad_attended, came)
        state[0] = attention_backward(
            mixed, feature, feature_key, grad_here, attended_low, cos, sin, state[0],
            sum(BACKWARD_CALLS[:number]), BACKWARD_CALLS[number],
        )
        return state[0]

    def qkv_end(sooner=None):
        follows = state[0] if sooner is None else hold_back(state[0], sooner)
        return qkv_grads(side, first_low, follows)

    def row_end(sooner=None):
        follows = state[0] if sooner is None else hold_back(state[0], sooner)
        return last_part(
            places, tiles, member_tile, follows, qkv_full, row_in, grad_middle, modulation, flat, condition_low,
            sums, bias_sums,
        )

    vector_arrays = (vectors, vectors_first, vectors_second)
    of_qkv, of_out = (qkv_weight, qkv_first, qkv_second), (out_weight, out_first, out_second)
    of_up, of_down = (up_weight, up_first, up_second), (down_weight, down_first, down_second)
    of_mod = (mod_weight, mod_first, mod_second)
    if rounds:
        later = Scatter(mine_later, give_later, places)
        backward_part(0, None)
        sent = later.send_far(state[0])
        backward_part(1, sent)
        sent = later.send_first(state[0])
        backward_part(2, sent)
        sent = later.send_column(state[0])
        qkv_parts = qkv_end(sent)
        sooner = Scatter(*qkv_parts, places)
        sent = sooner.send_plane()
        grad_in, *small_parts = row_end(sent)
        small = SmallScatter(*small_parts, places)
        sent = sooner.send_column(grad_in)
        sent = small.send_column((sent, sooner.came, later.came))
        later_sums = later.finish(sent)
        (out_new, up_new, down_new), later_table = update_moments(
            update_later_kernel, side, later_sums, of_out + of_up + of_down
        )
        qkv_sums = sooner.finish(sent)
        small_sums = small.finish()
        (qkv_new, mod_new), sooner_table = update_moments(
            update_sooner_kernel, side, qkv_sums + (small_sums,), of_qkv + tuple(part.T for part in of_mod)
        )
        results = [qkv_new, out_new, up_new, down_new, mod_new]
        *renewed, norm_roots = renew(
            sum_small(later_table + sooner_table),
            [*matrices[:4], mod_weight.T],
            [record[2] for record in results],
        )
        renewed[4] = renewed[4].T
        results[4] = [part.T for part in mod_new]
        grad_vectors = small_sums[:5, 6 * COND :].reshape(-1)[:VECTOR_PART]
    else:
        for number in range(3):
            backward_part(number, None)
        grad_out, grad_up, grad_down = reduce_plain(unpack_second((mine_later, give_later)), (0, 0, 0))
        grad_in, *small_parts = row_end()
        grad_qkv, grad_mod, grad_vectors = reduce_plain(
            (unpack_qkv(qkv_end()), *unpack_small(*small_parts)), (0, 1, 0)
        )
        grads = (grad_qkv, grad_out, grad_up, grad_down, grad_mod)
        olds = (of_qkv, of_out, of_up, of_down, of_mod)
        results = [adam_direction(*old, grad, DECAY_RATE) for old, grad in zip(olds, grads)]
        squares = [
            jnp.stack([jnp.sum(values[number] * values[number]) for number in range(5)])
            for values in (matrices, [record[2] for record in results])
        ]
        norm_roots = jnp.sqrt(lax.psum(jnp.stack(squares), "fsdp"))
        trust = norm_roots[0] / (norm_roots[1] + EPSILON)
        renewed = [matrices[number] - MATRIX_RATE * trust[number] * results[number][2] for number in range(5)]
    vector_record = adam_direction(*vector_arrays, grad_vectors, 0.0)
    return (
        out_hidden[None],
        grad_in[None],
        *renewed,
        *[record[0] for record in results],
        *[record[1] for record in results],
        vectors - VECTOR_RATE * vector_record[2],
        vector_record[0],
        vector_record[1],
        norm_roots,
    )


def solution(mesh):
    rows = P(("rep", "fsdp"))
    matrix, turned, vector = P("fsdp", None), P(None, "fsdp"), P("fsdp")
    five = (matrix, matrix, matrix, matrix, turned)
    return jax.shard_map(
        on_device,
        mesh=mesh,
        in_specs=(rows,) * 6 + five * 3 + (vector,) * 3,
        out_specs=(rows, rows) + five * 3 + (vector,) * 3 + (P(),),
        check_vma=False,
    )
```

profile of v0, /device:TPU:0, one launch (start us, length us, event | category | flops | bytes accessed | tf_op | source)
XLA Modules:
  0.0 359.2 jit_solution(14248958340972228262)
XLA Ops:
  3.4 5.1 %collective-permute-start.2 = (bf16[48,1664]{1,0:T(8,128)(2,1)S(1)}, bf16[48,1664]{1,0:T(8,128)(2,1)S(1)}, u32[]{:S(2)}, u32[]{:S(2)}) collective-permute-start(bf16[48,1664]{1,0:T(8,128)(2,1)S(1)} %maximum_bitcast_fusion), channel_id=1, source_target_pairs={{0,12},{1,13},{2,14},{3,15},{4,0},{5,1},{6,2},{7,3},{8,4},{9,5},{1... | collective-permute-start | bytes 479240 | tf_op jit(solution)/shard_map/ppermute | solution.py:794
  17.7 4.3 %collective-permute-done.1 = bf16[48,1664]{1,0:T(8,128)(2,1)S(1)} collective-permute-done((bf16[48,1664]{1,0:T(8,128)(2,1)S(1)}, bf16[48,1664]{1,0:T(8,128)(2,1)S(1)}, u32[]{:S(2)}, u32[]{:S(2)}) %collective-permute-start.1) | collective-permute-done | bytes 159776 | tf_op jit(solution)/shard_map/ppermute | solution.py:794
  34.9 20.1 %collective-permute-done.4 = bf16[48,3456]{1,0:T(8,128)(2,1)S(1)} collective-permute-done((bf16[48,3456]{1,0:T(8,128)(2,1)S(1)}, bf16[48,3456]{1,0:T(8,128)(2,1)S(1)}, u32[]{:S(2)}, u32[]{:S(2)}) %collective-permute-start.4) | collective-permute-done | bytes 331808 | tf_op jit(solution)/shard_map/ppermute | solution.py:794
  59.1 6.3 %collective-permute-done.13.refs_3_ = bf16[4,48,1664]{2,1,0:T(8,128)(2,1)S(1)} collective-permute-done((bf16[4,48,1664]{2,1,0:T(8,128)(2,1)S(1)}, bf16[4,48,1664]{2,1,0:T(8,128)(2,1)S(1)}, u32[]{:S(2)}, u32[]{:S(2)}) %collective-permute-start.13) | collective-permute-done | bytes 639008 | tf_op jit(solution)/shard_map/ppermute | solution.py:803
  71.9 13.5 %shard_map.409 = (bf16[1024,2304]{1,0:T(8,128)(2,1)}, bf16[1024,768]{1,0:T(8,128)(2,1)}, bf16[768,2304]{1,0:T(8,128)(2,1)}, f32[8,4608]{1,0:T(8,128)}, f32[80,128]{1,0:T(8,128)}) custom-call(s32[32]{0:T(128)} %pad_add_fusion.order_ref, s32[1]{0:T(128)} %bitcast.2.core_ref.side_ref, s32[8]{0:T(128)} %get-tuple-element.238.tiles_ref, ...), custom_call_target="tpu_custom_call" | custom-call | flops 3623878656 | bytes 20971520 | tf_op jit(solution)/shard_map/pallas_call | solution.py:325
  85.5 7.6 %shard_map.410 = (bf16[1024,768]{1,0:T(8,128)(2,1)S(1)}, bf16[1024,768]{1,0:T(8,128)(2,1)S(1)}) custom-call(bf16[1024,2304]{1,0:T(8,128)(2,1)} %get-tuple-element.125.q_ref.k_ref.v_ref, bf16[1024,2304]{1,0:T(8,128)(2,1)} %get-tuple-element.125.q_ref.k_ref.v_ref, bf16[1024,2304]{1,0:T(8,128)(2,1)} %get-tuple-element.125.q_ref.k_ref.v_ref, ...), custom_call_target="tpu_custom_call" | custom-call | flops 12582912000 | bytes 2621440 | tf_op jit(solution)/shard_map/pallas_call | solution.py:97
  96.5 11.0 %shard_map.411 = (bf16[1024,768]{1,0:T(8,128)(2,1)S(1)}, bf16[1024,768]{1,0:T(8,128)(2,1)S(1)}) custom-call(bf16[1024,2304]{1,0:T(8,128)(2,1)} %get-tuple-element.125.q_ref.k_ref.v_ref, bf16[1024,2304]{1,0:T(8,128)(2,1)} %get-tuple-element.125.q_ref.k_ref.v_ref, ...), custom_call_target="tpu_custom_call", output_to_operand_aliasing={{0}: (5, {}), {1}: (6, {})} | custom-call | flops 18874368000 | bytes 3932160 | tf_op jit(solution)/shard_map/pallas_call | solution.py:97
  108.9 4.9 %shard_map.412 = (bf16[1024,768]{1,0:T(8,128)(2,1)S(1)}, bf16[1024,768]{1,0:T(8,128)(2,1)S(1)}) custom-call(bf16[1024,2304]{1,0:T(8,128)(2,1)} %get-tuple-element.125.q_ref.k_ref.v_ref, bf16[1024,2304]{1,0:T(8,128)(2,1)} %get-tuple-element.125.q_ref.k_ref.v_ref, ...), custom_call_target="tpu_custom_call", output_to_operand_aliasing={{0}: (5, {}), {1}: (6, {})} | custom-call | flops 6291456000 | bytes 1310720 | tf_op jit(solution)/shard_map/pallas_call | solution.py:97
  116.1 38.5 %shard_map.413 = (bf16[1024,768]{1,0:T(8,128)(2,1)}, bf16[1024,4608]{1,0:T(8,128)(2,1)}, bf16[1024,4608]{1,0:T(8,128)(2,1)}, f32[1024,768]{1,0:T(8,128)}, bf16[1...) custom-call(s32[32]{0:T(128)} %pad_add_fusion.order_ref, s32[1]{0:T(128)} %bitcast.2.core_ref.side_ref, ...), custom_call_target="tpu_custom_call" | custom-call | flops 21743271936 | bytes 52428800 | tf_op jit(solution)/shard_map/pallas_call | solution.py:444
  154.7 19.5 %shard_map.414 = (bf16[16,48,3456]{2,1,0:T(8,128)(2,1)S(1)}, bf16[16,48,3456]{2,1,0:T(8,128)(2,1)}) custom-call(s32[1]{0:T(128)} %bitcast.2.core_ref.side_ref, bf16[1024,4608]{1,0:T(8,128)(2,1)} %get-tuple-element.147.left_ref, bf16[1024,4608]{1,0:T(8,128)(2,1)} %get-tuple-element.148.right_ref), custom_call_target="tpu_custom_call" | custom-call | flops 10871635968 | bytes 41943040 | tf_op jit(solution)/shard_map/pallas_call | solution.py:526
  177.2 8.8 %shard_map.415.refs_0_ = bf16[3,1024,768]{2,1,0:T(8,128)(2,1)} custom-call(bf16[1024,2304]{1,0:T(8,128)(2,1)} %get-tuple-element.125.q_ref.k_ref.v_ref, bf16[1024,2304]{1,0:T(8,128)(2,1)} %get-tuple-element.125.q_ref.k_ref.v_ref, bf16[1024,2304]{1,0:T(8,128)(2,1)} %get-tuple-element.125.q_ref.k_ref.v_ref, bf16[1024,768]{1,0:T(8,128)(2,1)S(1)} %get-tuple-element.145.fo_ref, ...), custom_call_target="tpu_custom_call" | custom-call | flops 4194304000 | bytes 2621440 | tf_op jit(solution)/shard_map/pallas_call | solution.py:175
  188.3 4.0 %shard_map.416 = (bf16[4,48,3456]{2,1,0:T(8,128)(2,1)S(1)}, bf16[4,48,3456]{2,1,0:T(8,128)(2,1)S(1)}) custom-call(s32[8]{0:T(128)S(1)} %fusion.9.places_ref.refs_0_, bf16[4,4,48,3456]{3,2,1,0:T(8,128)(2,1)} %bitcast.80, bf16[4,4,48,3456]{3,2,1,0:T(8,128)(2,1)} %bitcast.105, bf16[4,4,48,3456]{3,2,1,0:T(8,128)(2,1)} %bitcast.81, bf16[4,4,48,3456]{3,2,1,0:T(8,128)(2,1)} %bitcast.106), custom_call_target="tpu_custom_call" | custom-call | bytes 12582912 | tf_op jit(solution)/shard_map/pallas_call | solution.py:864
  194.4 22.5 %shard_map.417.refs_0_ = bf16[3,1024,768]{2,1,0:T(8,128)(2,1)} custom-call(bf16[1024,2304]{1,0:T(8,128)(2,1)} %get-tuple-element.125.q_ref.k_ref.v_ref, bf16[1024,2304]{1,0:T(8,128)(2,1)} %get-tuple-element.125.q_ref.k_ref.v_ref, bf16[1024,2304]{1,0:T(8,128)(2,1)} %get-tuple-element.125.q_ref.k_ref.v_ref, ...), custom_call_target="tpu_custom_call", output_to_operand_aliasing={{}: (9, {})} | custom-call | flops 12582912000 | bytes 7864320 | tf_op jit(solution)/shard_map/pallas_call | solution.py:175
  216.9 7.5 %collective-permute-done.29.refs_3_.refs_7_.refs_11_.refs_15_ = bf16[4,48,3456]{2,1,0:T(8,128)(2,1)S(1)} collective-permute-done((bf16[4,48,3456]{2,1,0:T(8,128)(2,1)S(1)}, bf16[4,48,3456]{2,1,0:T(8,128)(2,1)S(1)}, u32[]{:S(2)}, u32[]{:S(2)}) %collective-permute-start.29) | collective-permute-done | bytes 1327136 | tf_op jit(solution)/shard_map/ppermute | solution.py:803
  228.8 16.0 %shard_map.419.g_ref = bf16[3,1024,768]{2,1,0:T(8,128)(2,1)} custom-call(bf16[1024,2304]{1,0:T(8,128)(2,1)} %get-tuple-element.125.q_ref.k_ref.v_ref, bf16[1024,2304]{1,0:T(8,128)(2,1)} %get-tuple-element.125.q_ref.k_ref.v_ref, bf16[1024,2304]{1,0:T(8,128)(2,1)} %get-tuple-element.125.q_ref.k_ref.v_ref, ...), custom_call_target="tpu_custom_call", output_to_operand_aliasing={{}: (9, {})} | custom-call | flops 8388608000 | bytes 5242880 | tf_op jit(solution)/shard_map/pallas_call | solution.py:175
  245.5 3.4 shard_map.420
  250.4 7.8 %shard_map.421 = (bf16[16,48,1152]{2,1,0:T(8,128)(2,1)S(1)}, bf16[16,48,1152]{2,1,0:T(8,128)(2,1)}) custom-call(s32[1]{0:T(128)} %bitcast.2.core_ref.side_ref, bf16[1024,768]{1,0:T(8,128)(2,1)S(1)} %copy-done.9, bf16[3,1024,768]{2,1,0:T(8,128)(2,1)} %shard_map.419.g_ref), custom_call_target="tpu_custom_call" | custom-call | flops 603979776 | bytes 1048576 | tf_op jit(solution)/shard_map/pallas_call | solution.py:567
  258.4 3.8 %collective-permute-done.31 = bf16[16,48,1152]{2,1,0:T(8,128)(2,1)S(1)} collective-permute-done((bf16[16,48,1152]{2,1,0:T(8,128)(2,1)}, bf16[16,48,1152]{2,1,0:T(8,128)(2,1)S(1)}, u32[]{:S(2)}, u32[]{:S(2)}) %collective-permute-start.31) | collective-permute-done | bytes 1769504 | tf_op jit(solution)/shard_map/ppermute | solution.py:811
  270.6 13.4 %shard_map.423 = (f32[1024,768]{1,0:T(8,128)}, bf16[4,48,896]{2,1,0:T(8,128)(2,1)}, bf16[4,48,896]{2,1,0:T(8,128)(2,1)}, bf16[4,48,896]{2,1,0:T(8,128)(2,1)}, bf16[4,48,896]{2,1,0:T(8,128)(2,1)}) custom-call(s32[8]{0:T(128)} %copy-done.26, s32[8]{0:T(128)} %get-tuple-element.238.tiles_ref, f32[8,8]{1,0:T(8,128)} %convert_bitcast_fusion.member_ref, ...), custom_call_target="tpu_custom_call" | custom-call | flops 3623878656 | bytes 31457280 | tf_op jit(solution)/shard_map/pallas_call | solution.py:661
  292.6 9.3 %collective-permute-done.33 = bf16[48,3456]{1,0:T(8,128)(2,1)S(1)} collective-permute-done((bf16[48,3456]{1,0:T(8,128)(2,1)}, bf16[48,3456]{1,0:T(8,128)(2,1)S(1)}, u32[]{:S(2)}, u32[]{:S(2)}) %collective-permute-start.33) | collective-permute-done | bytes 331808 | tf_op jit(solution)/shard_map/ppermute | solution.py:794
  301.9 5.8 %collective-permute-start.41 = (bf16[48,1152]{1,0:T(8,128)(2,1)S(1)}, bf16[48,1152]{1,0:T(8,128)(2,1)S(1)}, u32[]{:S(2)}, u32[]{:S(2)}) collective-permute-start(bf16[48,1152]{1,0:T(8,128)(2,1)S(1)} %get-tuple-element.185), channel_id=1, source_target_pairs={{0,4},{1,5},{2,6},{3,7},{4,8},{5,9},{6,10},{7,11},{8,12},{9,13},{1... | collective-permute-start | bytes 331784 | tf_op jit(solution)/shard_map/ppermute | solution.py:794
  314.4 4.1 %collective-permute-done.42 = bf16[48,1152]{1,0:T(8,128)(2,1)S(1)} collective-permute-done((bf16[48,1152]{1,0:T(8,128)(2,1)S(1)}, bf16[48,1152]{1,0:T(8,128)(2,1)S(1)}, u32[]{:S(2)}, u32[]{:S(2)}) %collective-permute-start.42) | collective-permute-done | bytes 110624 | tf_op jit(solution)/shard_map/ppermute | solution.py:794
  327.5 6.6 %collective-permute-done.47 = bf16[48,896]{1,0:T(8,128)(2,1)S(1)} collective-permute-done((bf16[48,896]{1,0:T(8,128)(2,1)}, bf16[48,896]{1,0:T(8,128)(2,1)S(1)}, u32[]{:S(2)}, u32[]{:S(2)}) %collective-permute-start.47) | collective-permute-done | bytes 86048 | tf_op jit(solution)/shard_map/ppermute | solution.py:794
  349.4 3.6 %collective-permute-done.52 = f32[8,128]{1,0:T(8,128)S(1)} collective-permute-done((f32[8,128]{1,0:T(8,128)S(1)}, f32[8,128]{1,0:T(8,128)S(1)}, u32[]{:S(2)}, u32[]{:S(2)}) %collective-permute-start.52) | collective-permute-done | bytes 4128 | tf_op jit(solution)/shard_map/ppermute | solution.py:960
  (297 shorter events, 109.9 us)
Async XLA Ops:
  3.4 14.3 %collective-permute-start.2 = (bf16[48,1664]{1,0:T(8,128)(2,1)S(1)}, bf16[48,1664]{1,0:T(8,128)(2,1)S(1)}, u32[]{:S(2)}, u32[]{:S(2)}) collective-permute-start(bf16[48,1664]{1,0:T(8,128)(2,1)S(1)} %maximum_bitcast_fusion), channel_id=1, source_target_pairs={{0,12},{1,13},{2,14},{3,15},{4,0},{5,1},{6,2},{7,3},{8,4},{9,5},{1... | collective-permute-start | bytes 479240 | tf_op jit(solution)/shard_map/ppermute | solution.py:794
  8.5 13.5 %collective-permute-start.1 = (bf16[48,1664]{1,0:T(8,128)(2,1)S(1)}, bf16[48,1664]{1,0:T(8,128)(2,1)S(1)}, u32[]{:S(2)}, u32[]{:S(2)}) collective-permute-start(bf16[48,1664]{1,0:T(8,128)(2,1)S(1)} %maximum_bitcast_fusion), channel_id=1, source_target_pairs={{0,8},{1,9},{2,10},{3,11},{4,12},{5,13},{6,14},{7,15},{8,0},{9,1},... | collective-permute-start | bytes 479240 | tf_op jit(solution)/shard_map/ppermute | solution.py:794
  12.9 13.9 %collective-permute-start.6 = (bf16[1,48,3456]{2,1,0:T(8,128)(2,1)S(1)}, bf16[1,48,3456]{2,1,0:T(8,128)(2,1)S(1)}, u32[]{:S(2)}, u32[]{:S(2)}) collective-permute-start(bf16[1,48,3456]{2,1,0:T(8,128)(2,1)S(1)} %get-tuple-element.131.refs_0_), channel_id=1, source_target_pairs={{0,1},{1,0},{2,3},{3,2},{4,5},{5,4},{6,7},{7,6},{8,9},{9,8},{10,11... | collective-permute-start | bytes 995336 | tf_op jit(solution)/shard_map/ppermute | solution.py:803
  14.4 14.3 %collective-permute-start.8 = (bf16[1,48,3456]{2,1,0:T(8,128)(2,1)S(1)}, bf16[1,48,3456]{2,1,0:T(8,128)(2,1)S(1)}, u32[]{:S(2)}, u32[]{:S(2)}) collective-permute-start(bf16[1,48,3456]{2,1,0:T(8,128)(2,1)S(1)} %get-tuple-element.131.refs_0_), channel_id=1, source_target_pairs={{0,2},{1,3},{2,0},{3,1},{4,6},{5,7},{6,4},{7,5},{8,10},{9,11},{10,... | collective-permute-start | bytes 995336 | tf_op jit(solution)/shard_map/ppermute | solution.py:803
  22.1 32.8 %collective-permute-start.11 = (bf16[4,48,1664]{2,1,0:T(8,128)(2,1)S(1)}, bf16[4,48,1664]{2,1,0:T(8,128)(2,1)S(1)}, u32[]{:S(2)}, u32[]{:S(2)}) collective-permute-start(bf16[4,48,1664]{2,1,0:T(8,128)(2,1)S(1)} %pad_maximum_fusion.1.refs_0_), channel_id=1, source_target_pairs={{0,1},{1,0},{2,3},{3,2},{4,5},{5,4},{6,7},{7,6},{8,9},{9,8},{10,11... | collective-permute-start | bytes 1916936 | tf_op jit(solution)/shard_map/ppermute | solution.py:803
  25.0 29.9 %collective-permute-start.4 = (bf16[48,3456]{1,0:T(8,128)(2,1)S(1)}, bf16[48,3456]{1,0:T(8,128)(2,1)S(1)}, u32[]{:S(2)}, u32[]{:S(2)}) collective-permute-start(bf16[48,3456]{1,0:T(8,128)(2,1)S(1)} %get-tuple-element.123), channel_id=1, source_target_pairs={{0,8},{1,9},{2,10},{3,11},{4,12},{5,13},{6,14},{7,15},{8,0},{9,1},... | collective-permute-start | bytes 995336 | tf_op jit(solution)/shard_map/ppermute | solution.py:794
  26.7 28.2 %collective-permute-start.3 = (bf16[48,3456]{1,0:T(8,128)(2,1)S(1)}, bf16[48,3456]{1,0:T(8,128)(2,1)S(1)}, u32[]{:S(2)}, u32[]{:S(2)}) collective-permute-start(bf16[48,3456]{1,0:T(8,128)(2,1)S(1)} %get-tuple-element.123), channel_id=1, source_target_pairs={{0,4},{1,5},{2,6},{3,7},{4,8},{5,9},{6,10},{7,11},{8,12},{9,13},{1... | collective-permute-start | bytes 995336 | tf_op jit(solution)/shard_map/ppermute | solution.py:794
  28.7 26.2 %collective-permute-start.10 = (bf16[1,48,3456]{2,1,0:T(8,128)(2,1)S(1)}, bf16[1,48,3456]{2,1,0:T(8,128)(2,1)S(1)}, u32[]{:S(2)}, u32[]{:S(2)}) collective-permute-start(bf16[1,48,3456]{2,1,0:T(8,128)(2,1)S(1)} %collective-permute-done.6.refs_2_), channel_id=1, source_target_pairs={{0,2},{1,3},{2,0},{3,1},{4,6},{5,7},{6,4},{7,5},{8,10},{9,11},{10,... | collective-permute-start | bytes 995336 | tf_op jit(solution)/shard_map/ppermute | solution.py:803
  33.5 25.6 %collective-permute-start.12 = (bf16[4,48,1664]{2,1,0:T(8,128)(2,1)S(1)}, bf16[4,48,1664]{2,1,0:T(8,128)(2,1)S(1)}, u32[]{:S(2)}, u32[]{:S(2)}) collective-permute-start(bf16[4,48,1664]{2,1,0:T(8,128)(2,1)S(1)} %pad_maximum_fusion.1.refs_0_), channel_id=1, source_target_pairs={{0,2},{1,3},{2,0},{3,1},{4,6},{5,7},{6,4},{7,5},{8,10},{9,11},{10,... | collective-permute-start | bytes 1916936 | tf_op jit(solution)/shard_map/ppermute | solution.py:803
  68.1 25.0 %collective-permute-start.7 = (bf16[3,48,3456]{2,1,0:T(8,128)(2,1)S(1)}, bf16[3,48,3456]{2,1,0:T(8,128)(2,1)S(1)}, u32[]{:S(2)}, u32[]{:S(2)}) collective-permute-start(bf16[3,48,3456]{2,1,0:T(8,128)(2,1)S(1)} %pad_maximum_fusion.refs_1_), channel_id=1, source_target_pairs={{0,1},{1,0},{2,3},{3,2},{4,5},{5,4},{6,7},{7,6},{8,9},{9,8},{10,11... | collective-permute-start | bytes 2985992 | tf_op jit(solution)/shard_map/ppermute | solution.py:803
  69.7 23.5 %collective-permute-start.9 = (bf16[3,48,3456]{2,1,0:T(8,128)(2,1)S(1)}, bf16[3,48,3456]{2,1,0:T(8,128)(2,1)S(1)}, u32[]{:S(2)}, u32[]{:S(2)}) collective-permute-start(bf16[3,48,3456]{2,1,0:T(8,128)(2,1)S(1)} %pad_maximum_fusion.refs_1_), channel_id=1, source_target_pairs={{0,2},{1,3},{2,0},{3,1},{4,6},{5,7},{6,4},{7,5},{8,10},{9,11},{10,... | collective-permute-start | bytes 2985992 | tf_op jit(solution)/shard_map/ppermute | solution.py:803
  93.8 14.2 %collective-permute-start.18 = (bf16[3,48,3456]{2,1,0:T(8,128)(2,1)S(1)}, bf16[3,48,3456]{2,1,0:T(8,128)(2,1)S(1)}, u32[]{:S(2)}, u32[]{:S(2)}) collective-permute-start(bf16[3,48,3456]{2,1,0:T(8,128)(2,1)S(1)} %collective-permute-done.7.refs_3_), channel_id=1, source_target_pairs={{0,2},{1,3},{2,0},{3,1},{4,6},{5,7},{6,4},{7,5},{8,10},{9,11},{10,... | collective-permute-start | bytes 2985992 | tf_op jit(solution)/shard_map/ppermute | solution.py:803
  192.3 24.6 %collective-permute-start.28 = (bf16[4,48,3456]{2,1,0:T(8,128)(2,1)S(1)}, bf16[4,48,3456]{2,1,0:T(8,128)(2,1)S(1)}, u32[]{:S(2)}, u32[]{:S(2)}) collective-permute-start(bf16[4,48,3456]{2,1,0:T(8,128)(2,1)S(1)} %get-tuple-element.152), channel_id=1, source_target_pairs={{0,2},{1,3},{2,0},{3,1},{4,6},{5,7},{6,4},{7,5},{8,10},{9,11},{10,... | collective-permute-start | bytes 3981320 | tf_op jit(solution)/shard_map/ppermute | solution.py:803
  193.9 30.5 %collective-permute-start.29 = (bf16[4,48,3456]{2,1,0:T(8,128)(2,1)S(1)}, bf16[4,48,3456]{2,1,0:T(8,128)(2,1)S(1)}, u32[]{:S(2)}, u32[]{:S(2)}) collective-permute-start(bf16[4,48,3456]{2,1,0:T(8,128)(2,1)S(1)} %get-tuple-element.153), channel_id=1, source_target_pairs={{0,2},{1,3},{2,0},{3,1},{4,6},{5,7},{6,4},{7,5},{8,10},{9,11},{10,... | collective-permute-start | bytes 3981320 | tf_op jit(solution)/shard_map/ppermute | solution.py:803
  227.6 17.8 %collective-permute-start.30 = (bf16[4,48,3456]{2,1,0:T(8,128)(2,1)S(1)}, bf16[4,48,3456]{2,1,0:T(8,128)(2,1)S(1)}, u32[]{:S(2)}, u32[]{:S(2)}) collective-permute-start(bf16[4,48,3456]{2,1,0:T(8,128)(2,1)S(1)} %shard_map.418), channel_id=1, source_target_pairs={{0,1},{1,0},{2,3},{3,2},{4,5},{5,4},{6,7},{7,6},{8,9},{9,8},{10,11... | collective-permute-start | bytes 3981320 | tf_op jit(solution)/shard_map/ppermute | solution.py:803
  264.4 21.1 %collective-permute-start.38 = (bf16[4,48,1152]{2,1,0:T(8,128)(2,1)}, bf16[4,48,1152]{2,1,0:T(8,128)(2,1)S(1)}, u32[]{:S(2)}, u32[]{:S(2)}) collective-permute-start(bf16[4,48,1152]{2,1,0:T(8,128)(2,1)} %get-tuple-element.165), channel_id=1, source_target_pairs={{0,3},{1,2},{2,1},{3,0},{4,7},{5,6},{6,5},{7,4},{8,11},{9,10},{10,... | collective-permute-start | bytes 1327112 | tf_op jit(solution)/shard_map/ppermute | solution.py:807
  266.5 18.9 %collective-permute-start.32 = (bf16[48,3456]{1,0:T(8,128)(2,1)}, bf16[48,3456]{1,0:T(8,128)(2,1)}, u32[]{:S(2)}, u32[]{:S(2)}) collective-permute-start(bf16[48,3456]{1,0:T(8,128)(2,1)} %get-tuple-element.172), channel_id=1, source_target_pairs={{0,4},{1,5},{2,6},{3,7},{4,8},{5,9},{6,10},{7,11},{8,12},{9,13},{1... | collective-permute-start | bytes 995336 | tf_op jit(solution)/shard_map/ppermute | solution.py:794
  268.5 19.6 %collective-permute-start.39 = (bf16[4,48,1152]{2,1,0:T(8,128)(2,1)}, bf16[4,48,1152]{2,1,0:T(8,128)(2,1)}, u32[]{:S(2)}, u32[]{:S(2)}) collective-permute-start(bf16[4,48,1152]{2,1,0:T(8,128)(2,1)} %get-tuple-element.179), channel_id=1, source_target_pairs={{0,1},{1,0},{2,3},{3,2},{4,5},{5,4},{6,7},{7,6},{8,9},{9,8},{10,11... | collective-permute-start | bytes 1327112 | tf_op jit(solution)/shard_map/ppermute | solution.py:803
  269.6 19.3 %collective-permute-start.40 = (bf16[4,48,1152]{2,1,0:T(8,128)(2,1)}, bf16[4,48,1152]{2,1,0:T(8,128)(2,1)}, u32[]{:S(2)}, u32[]{:S(2)}) collective-permute-start(bf16[4,48,1152]{2,1,0:T(8,128)(2,1)} %get-tuple-element.180), channel_id=1, source_target_pairs={{0,2},{1,3},{2,0},{3,1},{4,6},{5,7},{6,4},{7,5},{8,10},{9,11},{10,... | collective-permute-start | bytes 1327112 | tf_op jit(solution)/shard_map/ppermute | solution.py:803
  284.0 27.0 %collective-permute-start.35 = (bf16[4,48,896]{2,1,0:T(8,128)(2,1)}, bf16[4,48,896]{2,1,0:T(8,128)(2,1)S(1)}, u32[]{:S(2)}, u32[]{:S(2)}) collective-permute-start(bf16[4,48,896]{2,1,0:T(8,128)(2,1)} %get-tuple-element.176), channel_id=1, source_target_pairs={{0,3},{1,2},{2,1},{3,0},{4,7},{5,6},{6,5},{7,4},{8,11},{9,10},{10,... | collective-permute-start | bytes 1032200 | tf_op jit(solution)/shard_map/ppermute | solution.py:807
  285.4 16.5 %collective-permute-start.33 = (bf16[48,3456]{1,0:T(8,128)(2,1)}, bf16[48,3456]{1,0:T(8,128)(2,1)S(1)}, u32[]{:S(2)}, u32[]{:S(2)}) collective-permute-start(bf16[48,3456]{1,0:T(8,128)(2,1)} %copy-done.29), channel_id=1, source_target_pairs={{0,8},{1,9},{2,10},{3,11},{4,12},{5,13},{6,14},{7,15},{8,0},{9,1},... | collective-permute-start | bytes 995336 | tf_op jit(solution)/shard_map/ppermute | solution.py:794
  285.5 22.2 %collective-permute-start.34 = (bf16[48,3456]{1,0:T(8,128)(2,1)}, bf16[48,3456]{1,0:T(8,128)(2,1)S(1)}, u32[]{:S(2)}, u32[]{:S(2)}) collective-permute-start(bf16[48,3456]{1,0:T(8,128)(2,1)} %copy-done.28), channel_id=1, source_target_pairs={{0,12},{1,13},{2,14},{3,15},{4,0},{5,1},{6,2},{7,3},{8,4},{9,5},{1... | collective-permute-start | bytes 995336 | tf_op jit(solution)/shard_map/ppermute | solution.py:794
  288.2 23.7 %collective-permute-start.36 = (bf16[4,48,896]{2,1,0:T(8,128)(2,1)}, bf16[4,48,896]{2,1,0:T(8,128)(2,1)S(1)}, u32[]{:S(2)}, u32[]{:S(2)}) collective-permute-start(bf16[4,48,896]{2,1,0:T(8,128)(2,1)} %get-tuple-element.177), channel_id=1, source_target_pairs={{0,1},{1,0},{2,3},{3,2},{4,5},{5,4},{6,7},{7,6},{8,9},{9,8},{10,11... | collective-permute-start | bytes 1032200 | tf_op jit(solution)/shard_map/ppermute | solution.py:803
  288.9 22.9 %collective-permute-start.37 = (bf16[4,48,896]{2,1,0:T(8,128)(2,1)}, bf16[4,48,896]{2,1,0:T(8,128)(2,1)S(1)}, u32[]{:S(2)}, u32[]{:S(2)}) collective-permute-start(bf16[4,48,896]{2,1,0:T(8,128)(2,1)} %get-tuple-element.178), channel_id=1, source_target_pairs={{0,2},{1,3},{2,0},{3,1},{4,6},{5,7},{6,4},{7,5},{8,10},{9,11},{10,... | collective-permute-start | bytes 1032200 | tf_op jit(solution)/shard_map/ppermute | solution.py:803
  (99 other events, 1241.5 us)
where the time goes:
time: 365 us; the launch traced here: 359 us
  Pallas kernels  188 us (52%)
  waiting for transfers between devices  81.7 us (22%)
  starting transfers between devices  57.9 us (16%)
  local copies, waits for them, and re-layouts  16.2 us (4%)
  other arithmetic  13.5 us (4%)
    ppermute x15, waiting for transfers between devices, along_z(): lax.ppermute(values, 'fsdp', [(chip, chip % 4 + 4 * ((chip // 4 + ahead)...  50 us
    pallas_call x3, Pallas kernels, attention_backward(): pl.pallas_call(functools.partial(attention_backward_kernel, block), grid=...  47.2 us
    pallas_call x1, Pallas kernels, middle_part(): pl.pallas_call(functools.partial(middle_kernel, rows), grid=(SLOTS // row...  38.5 us
    ppermute x15, starting transfers between devices, along_z(): lax.ppermute(values, 'fsdp', [(chip, chip % 4 + 4 * ((chip // 4 + ahead)...  29.8 us
    pallas_call x3, Pallas kernels, attention_forward(): pl.pallas_call(functools.partial(attention_forward_kernel, block), grid=(...  23.6 us
    pallas_call x1, Pallas kernels, later_grads(): pl.pallas_call(later_grads_kernel, grid=(2 * chunks + 1,), in_specs=[SMAL...  19.5 us
    ppermute x16, starting transfers between devices, along_plane(): return lax.ppermute(values, ('rep', 'fsdp'), moves)  18.7 us
    ppermute x16, waiting for transfers between devices, along_plane(): return lax.ppermute(values, ('rep', 'fsdp'), moves)  15.4 us
  transfers between devices with their start and end apart: 54, of which 19 were waited for; matrix products, arithmetic and copies ran while one was open for 4% of the time, Pallas kernels for 28%

commit v1 on v0

--- a/solution.py
+++ b/solution.py
@@ -103,7 +103,7 @@
         scratch_shapes=[pltpu.VMEM((slots, PAIR), BF)] * 4,
         input_output_aliases={5: 0, 6: 1} if extra else {},
         cost_estimate=pl.CostEstimate(flops=elements * 3000, bytes_accessed=10 * slots * count * PAIR, transcendentals=elements),
-        compiler_params=pltpu.CompilerParams(vmem_limit_bytes=48 * 2**20),
+        compiler_params=pltpu.CompilerParams(vmem_limit_bytes=62 * 2**20),
     )(qkv, qkv, qkv, fq, fk, *extra)
 
 
@@ -183,7 +183,7 @@
         + [pltpu.VMEM((slots, PAIR), F32)] * 4,
         input_output_aliases={9: 0} if extra else {},
         cost_estimate=pl.CostEstimate(flops=elements * 2000, bytes_accessed=20 * slots * count * PAIR, transcendentals=elements),
-        compiler_params=pltpu.CompilerParams(vmem_limit_bytes=48 * 2**20),
+        compiler_params=pltpu.CompilerParams(vmem_limit_bytes=62 * 2**20),
     )(qkv, qkv, qkv, fo, fk, do, o, cos, sin, *extra)
 
 
@@ -213,7 +213,7 @@
 
 
 def whole(shape):
-    return pl.BlockSpec(shape, lambda *_: (0,) * len(shape))
+    return pl.BlockSpec(shape, lambda *_: (0,) * len(shape), pipeline_mode=pl.Buffered(1))
 
 
 def line(flat_ref, start, count):
@@ -221,8 +221,9 @@
 
 
 def unit_of(units, half, place):
-    if len(units) == 8:
-        return units[half * 4 + place // 4].at[place % 4]
+    if len(units) == 10:
+        kind, back = place // 4, place % 4
+        return units[half * 5 + (kind if kind < 3 else 3 + back // 2)].at[back if kind < 3 else back % 2]
     return units[half * 8 + place // 4 * 2 + min(place % 4, 1)].at[max(place % 4 - 1, 0)]
 
 
@@ -261,8 +262,8 @@
 
 
 def first_kernel(rows, order_ref, core_ref, tiles_ref, *refs):
-    units = refs[:8]
-    x_ref, cond_ref, cos_ref, sin_ref, qkv_ref, first_ref, w_ref, mod_ref, flat_ref, modt, vecs, sems = refs[8:]
+    units = refs[:10]
+    x_ref, cond_ref, cos_ref, sin_ref, qkv_ref, first_ref, w_ref, mod_ref, flat_ref, modt, vecs, sems = refs[10:]
     step = pl.program_id(0)
 
     @pl.when(step == 0)
@@ -325,7 +326,7 @@
     return pl.pallas_call(
         functools.partial(first_kernel, rows),
         grid=(SLOTS // rows,),
-        in_specs=[SMALL_VMEM] * 3 + [pl.BlockSpec(memory_space=HBM)] * 8
+        in_specs=[SMALL_VMEM] * 3 + [pl.BlockSpec(memory_space=HBM)] * 10
         + [row(D), whole((NSEG, COND)), row(PAIR), row(PAIR)],
         out_specs=[row(3 * D), row(D), whole((D, 3 * D)), whole((NSEG, 6 * D)), whole((FLAT_ROWS, 128))],
         out_shape=[shape((SLOTS, 3 * D), BF), shape((SLOTS, D), BF), shape((D, 3 * D), BF),
@@ -338,12 +339,39 @@
 
 def middle_kernel(rows, order_ref, core_ref, tiles_ref, *refs):
     units = refs[:16]
-    (att_ref, x_ref, cot_ref, mask_ref, mod_ref, flat_ref,
-     out_ref, left_ref, right_ref, gmid_ref, gatt_ref, sums_ref, bias_ref,
-     wo, wu, wd, slope, branch_s, middle_s, sems) = refs[16:]
+    (att_all, x_ref, cot_ref, mask_ref, mod_ref, flat_ref,
+     out_ref, gmid_ref, gatt_ref, sums_ref, bias_ref, mine_ref, give_ref,
+     wo, wu, wd, hidden_s, second_s, grad_mlp_s, grad_up_s, grad_branch_s, branch_s, buffer, sems, out_sems) = refs[16:]
     step = pl.program_id(0)
     core = core_ref[0]
+
+    @pl.when(step < SLOTS // rows)
+    def _():
+        middle_rows(
+            rows, step, core, order_ref, tiles_ref, units, att_all, x_ref, cot_ref, mask_ref, mod_ref, flat_ref,
+            out_ref, gmid_ref, gatt_ref, sums_ref, bias_ref,
+            wo, wu, wd, hidden_s, second_s, grad_mlp_s, grad_up_s, grad_branch_s, branch_s, sems,
+        )
+
+    @pl.when(step >= SLOTS // rows)
+    def _():
+        later_grads(
+            step - SLOTS // rows, core, hidden_s, second_s, att_all, grad_mlp_s, grad_up_s, grad_branch_s,
+            mine_ref, give_ref, buffer, out_sems,
+        )
+
+
+def middle_rows(
+    rows, step, core, order_ref, tiles_ref, units, att_all, x_ref, cot_ref, mask_ref, mod_ref, flat_ref,
+    out_ref, gmid_ref, gatt_ref, sums_ref, bias_ref,
+    wo, wu, wd, hidden_s, second_s, grad_mlp_s, grad_up_s, grad_branch_s, branch_s, sems,
+):
     chunks = FF // D
+    here = pl.ds(pl.multiple_of(step * rows, rows), rows)
+
+    def part_of(part):
+        return pl.ds(pl.multiple_of(step * rows + part * TILE, TILE), TILE)
+
     tiles = rows // TILE
     each = 2 * UNITS
     copies = [
@@ -371,16 +399,14 @@
         row = mask_ref[pl.ds(step * tiles + part, 1), :]
         return jnp.broadcast_to(row, (TILE, TILE)).T[:, :1]
 
-    att = att_ref[...]
-    left_ref[:, FF + D :] = att
-    branch_s[...] = mm(att, wo[...])
+    branch_s[...] = mm(att_all[here, :], wo[...])
     gain = line(flat_ref, D // 128, D // 128)
     for part in range(tiles):
         at = pl.ds(part * TILE, TILE)
         middle = x_ref[at, :].astype(F32) + table(part, 2) * branch_s[at, :]
-        middle_s[at, :] = middle
+        gmid_ref[at, :] = middle
         normal, _ = layer_norm(middle)
-        left_ref[at, FF : FF + D] = (normal * (gain * (1.0 + table(part, 4))) + table(part, 3)).astype(BF)
+        second_s[part_of(part), :] = (normal * (gain * (1.0 + table(part, 4))) + table(part, 3)).astype(BF)
 
     @pl.when(step == 0)
     def _():
@@ -388,44 +414,42 @@
             for copy in group:
                 copy.wait()
 
-    second = left_ref[:, FF : FF + D]
+    for part in range(tiles):
+        at = pl.ds(part * TILE, TILE)
+        grad_mlp = (cot_ref[at, :].astype(F32) * mask_column(part) * table(part, 5)).astype(BF)
+        grad_mlp_s[part_of(part), :] = grad_mlp
+        bias_ref[0:1, FF:] += jnp.sum(grad_mlp.astype(F32), axis=0, keepdims=True)
+    second = second_s[here, :]
+    grad_mlp = grad_mlp_s[here, :]
     factor = math.sqrt(2.0 / math.pi)
-    feed = None
+    feed, grad_second = None, None
     for j in range(chunks):
         at = pl.ds(j * D, D)
         u = mm(second, wu[:, at]) + line(flat_ref, 2 * D // 128 + j * (D // 128), D // 128)
+        grad_hidden = mm(grad_mlp, wd[at, :], NT)
         square = u * u
         bent = jnp.tanh(u * (factor + (factor * 0.044715) * square))
         half = 0.5 * u
         bow = half * bent
         hidden = (half + bow).astype(BF)
-        left_ref[:, at] = hidden
-        slope[:, at] = (0.5 + 0.5 * bent) + (half - bow * bent) * (factor + (3 * factor * 0.044715) * square)
-        share = mm(hidden, wd[at, :])
+        slope = (0.5 + 0.5 * bent) + (half - bow * bent) * (factor + (3 * factor * 0.044715) * square)
+        grad_up = (grad_hidden * slope).astype(BF)
+        hidden_s[here, at] = hidden
+        grad_up_s[here, at] = grad_up
+        bias_ref[0:1, at] += jnp.sum(grad_up.astype(F32), axis=0, keepdims=True)
+        share, grad_share = mm(hidden, wd[at, :]), mm(grad_up, wu[:, at], NT)
         feed = share if feed is None else feed + share
+        grad_second = grad_share if grad_second is None else grad_second + grad_share
     bias_down = line(flat_ref, (2 * D + FF) // 128, D // 128)
     for part in range(tiles):
         at = pl.ds(part * TILE, TILE)
-        gate = table(part, 5)
         feed_out = feed[part * TILE : (part + 1) * TILE] + bias_down
-        out_ref[at, :] = (middle_s[at, :] + gate * feed_out).astype(BF)
+        out_ref[at, :] = (gmid_ref[at, :] + table(part, 5) * feed_out).astype(BF)
         grad_out = cot_ref[at, :].astype(F32) * mask_column(part)
         sums_ref[part, 3:4, :] = jnp.sum(grad_out * feed_out, axis=0, keepdims=True)
-        grad_mlp = (grad_out * gate).astype(BF)
-        right_ref[at, 0:D] = grad_mlp
-        bias_ref[0:1, FF:] += jnp.sum(grad_mlp.astype(F32), axis=0, keepdims=True)
-    grad_mlp = right_ref[:, 0:D]
-    grad_second = None
-    for j in range(chunks):
-        at = pl.ds(j * D, D)
-        grad_up = (mm(grad_mlp, wd[at, :], NT) * slope[:, at]).astype(BF)
-        right_ref[:, D + j * D : 2 * D + j * D] = grad_up
-        bias_ref[0:1, at] += jnp.sum(grad_up.astype(F32), axis=0, keepdims=True)
-        share = mm(grad_up, wu[:, at], NT)
-        grad_second = share if grad_second is None else grad_second + share
     for part in range(tiles):
         at = pl.ds(part * TILE, TILE)
-        normal, root = layer_norm(middle_s[at, :])
+        normal, root = layer_norm(gmid_ref[at, :])
         grad = grad_second[part * TILE : (part + 1) * TILE]
         sums_ref[part, 1:2, :] = jnp.sum(grad, axis=0, keepdims=True)
         sums_ref[part, 2:3, :] = jnp.sum(grad * normal, axis=0, keepdims=True)
@@ -434,105 +458,83 @@
         )
         gmid_ref[at, :] = grad_middle
         sums_ref[part, 0:1, :] = jnp.sum(grad_middle * branch_s[at, :], axis=0, keepdims=True)
-        right_ref[at, FF + D :] = (grad_middle * table(part, 2)).astype(BF)
-    gatt_ref[...] = mm(right_ref[:, FF + D :], wo[...], NT).astype(BF)
-
-
-def middle_part(units, order, core, tiles, att, x, cot, mask, modulation, flat, rows=256):
-    row = lambda width: pl.BlockSpec((rows, width), lambda i: (i, 0))
-    shape = lambda s, t: jax.ShapeDtypeStruct(s, t)
-    return pl.pallas_call(
-        functools.partial(middle_kernel, rows),
-        grid=(SLOTS // rows,),
-        in_specs=[SMALL_VMEM] * 3 + [pl.BlockSpec(memory_space=HBM)] * 16
-        + [row(D), row(D), row(D), whole((BLOCKS, TILE)), whole((NSEG, 6 * D)), whole((FLAT_ROWS, 128))],
-        out_specs=[row(D), row(FF + 2 * D), row(FF + 2 * D), row(D), row(D),
-                   pl.BlockSpec((rows // TILE, 8, D), lambda i: (i, 0, 0)), whole((8, FF + D))],
-        out_shape=[shape((SLOTS, D), BF), shape((SLOTS, FF + 2 * D), BF), shape((SLOTS, FF + 2 * D), BF),
-                   shape((SLOTS, D), F32), shape((SLOTS, D), BF), shape((BLOCKS, 8, D), F32), shape((8, FF + D), F32)],
-        scratch_shapes=[pltpu.VMEM((D, D), BF), pltpu.VMEM((D, FF), BF), pltpu.VMEM((FF, D), BF),
-                        pltpu.VMEM((rows, FF), F32), pltpu.VMEM((rows, D), F32), pltpu.VMEM((rows, D), F32),
-                        pltpu.SemaphoreType.DMA((8 * UNITS,))],
-        cost_estimate=pl.CostEstimate(flops=4 * SLOTS * D * (D + 2 * FF), bytes_accessed=50 * 2**20, transcendentals=SLOTS * FF),
-        compiler_params=pltpu.CompilerParams(vmem_limit_bytes=60 * 2**20),
-    )(order, core, tiles, *units, att, x, cot, mask, modulation, flat)
-
-
-def later_grads_kernel(core_ref, left_ref, right_ref, mine_ref, give_ref, buffer, sems):
-    step = pl.program_id(0)
-    steps = 2 * (FF // D) + 1
+        grad_branch_s[part_of(part), :] = (grad_middle * table(part, 2)).astype(BF)
+    gatt_ref[...] = mm(grad_branch_s[here, :], wo[...], NT).astype(BF)
+
+
+def later_grads(step, core, hidden_s, second_s, att_all, grad_mlp_s, grad_up_s, grad_branch_s, mine_ref, give_ref, buffer, sems):
+    down_steps = FF // D
+    steps = 2 * down_steps + 1
     slot = step % 2
-    down_steps = FF // D
-    core = core_ref[0]
 
     def wait(at_slot):
         for number in range(16):
             pltpu.make_async_copy(buffer.at[at_slot, number], buffer.at[at_slot, number], sems.at[at_slot, number]).wait()
 
+    def send(source, side, place, number):
+        for ref, wanted in ((mine_ref, 0), (give_ref, 1)):
+            @pl.when((core ^ side) == wanted)
+            def _():
+                pltpu.make_async_copy(source, ref.at[place], sems.at[slot, number]).start()
+
+    def keep(left, right):
+        buffer[slot] = mm(left, right, TN).astype(BF).reshape(16, 48, D)
+
     @pl.when(step >= 2)
     def _():
         wait(slot)
 
-    product = mm(left_ref[...], right_ref[...], TN).astype(BF)
-    buffer[slot] = product.reshape(16, 48, D)
-
     @pl.when(step < down_steps)
     def _():
+        keep(hidden_s[:, pl.ds(pl.multiple_of(step * D, D), D)], grad_mlp_s[...])
         for number in range(16):
             local, side, block = number // 4, (number // 2) % 2, number % 2
-            for ref, wanted in ((mine_ref, 0), (give_ref, 1)):
-                @pl.when((core ^ side) == wanted)
-                def _(ref=ref):
-                    pltpu.make_async_copy(
-                        buffer.at[slot, number],
-                        ref.at[4 * step + local, :, pl.ds(DOWN_AT + block * D, D)],
-                        sems.at[slot, number],
-                    ).start()
+            send(buffer.at[slot, number], side, (4 * step + local, pl.ds(0, 48), pl.ds(DOWN_AT + block * D, D)), number)
+
+    @pl.when((step >= down_steps) & (step < steps - 1))
+    def _():
+        keep(second_s[...], grad_up_s[:, pl.ds(pl.multiple_of((step - down_steps) * D, D), D)])
 
     for j in range(down_steps):
         @pl.when(step == down_steps + j)
         def _():
             for number in range(16):
-                for ref, wanted in ((mine_ref, 0), (give_ref, 1)):
-                    @pl.when((core ^ (j // 2)) == wanted)
-                    def _(ref=ref):
-                        pltpu.make_async_copy(
-                            buffer.at[slot, number],
-                            ref.at[number, :, pl.ds(UP_AT + (j % 2) * D, D)],
-                            sems.at[slot, number],
-                        ).start()
+                send(buffer.at[slot, number], j // 2, (number, pl.ds(0, 48), pl.ds(UP_AT + (j % 2) * D, D)), number)
 
     @pl.when(step == steps - 1)
     def _():
+        keep(att_all[...], grad_branch_s[...])
         for number in range(16):
             for side in range(2):
-                for ref, wanted in ((mine_ref, 0), (give_ref, 1)):
-                    @pl.when((core ^ side) == wanted)
-                    def _(ref=ref):
-                        pltpu.make_async_copy(
-                            buffer.at[slot, number, :, pl.ds(side * (D // 2), D // 2)],
-                            ref.at[number, :, pl.ds(OUT_AT, D // 2)],
-                            sems.at[slot, number],
-                        ).start()
+                source = buffer.at[slot, number, pl.ds(0, 48), pl.ds(side * (D // 2), D // 2)]
+                send(source, side, (number, pl.ds(0, 48), pl.ds(OUT_AT, D // 2)), number)
         wait(1 - slot)
         wait(slot)
 
 
-def later_grads(core, left, right):
-    chunks = FF // D
-    left_at = lambda i: (0, jnp.minimum(i, chunks) + jnp.maximum(i - 2 * chunks + 1, 0))
-    right_at = lambda i: (0, jnp.maximum(i - chunks + 1, 0))
-    shape = jax.ShapeDtypeStruct((UNITS, 48, SECOND_WIDE), BF)
+def middle_part(units, order, core, tiles, att, x, cot, mask, modulation, flat, rows=512):
+    last = SLOTS // rows - 1
+    row = lambda width: pl.BlockSpec((rows, width), lambda i: (jnp.minimum(i, last), 0))
+    shape = lambda s, t: jax.ShapeDtypeStruct(s, t)
+    units_shape = shape((UNITS, 48, SECOND_WIDE), BF)
+    kept = lambda width: pltpu.VMEM((SLOTS, width), BF)
     return pl.pallas_call(
-        later_grads_kernel,
-        grid=(2 * chunks + 1,),
-        in_specs=[SMALL_VMEM, pl.BlockSpec((SLOTS, D), left_at), pl.BlockSpec((SLOTS, D), right_at)],
-        out_specs=[pl.BlockSpec(memory_space=HBM)] * 2,
-        out_shape=[shape, shape],
-        scratch_shapes=[pltpu.VMEM((2, 16, 48, D), BF), pltpu.SemaphoreType.DMA((2, 16))],
-        cost_estimate=pl.CostEstimate(flops=2 * SLOTS * D * (2 * FF + D), bytes_accessed=40 * 2**20, transcendentals=0),
-        compiler_params=pltpu.CompilerParams(vmem_limit_bytes=48 * 2**20),
-    )(core, left, right)
+        functools.partial(middle_kernel, rows),
+        grid=(SLOTS // rows + 2 * (FF // D) + 1,),
+        in_specs=[SMALL_VMEM] * 3 + [pl.BlockSpec(memory_space=HBM)] * 16
+        + [whole((SLOTS, D)), row(D), row(D), whole((BLOCKS, TILE)), whole((NSEG, 6 * D)), whole((FLAT_ROWS, 128))],
+        out_specs=[row(D), row(D), row(D),
+                   pl.BlockSpec((rows // TILE, 8, D), lambda i: (jnp.minimum(i, last), 0, 0)), whole((8, FF + D))]
+        + [pl.BlockSpec(memory_space=HBM)] * 2,
+        out_shape=[shape((SLOTS, D), BF), shape((SLOTS, D), F32), shape((SLOTS, D), BF), shape((BLOCKS, 8, D), F32),
+                   shape((8, FF + D), F32), units_shape, units_shape],
+        scratch_shapes=[pltpu.VMEM((D, D), BF), pltpu.VMEM((D, FF), BF), pltpu.VMEM((FF, D), BF),
+                        kept(FF), kept(D), kept(D), kept(FF), kept(D),
+                        pltpu.VMEM((rows, D), F32), pltpu.VMEM((2, 16, 48, D), BF),
+                        pltpu.SemaphoreType.DMA((8 * UNITS,)), pltpu.SemaphoreType.DMA((2, 16))],
+        cost_estimate=pl.CostEstimate(flops=6 * SLOTS * D * (D + 2 * FF), bytes_accessed=50 * 2**20, transcendentals=SLOTS * FF),
+        compiler_params=pltpu.CompilerParams(vmem_limit_bytes=63 * 2**20),
+    )(order, core, tiles, *units, att, x, cot, mask, modulation, flat)
 
 
 def qkv_grads_kernel(core_ref, first_ref, g_ref, mine_ref, give_ref, units, sems):
@@ -803,10 +805,6 @@
     return lax.ppermute(values, ("rep", "fsdp"), moves)
 
 
-def across_plane(values):
-    return lax.ppermute(values, "fsdp", [(chip, chip ^ 3) for chip in range(UNITS)])
-
-
 def swap_core(values):
     return lax.ppermute(values, "rep", [(0, 1), (1, 0)])
 
@@ -880,12 +878,6 @@
         self.mine, self.places = mine, places
         self.given = swap_core(give)
 
-    def send_plane(self, sooner=None):
-        given = self.given if sooner is None else hold_back(self.given, sooner)
-        sums = column_sums(self.places, self.mine, given, [(3, []), (1, []), (2, [])])
-        self.arrived = [across_plane(sums[0]), along_plane(sums[1], 0), along_plane(sums[2], 1)]
-        return sums[0]
-
     def send_far(self, sooner=None):
         given = self.given if sooner is None else hold_back(self.given, sooner)
         far, second = column_sums(self.places, self.mine, given, [(3, []), (2, [])])
@@ -916,34 +908,49 @@
         return (own, swap_core(own))
 
 
-def arrivals_kernel(*refs):
-    inputs, outs = refs[1 : len(refs) - 4], refs[len(refs) - 4 :]
-    each = len(inputs) // 4
+def arrivals_kernel(outputs, *refs):
+    inputs, outs = refs[1 : len(refs) - outputs], refs[len(refs) - outputs :]
+    each = len(inputs) // outputs
     for number, out_ref in enumerate(outs):
-        total = inputs[number * each][0].astype(F32)
+        total = inputs[number * each][...].astype(F32)
         for part in inputs[number * each + 1 : (number + 1) * each]:
-            total = total + part[0].astype(F32)
-        out_ref[...] = total.astype(BF)
+            total = total + part[...].astype(F32)
+        out_ref[...] = total.reshape(out_ref.shape).astype(BF)
+
+
+def arrival_sums(places, parts, apart):
+    block = parts[0].shape[1:]
+    if apart:
+        specs = [
+            pl.BlockSpec((1,) + block, lambda i, s, ahead=ahead: (s[4 + ahead], 0, 0)) for ahead in range(4) for _ in parts
+        ]
+        out_spec, out_shape, outputs = pl.BlockSpec(block, lambda i, s: (0, 0)), block, 4
+    else:
+        out_spec = pl.BlockSpec((4,) + block, lambda i, s: (0, 0, 0))
+        specs, out_shape, outputs = [out_spec] * len(parts), (4,) + block, 1
+    return pl.pallas_call(
+        functools.partial(arrivals_kernel, outputs),
+        grid_spec=pltpu.PrefetchScalarGridSpec(
+            num_scalar_prefetch=1, grid=(1,), in_specs=specs, out_specs=[out_spec] * outputs
+        ),
+        out_shape=[jax.ShapeDtypeStruct(out_shape, BF)] * outputs,
+    )(places, *(list(parts) * outputs))
 
 
 class SmallScatter:
     def __init__(self, own, first, second, far, places):
-        self.places = places
-        self.parts = [own, across_plane(far), along_plane(first, 0), along_plane(second, 1)]
-
-    def send_column(self, sooner=None):
-        parts = self.parts if sooner is None else hold_back(self.parts, sooner)
-        block = parts[0].shape[1:]
-        picks = [
-            pl.BlockSpec((1,) + block, lambda i, s, ahead=ahead: (s[4 + ahead], 0, 0)) for ahead in range(4) for _ in parts
-        ]
-        self.own, *units = pl.pallas_call(
-            arrivals_kernel,
-            grid_spec=pltpu.PrefetchScalarGridSpec(
-                num_scalar_prefetch=1, grid=(1,), in_specs=picks, out_specs=[pl.BlockSpec(block, lambda i, s: (0, 0))] * 4
-            ),
-            out_shape=[jax.ShapeDtypeStruct(block, BF)] * 4,
-        )(self.places, *(parts * 4))
+        self.places, self.own, self.first = places, own, first
+        self.far_came, self.second_came = along_plane(far, 1), along_plane(second, 1)
+
+    def send_first(self, sooner):
+        far_came, self.second_came = hold_back((self.far_came, self.second_came), sooner)
+        (first,) = arrival_sums(self.places, [self.first, far_came], False)
+        self.first_came = along_plane(first, 0)
+        return first
+
+    def send_column(self, sooner):
+        came = hold_back(self.first_came, sooner)
+        self.own, *units = arrival_sums(self.places, [self.own, came, self.second_came], True)
         self.came = [along_z(unit, ahead + 1) for ahead, unit in enumerate(units)]
         return self.own
 
@@ -1020,10 +1027,9 @@
     return [lax.all_gather(part, "fsdp", axis=axis, tiled=True) for part, axis in zip(parts, axes)]
 
 
-def virtual_units(pack, cuts):
-    return [
-        packed[4 * part + start : 4 * part + stop] for packed in (pack(0), pack(1)) for part in range(4) for start, stop in cuts
-    ]
+def virtual_units(pack, pieces=False):
+    cuts = [0, 1, 4, 5, 8, 9, 12, 13, 16] if pieces else [0, 4, 8, 12, 14, 16]
+    return [packed[start:stop] for packed in (pack(0), pack(1)) for start, stop in zip(cuts, cuts[1:])]
 
 
 def reduce_plain(grads, axes):
@@ -1094,9 +1100,9 @@
         first_near = near_of(first_column)
         second_from = hold_back(unit_second, first_column)
         second_back = [along_z(second_from, back) for back in range(1, 4)]
-        second_far = far_from(second_near)
-        first_near[0] = hold_back(first_near[0], (second_far, second_near, second_back))
-        units_first = [first_column] + first_near + [far_from(first_near)]
+        first_near, second_near = lax.optimization_barrier((first_near, second_near))
+        first_far = [along_plane(first_near[0][start : start + 2], 1) for start in (0, 2)]
+        units_first, second_back = lax.optimization_barrier(([first_column] + first_near + first_far, second_back))
         units_first = units_first + swapped(units_first)
     else:
         order = jnp.concatenate([jnp.arange(UNITS, dtype=jnp.int32)] * 2)
@@ -1104,8 +1110,8 @@
         side = jnp.zeros((1,), jnp.int32)
         qkv_all, mod_all, vector_all = gather_plain((qkv_low, mod_low, vector_low), (0, 1, 0))
         out_all, up_all, down_all = gather_plain((out_low, up_low, down_low), (0, 0, 0))
-        units_first = virtual_units(lambda s: pack_first(qkv_all, mod_all.T, vector_all.reshape(UNITS, -1), s), ((0, 4),))
-        units_second = virtual_units(lambda s: pack_second(out_all, up_all, down_all, s), ((0, 1), (1, 4)))
+        units_first = virtual_units(lambda s: pack_first(qkv_all, mod_all.T, vector_all.reshape(UNITS, -1), s))
+        units_second = virtual_units(lambda s: pack_second(out_all, up_all, down_all, s), True)
 
     segment, member, position, valid_slot = layout_tables(seg_sizes[0], seq_lengths[0])
     tiles = segment.reshape(BLOCKS, TILE)[:, 0]
@@ -1126,8 +1132,8 @@
         if rounds and number == 1:
             second_rest_far = far_from(hold_back(second_rest_near, forward))
             second_own = [second_one, second_rest, second_near[0], second_rest_near[0], second_near[1], second_rest_near[1]]
-            second_own.append(second_far)
-            second_other = swapped(hold_back(second_own, forward))
+            second_own.append(far_from(second_near))
+            second_other = swapped(hold_back(second_own[:-1], forward)) + swapped(second_own[-1:])
         if rounds and number == 2:
             forward, second_rest_far = hold_back((forward, second_rest_far), second_other)
         forward = attention_forward(mixed, feature_query, feature_key, forward, first_pair, count)
@@ -1135,11 +1141,9 @@
     if rounds:
         units_second = second_own + [second_rest_far] + second_other + [swap_core(second_rest_far)]
     attended_low, feature = forward
-    out_hidden, left, right, grad_middle, grad_attended, sums, bias_sums = middle_part(
+    out_hidden, grad_middle, grad_attended, sums, bias_sums, mine_later, give_later = middle_part(
         units_second, order, side, tiles, attended_low, row_in, row_cot, weight_mask, modulation, flat
     )
-    mine_later, give_later = later_grads(side, left, right)
-
     state = [None]
 
     def backward_part(number, came):
@@ -1172,19 +1176,21 @@
         backward_part(1, sent)
         sent = later.send_first(state[0])
         backward_part(2, sent)
-        sent = later.send_column(state[0])
-        qkv_parts = qkv_end(sent)
+        qkv_parts = qkv_end(later.arrived)
         sooner = Scatter(*qkv_parts, places)
-        sent = sooner.send_plane()
+        sent = later.send_column(qkv_parts)
+        sent = sooner.send_far(sent)
         grad_in, *small_parts = row_end(sent)
         small = SmallScatter(*small_parts, places)
-        sent = sooner.send_column(grad_in)
-        sent = small.send_column((sent, sooner.came, later.came))
+        sent = sooner.send_first((grad_in, later.came[0], later.came[2]))
+        sent = sooner.send_column(sent)
+        sent = small.send_first((sent, later.came[1]))
+        sent = small.send_column((sent, sooner.came))
         later_sums = later.finish(sent)
         (out_new, up_new, down_new), later_table = update_moments(
             update_later_kernel, side, later_sums, of_out + of_up + of_down
         )
-        qkv_sums = sooner.finish(sent)
+        qkv_sums = sooner.finish(later_table)
         small_sums = small.finish()
         (qkv_new, mod_new), sooner_table = update_moments(
             update_sooner_kernel, side, qkv_sums + (small_sums,), of_qkv + tuple(part.T for part in of_mod)

time: 365 us -> 355 us (0.973)
  waiting for transfers between devices: 81.7 us -> 70.9 us
  Pallas kernels: 188 us -> 195 us
    pallas_call x2, Pallas kernels: 22.5 us -> 5.42 us  [arrival_sums(): pl.pallas_call(functools.partial(arrivals_kernel, outputs), grid_spec=plt...]
    pallas_call x1, Pallas kernels: 38.5 us -> 54.7 us  [middle_part(): pl.pallas_call(functools.partial(middle_kernel, rows), grid=(SLOTS // row...]
    ppermute x15, waiting for transfers between devices: 50 us -> 34.8 us  [along_z(): lax.ppermute(values, 'fsdp', [(chip, chip % 4 + 4 * ((chip // 4 + ahead)...]
    ppermute x16 -> x19, waiting for transfers between devices: 15.4 us -> 23.2 us  [along_plane(): return lax.ppermute(values, ('rep', 'fsdp'), moves)]
    pallas_call x5 -> x6, Pallas kernels: 14.9 us -> 19 us  [column_sums(): pl.pallas_call(functools.partial(column_sums_kernel, counts), grid_spec=p...]
    ppermute x15, starting transfers between devices: 29.8 us -> 26 us  [along_z(): lax.ppermute(values, 'fsdp', [(chip, chip % 4 + 4 * ((chip // 4 + ahead)...]
    unnamed x139 -> x111, local copies, waits for them, and re-layouts: 11 us -> 8.52 us
    ppermute x16 -> x19, starting transfers between devices: 18.7 us -> 20.6 us  [along_plane(): return lax.ppermute(values, ('rep', 'fsdp'), moves)]
  transfers between devices with their start and end apart: 54 -> 56, of which waited for: 19 -> 21; matrix products, arithmetic and copies ran while one was open for 4% -> 5% of each run, Pallas kernels for 28% -> 31%
where the time goes in v1:
time: 355 us; the launch traced here: 351 us
  Pallas kernels  195 us (55%)
  waiting for transfers between devices  70.9 us (20%)
  starting transfers between devices  55 us (15%)
  other arithmetic  14.9 us (4%)
  local copies, waits for them, and re-layouts  13.8 us (4%)
    pallas_call x1, Pallas kernels, middle_part(): pl.pallas_call(functools.partial(middle_kernel, rows), grid=(SLOTS // row...  54.7 us
    pallas_call x3, Pallas kernels, attention_backward(): pl.pallas_call(functools.partial(attention_backward_kernel, block), grid=...  49.5 us
    ppermute x15, waiting for transfers between devices, along_z(): lax.ppermute(values, 'fsdp', [(chip, chip % 4 + 4 * ((chip // 4 + ahead)...  34.8 us
    ppermute x15, starting transfers between devices, along_z(): lax.ppermute(values, 'fsdp', [(chip, chip % 4 + 4 * ((chip // 4 + ahead)...  26 us
    pallas_call x3, Pallas kernels, attention_forward(): pl.pallas_call(functools.partial(attention_forward_kernel, block), grid=(...  25.5 us
    ppermute x19, waiting for transfers between devices, along_plane(): return lax.ppermute(values, ('rep', 'fsdp'), moves)  23.2 us
    ppermute x19, starting transfers between devices, along_plane(): return lax.ppermute(values, ('rep', 'fsdp'), moves)  20.6 us
    pallas_call x6, Pallas kernels, column_sums(): pl.pallas_call(functools.partial(column_sums_kernel, counts), grid_spec=p...  19 us
  transfers between devices with their start and end apart: 56, of which 21 were waited for; matrix products, arithmetic and copies ran while one was open for 5% of the time, Pallas kernels for 31%

profile of v1, /device:TPU:0, one launch (start us, length us, event | category | flops | bytes accessed | tf_op | source)
XLA Modules:
  0.0 350.9 jit_solution(12190722685635403506)
XLA Ops:
  3.4 5.1 %collective-permute-start.2 = (bf16[48,1664]{1,0:T(8,128)(2,1)S(1)}, bf16[48,1664]{1,0:T(8,128)(2,1)S(1)}, u32[]{:S(2)}, u32[]{:S(2)}) collective-permute-start(bf16[48,1664]{1,0:T(8,128)(2,1)S(1)} %maximum_bitcast_fusion), channel_id=1, source_target_pairs={{0,12},{1,13},{2,14},{3,15},{4,0},{5,1},{6,2},{7,3},{8,4},{9,5},{1... | collective-permute-start | bytes 479240 | tf_op jit(solution)/shard_map/ppermute | solution.py:796
  18.1 4.0 %collective-permute-done.1 = bf16[48,1664]{1,0:T(8,128)(2,1)S(1)} collective-permute-done((bf16[48,1664]{1,0:T(8,128)(2,1)S(1)}, bf16[48,1664]{1,0:T(8,128)(2,1)S(1)}, u32[]{:S(2)}, u32[]{:S(2)}) %collective-permute-start.1) | collective-permute-done | bytes 159776 | tf_op jit(solution)/shard_map/ppermute | solution.py:796
  33.5 5.7 %collective-permute-done.4.refs_2_ = bf16[4,48,1664]{2,1,0:T(8,128)(2,1)S(1)} collective-permute-done((bf16[4,48,1664]{2,1,0:T(8,128)(2,1)S(1)}, bf16[4,48,1664]{2,1,0:T(8,128)(2,1)S(1)}, u32[]{:S(2)}, u32[]{:S(2)}) %collective-permute-start.4) | collective-permute-done | bytes 639008 | tf_op jit(solution)/shard_map/ppermute | solution.py:805
  44.2 14.9 %collective-permute-done.10 = bf16[48,3456]{1,0:T(8,128)(2,1)S(1)} collective-permute-done((bf16[48,3456]{1,0:T(8,128)(2,1)S(1)}, bf16[48,3456]{1,0:T(8,128)(2,1)S(1)}, u32[]{:S(2)}, u32[]{:S(2)}) %collective-permute-start.10) | collective-permute-done | bytes 331808 | tf_op jit(solution)/shard_map/ppermute | solution.py:796
  66.2 13.0 %shard_map.409 = (bf16[1024,2304]{1,0:T(8,128)(2,1)}, bf16[1024,768]{1,0:T(8,128)(2,1)}, bf16[768,2304]{1,0:T(8,128)(2,1)}, f32[8,4608]{1,0:T(8,128)}, f32[80,128]{1,0:T(8,128)}) custom-call(s32[32]{0:T(128)} %pad_add_fusion.order_ref, s32[1]{0:T(128)} %bitcast.2.core_ref.side_ref, s32[8]{0:T(128)} %get-tuple-element.256.tiles_ref, ...), custom_call_target="tpu_custom_call" | custom-call | flops 3623878656 | bytes 20971520 | tf_op jit(solution)/shard_map/pallas_call | solution.py:326
  79.2 8.5 %shard_map.410 = (bf16[1024,768]{1,0:T(8,128)(2,1)}, bf16[1024,768]{1,0:T(8,128)(2,1)}) custom-call(bf16[1024,2304]{1,0:T(8,128)(2,1)} %get-tuple-element.144.q_ref.k_ref.v_ref, bf16[1024,2304]{1,0:T(8,128)(2,1)} %get-tuple-element.144.q_ref.k_ref.v_ref, bf16[1024,2304]{1,0:T(8,128)(2,1)} %get-tuple-element.144.q_ref.k_ref.v_ref, ...), custom_call_target="tpu_custom_call" | custom-call | flops 12582912000 | bytes 2621440 | tf_op jit(solution)/shard_map/pallas_call | solution.py:97
  91.4 11.7 %shard_map.411 = (bf16[1024,768]{1,0:T(8,128)(2,1)}, bf16[1024,768]{1,0:T(8,128)(2,1)}) custom-call(bf16[1024,2304]{1,0:T(8,128)(2,1)} %get-tuple-element.144.q_ref.k_ref.v_ref, bf16[1024,2304]{1,0:T(8,128)(2,1)} %get-tuple-element.144.q_ref.k_ref.v_ref, ...), custom_call_target="tpu_custom_call", output_to_operand_aliasing={{0}: (5, {}), {1}: (6, {})} | custom-call | flops 18874368000 | bytes 3932160 | tf_op jit(solution)/shard_map/pallas_call | solution.py:97
  104.8 5.3 %shard_map.412 = (bf16[1024,768]{1,0:T(8,128)(2,1)}, bf16[1024,768]{1,0:T(8,128)(2,1)}) custom-call(bf16[1024,2304]{1,0:T(8,128)(2,1)} %get-tuple-element.144.q_ref.k_ref.v_ref, bf16[1024,2304]{1,0:T(8,128)(2,1)} %get-tuple-element.144.q_ref.k_ref.v_ref, ...), custom_call_target="tpu_custom_call", output_to_operand_aliasing={{0}: (5, {}), {1}: (6, {})} | custom-call | flops 6291456000 | bytes 1310720 | tf_op jit(solution)/shard_map/pallas_call | solution.py:97
  111.0 54.7 %shard_map.413 = (bf16[1024,768]{1,0:T(8,128)(2,1)}, f32[1024,768]{1,0:T(8,128)}, bf16[1024,768]{1,0:T(8,128)(2,1)}, f32[8,8,768]{2,1,0:T(8,128)}, f32[8,3840]{1...) custom-call(s32[32]{0:T(128)} %pad_add_fusion.order_ref, s32[1]{0:T(128)} %bitcast.2.core_ref.side_ref, ...), custom_call_target="tpu_custom_call" | custom-call | flops 32614907904 | bytes 52428800 | tf_op jit(solution)/shard_map/pallas_call | solution.py:521
  166.9 9.5 %shard_map.414.refs_0_ = bf16[3,1024,768]{2,1,0:T(8,128)(2,1)} custom-call(bf16[1024,2304]{1,0:T(8,128)(2,1)} %get-tuple-element.144.q_ref.k_ref.v_ref, bf16[1024,2304]{1,0:T(8,128)(2,1)} %get-tuple-element.144.q_ref.k_ref.v_ref, bf16[1024,2304]{1,0:T(8,128)(2,1)} %get-tuple-element.144.q_ref.k_ref.v_ref, bf16[1024,768]{1,0:T(8,128)(2,1)} %get-tuple-element.163.fo_ref, ...), custom_call_target="tpu_custom_call" | custom-call | flops 4194304000 | bytes 2621440 | tf_op jit(solution)/shard_map/pallas_call | solution.py:175
  176.4 5.1 %shard_map.415 = (bf16[4,48,3456]{2,1,0:T(8,128)(2,1)}, bf16[4,48,3456]{2,1,0:T(8,128)(2,1)}) custom-call(s32[8]{0:T(128)S(1)} %fusion.9.places_ref.refs_0_, bf16[4,4,48,3456]{3,2,1,0:T(8,128)(2,1)} %bitcast.99, bf16[4,4,48,3456]{3,2,1,0:T(8,128)(2,1)} %bitcast.38.refs_1_.refs_3_, bf16[4,4,48,3456]{3,2,1,0:T(8,128)(2,1)} %bitcast.100, ...), custom_call_target="tpu_custom_call" | custom-call | bytes 12582912 | tf_op jit(solution)/shard_map/pallas_call | solution.py:862
  183.5 23.3 %shard_map.416.refs_0_ = bf16[3,1024,768]{2,1,0:T(8,128)(2,1)} custom-call(bf16[1024,2304]{1,0:T(8,128)(2,1)} %get-tuple-element.144.q_ref.k_ref.v_ref, bf16[1024,2304]{1,0:T(8,128)(2,1)} %get-tuple-element.144.q_ref.k_ref.v_ref, bf16[1024,2304]{1,0:T(8,128)(2,1)} %get-tuple-element.144.q_ref.k_ref.v_ref, ...), custom_call_target="tpu_custom_call", output_to_operand_aliasing={{}: (9, {})} | custom-call | flops 12582912000 | bytes 7864320 | tf_op jit(solution)/shard_map/pallas_call | solution.py:175
  206.8 7.0 %collective-permute-done.30.refs_2_ = bf16[4,48,3456]{2,1,0:T(8,128)(2,1)} collective-permute-done((bf16[4,48,3456]{2,1,0:T(8,128)(2,1)}, bf16[4,48,3456]{2,1,0:T(8,128)(2,1)}, u32[]{:S(2)}, u32[]{:S(2)}) %collective-permute-start.30) | collective-permute-done | bytes 1327136 | tf_op jit(solution)/shard_map/ppermute | solution.py:805
  213.8 4.7 %shard_map.417 = bf16[4,48,3456]{2,1,0:T(8,128)(2,1)} custom-call(s32[8]{0:T(128)S(1)} %fusion.9.places_ref.refs_0_, bf16[4,4,48,3456]{3,2,1,0:T(8,128)(2,1)} %bitcast.101, bf16[4,4,48,3456]{3,2,1,0:T(8,128)(2,1)} %bitcast.37.refs_1_.refs_5_.refs_9_.refs_13_, bf16[4,48,3456]{2,1,0:T(8,128)(2,1)} %collective-permute-done.30.refs_2_), custom_call_target="tpu_custom_call" | custom-call | bytes 12582912 | tf_op jit(solution)/shard_map/pallas_call | solution.py:862
  219.2 16.7 %shard_map.418.g_ref = bf16[3,1024,768]{2,1,0:T(8,128)(2,1)} custom-call(bf16[1024,2304]{1,0:T(8,128)(2,1)} %get-tuple-element.144.q_ref.k_ref.v_ref, bf16[1024,2304]{1,0:T(8,128)(2,1)} %get-tuple-element.144.q_ref.k_ref.v_ref, bf16[1024,2304]{1,0:T(8,128)(2,1)} %get-tuple-element.144.q_ref.k_ref.v_ref, ...), custom_call_target="tpu_custom_call", output_to_operand_aliasing={{}: (9, {})} | custom-call | flops 8388608000 | bytes 5242880 | tf_op jit(solution)/shard_map/pallas_call | solution.py:175
  236.6 7.7 %shard_map.419 = (bf16[16,48,1152]{2,1,0:T(8,128)(2,1)S(1)}, bf16[16,48,1152]{2,1,0:T(8,128)(2,1)}) custom-call(s32[1]{0:T(128)} %bitcast.2.core_ref.side_ref, bf16[1024,768]{1,0:T(8,128)(2,1)S(1)} %copy-done.5, bf16[3,1024,768]{2,1,0:T(8,128)(2,1)} %shard_map.418.g_ref), custom_call_target="tpu_custom_call" | custom-call | flops 603979776 | bytes 1048576 | tf_op jit(solution)/shard_map/pallas_call | solution.py:569
  245.8 3.8 %shard_map.420 = (bf16[48,3456]{1,0:T(8,128)(2,1)S(1)}, bf16[48,3456]{1,0:T(8,128)(2,1)}, bf16[48,3456]{1,0:T(8,128)(2,1)S(1)}, bf16[48,3456]{1,0:T(8,128)(2,1)}) custom-call(s32[8]{0:T(128)S(1)} %fusion.9.places_ref.refs_0_, bf16[4,4,48,3456]{3,2,1,0:T(8,128)(2,1)} %bitcast.102, bf16[4,4,48,3456]{3,2,1,0:T(8,128)(2,1)} %bitcast.37.refs_1_.refs_5_.refs_9_.refs_13_, ...), custom_call_target="tpu_custom_call" | custom-call | bytes 209715200 | tf_op jit(solution)/shard_map/pallas_call | solution.py:862
  255.1 3.8 %collective-permute-start.36 = (bf16[48,3456]{1,0:T(8,128)(2,1)}, bf16[48,3456]{1,0:T(8,128)(2,1)}, u32[]{:S(2)}, u32[]{:S(2)}) collective-permute-start(bf16[48,3456]{1,0:T(8,128)(2,1)} %get-tuple-element.191), channel_id=1, source_target_pairs={{0,12},{1,13},{2,14},{3,15},{4,0},{5,1},{6,2},{7,3},{8,4},{9,5},{1... | collective-permute-start | bytes 995336 | tf_op jit(solution)/shard_map/ppermute | solution.py:796
  258.9 13.4 %shard_map.422 = (f32[1024,768]{1,0:T(8,128)}, bf16[4,48,896]{2,1,0:T(8,128)(2,1)}, bf16[4,48,896]{2,1,0:T(8,128)(2,1)}, bf16[4,48,896]{2,1,0:T(8,128)(2,1)}, bf16[4,48,896]{2,1,0:T(8,128)(2,1)}) custom-call(s32[8]{0:T(128)} %copy-done.22, s32[8]{0:T(128)} %get-tuple-element.256.tiles_ref, f32[8,8]{1,0:T(8,128)} %convert_bitcast_fusion.member_ref, ...), custom_call_target="tpu_custom_call" | custom-call | flops 3623878656 | bytes 31457280 | tf_op jit(solution)/shard_map/pallas_call | solution.py:663
  280.0 8.0 %collective-permute-done.41.refs_2_.refs_6_.refs_10_.refs_14_ = bf16[4,48,1152]{2,1,0:T(8,128)(2,1)S(1)} collective-permute-done((bf16[4,48,1152]{2,1,0:T(8,128)(2,1)S(1)}, bf16[4,48,1152]{2,1,0:T(8,128)(2,1)S(1)}, u32[]{:S(2)}, u32[]{:S(2)}) %collective-permute-start.41) | collective-permute-done | bytes 442400 | tf_op jit(solution)/shard_map/ppermute | solution.py:805
  298.2 3.2 collective-permute-start.44
  302.0 4.2 %collective-permute-done.43 = bf16[48,1152]{1,0:T(8,128)(2,1)S(1)} collective-permute-done((bf16[48,1152]{1,0:T(8,128)(2,1)}, bf16[48,1152]{1,0:T(8,128)(2,1)S(1)}, u32[]{:S(2)}, u32[]{:S(2)}) %collective-permute-start.43) | collective-permute-done | bytes 110624 | tf_op jit(solution)/shard_map/ppermute | solution.py:796
  306.2 3.3 collective-permute-done.44
  326.8 3.3 shard_map.427
  (275 shorter events, 109.5 us)
Async XLA Ops:
  3.4 14.7 %collective-permute-start.2 = (bf16[48,1664]{1,0:T(8,128)(2,1)S(1)}, bf16[48,1664]{1,0:T(8,128)(2,1)S(1)}, u32[]{:S(2)}, u32[]{:S(2)}) collective-permute-start(bf16[48,1664]{1,0:T(8,128)(2,1)S(1)} %maximum_bitcast_fusion), channel_id=1, source_target_pairs={{0,12},{1,13},{2,14},{3,15},{4,0},{5,1},{6,2},{7,3},{8,4},{9,5},{1... | collective-permute-start | bytes 479240 | tf_op jit(solution)/shard_map/ppermute | solution.py:796
  12.9 16.5 %collective-permute-start.6 = (bf16[1,48,3456]{2,1,0:T(8,128)(2,1)S(1)}, bf16[1,48,3456]{2,1,0:T(8,128)(2,1)}, u32[]{:S(2)}, u32[]{:S(2)}) collective-permute-start(bf16[1,48,3456]{2,1,0:T(8,128)(2,1)S(1)} %get-tuple-element.150.refs_0_), channel_id=1, source_target_pairs={{0,2},{1,3},{2,0},{3,1},{4,6},{5,7},{6,4},{7,5},{8,10},{9,11},{10,... | collective-permute-start | bytes 995336 | tf_op jit(solution)/shard_map/ppermute | solution.py:805
  14.4 16.7 %collective-permute-start.5 = (bf16[1,48,3456]{2,1,0:T(8,128)(2,1)S(1)}, bf16[1,48,3456]{2,1,0:T(8,128)(2,1)}, u32[]{:S(2)}, u32[]{:S(2)}) collective-permute-start(bf16[1,48,3456]{2,1,0:T(8,128)(2,1)S(1)} %get-tuple-element.150.refs_0_), channel_id=1, source_target_pairs={{0,1},{1,0},{2,3},{3,2},{4,5},{5,4},{6,7},{7,6},{8,9},{9,8},{10,11... | collective-permute-start | bytes 995336 | tf_op jit(solution)/shard_map/ppermute | solution.py:805
  22.1 17.1 %collective-permute-start.4 = (bf16[4,48,1664]{2,1,0:T(8,128)(2,1)S(1)}, bf16[4,48,1664]{2,1,0:T(8,128)(2,1)S(1)}, u32[]{:S(2)}, u32[]{:S(2)}) collective-permute-start(bf16[4,48,1664]{2,1,0:T(8,128)(2,1)S(1)} %pad_maximum_fusion.1.refs_0_), channel_id=1, source_target_pairs={{0,2},{1,3},{2,0},{3,1},{4,6},{5,7},{6,4},{7,5},{8,10},{9,11},{10,... | collective-permute-start | bytes 1916936 | tf_op jit(solution)/shard_map/ppermute | solution.py:805
  23.7 15.5 %collective-permute-start.3 = (bf16[4,48,1664]{2,1,0:T(8,128)(2,1)S(1)}, bf16[4,48,1664]{2,1,0:T(8,128)(2,1)S(1)}, u32[]{:S(2)}, u32[]{:S(2)}) collective-permute-start(bf16[4,48,1664]{2,1,0:T(8,128)(2,1)S(1)} %pad_maximum_fusion.1.refs_0_), channel_id=1, source_target_pairs={{0,1},{1,0},{2,3},{3,2},{4,5},{5,4},{6,7},{7,6},{8,9},{9,8},{10,11... | collective-permute-start | bytes 1916936 | tf_op jit(solution)/shard_map/ppermute | solution.py:805
  29.4 29.7 %collective-permute-start.10 = (bf16[48,3456]{1,0:T(8,128)(2,1)S(1)}, bf16[48,3456]{1,0:T(8,128)(2,1)S(1)}, u32[]{:S(2)}, u32[]{:S(2)}) collective-permute-start(bf16[48,3456]{1,0:T(8,128)(2,1)S(1)} %get-tuple-element.133), channel_id=1, source_target_pairs={{0,8},{1,9},{2,10},{3,11},{4,12},{5,13},{6,14},{7,15},{8,0},{9,1},... | collective-permute-start | bytes 995336 | tf_op jit(solution)/shard_map/ppermute | solution.py:796
  31.1 28.0 %collective-permute-start.9 = (bf16[48,3456]{1,0:T(8,128)(2,1)S(1)}, bf16[48,3456]{1,0:T(8,128)(2,1)S(1)}, u32[]{:S(2)}, u32[]{:S(2)}) collective-permute-start(bf16[48,3456]{1,0:T(8,128)(2,1)S(1)} %get-tuple-element.133), channel_id=1, source_target_pairs={{0,4},{1,5},{2,6},{3,7},{4,8},{5,9},{6,10},{7,11},{8,12},{9,13},{1... | collective-permute-start | bytes 995336 | tf_op jit(solution)/shard_map/ppermute | solution.py:796
  39.3 19.8 %collective-permute-start.8 = (bf16[2,48,1664]{2,1,0:T(8,128)(2,1)S(1)}, bf16[2,48,1664]{2,1,0:T(8,128)(2,1)S(1)}, u32[]{:S(2)}, u32[]{:S(2)}) collective-permute-start(bf16[2,48,1664]{2,1,0:T(8,128)(2,1)S(1)} %get-tuple-element.246), channel_id=1, source_target_pairs={{0,2},{1,3},{2,0},{3,1},{4,6},{5,7},{6,4},{7,5},{8,10},{9,11},{10,... | collective-permute-start | bytes 958472 | tf_op jit(solution)/shard_map/ppermute | solution.py:805
  40.8 18.2 %collective-permute-start.7 = (bf16[2,48,1664]{2,1,0:T(8,128)(2,1)S(1)}, bf16[2,48,1664]{2,1,0:T(8,128)(2,1)S(1)}, u32[]{:S(2)}, u32[]{:S(2)}) collective-permute-start(bf16[2,48,1664]{2,1,0:T(8,128)(2,1)S(1)} %get-tuple-element.247), channel_id=1, source_target_pairs={{0,2},{1,3},{2,0},{3,1},{4,6},{5,7},{6,4},{7,5},{8,10},{9,11},{10,... | collective-permute-start | bytes 958472 | tf_op jit(solution)/shard_map/ppermute | solution.py:805
  42.0 20.7 %collective-permute-start.14 = (bf16[1,48,3456]{2,1,0:T(8,128)(2,1)}, bf16[1,48,3456]{2,1,0:T(8,128)(2,1)}, u32[]{:S(2)}, u32[]{:S(2)}) collective-permute-start(bf16[1,48,3456]{2,1,0:T(8,128)(2,1)} %collective-permute-done.5.refs_2_), channel_id=1, source_target_pairs={{0,2},{1,3},{2,0},{3,1},{4,6},{5,7},{6,4},{7,5},{8,10},{9,11},{10,... | collective-permute-start | bytes 995336 | tf_op jit(solution)/shard_map/ppermute | solution.py:805
  63.9 24.9 %collective-permute-start.13 = (bf16[3,48,3456]{2,1,0:T(8,128)(2,1)S(1)}, bf16[3,48,3456]{2,1,0:T(8,128)(2,1)}, u32[]{:S(2)}, u32[]{:S(2)}) collective-permute-start(bf16[3,48,3456]{2,1,0:T(8,128)(2,1)S(1)} %pad_maximum_fusion.refs_1_), channel_id=1, source_target_pairs={{0,2},{1,3},{2,0},{3,1},{4,6},{5,7},{6,4},{7,5},{8,10},{9,11},{10,... | collective-permute-start | bytes 2985992 | tf_op jit(solution)/shard_map/ppermute | solution.py:805
  64.4 24.3 %collective-permute-start.12 = (bf16[3,48,3456]{2,1,0:T(8,128)(2,1)S(1)}, bf16[3,48,3456]{2,1,0:T(8,128)(2,1)}, u32[]{:S(2)}, u32[]{:S(2)}) collective-permute-start(bf16[3,48,3456]{2,1,0:T(8,128)(2,1)S(1)} %pad_maximum_fusion.refs_1_), channel_id=1, source_target_pairs={{0,1},{1,0},{2,3},{3,2},{4,5},{5,4},{6,7},{7,6},{8,9},{9,8},{10,11... | collective-permute-start | bytes 2985992 | tf_op jit(solution)/shard_map/ppermute | solution.py:805
  64.9 25.3 %collective-permute-start.27 = (bf16[1,48,3456]{2,1,0:T(8,128)(2,1)}, bf16[1,48,3456]{2,1,0:T(8,128)(2,1)}, u32[]{:S(2)}, u32[]{:S(2)}) collective-permute-start(bf16[1,48,3456]{2,1,0:T(8,128)(2,1)} %collective-permute-done.14.refs_6_), channel_id=1, source_target_pairs={{0,16},{16,0},{1,17},{17,1},{2,18},{18,2},{3,19},{19,3},{4,20},{20... | collective-permute-start | bytes 995336 | tf_op jit(solution)/shard_map/ppermute | solution.py:809
  89.4 14.5 %collective-permute-start.20 = (bf16[3,48,3456]{2,1,0:T(8,128)(2,1)}, bf16[3,48,3456]{2,1,0:T(8,128)(2,1)}, u32[]{:S(2)}, u32[]{:S(2)}) collective-permute-start(bf16[3,48,3456]{2,1,0:T(8,128)(2,1)} %collective-permute-done.12.refs_3_), channel_id=1, source_target_pairs={{0,2},{1,3},{2,0},{3,1},{4,6},{5,7},{6,4},{7,5},{8,10},{9,11},{10,... | collective-permute-start | bytes 2985992 | tf_op jit(solution)/shard_map/ppermute | solution.py:805
  181.5 25.3 %collective-permute-start.31 = (bf16[4,48,3456]{2,1,0:T(8,128)(2,1)}, bf16[4,48,3456]{2,1,0:T(8,128)(2,1)S(1)}, u32[]{:S(2)}, u32[]{:S(2)}) collective-permute-start(bf16[4,48,3456]{2,1,0:T(8,128)(2,1)} %get-tuple-element.169), channel_id=1, source_target_pairs={{0,2},{1,3},{2,0},{3,1},{4,6},{5,7},{6,4},{7,5},{8,10},{9,11},{10,... | collective-permute-start | bytes 3981320 | tf_op jit(solution)/shard_map/ppermute | solution.py:805
  182.2 31.5 %collective-permute-start.30 = (bf16[4,48,3456]{2,1,0:T(8,128)(2,1)}, bf16[4,48,3456]{2,1,0:T(8,128)(2,1)}, u32[]{:S(2)}, u32[]{:S(2)}) collective-permute-start(bf16[4,48,3456]{2,1,0:T(8,128)(2,1)} %get-tuple-element.168), channel_id=1, source_target_pairs={{0,2},{1,3},{2,0},{3,1},{4,6},{5,7},{6,4},{7,5},{8,10},{9,11},{10,... | collective-permute-start | bytes 3981320 | tf_op jit(solution)/shard_map/ppermute | solution.py:805
  218.5 18.1 %collective-permute-start.32 = (bf16[4,48,3456]{2,1,0:T(8,128)(2,1)}, bf16[4,48,3456]{2,1,0:T(8,128)(2,1)}, u32[]{:S(2)}, u32[]{:S(2)}) collective-permute-start(bf16[4,48,3456]{2,1,0:T(8,128)(2,1)} %shard_map.417), channel_id=1, source_target_pairs={{0,1},{1,0},{2,3},{3,2},{4,5},{5,4},{6,7},{7,6},{8,9},{9,8},{10,11... | collective-permute-start | bytes 3981320 | tf_op jit(solution)/shard_map/ppermute | solution.py:805
  252.4 19.9 %collective-permute-start.40 = (bf16[4,48,1152]{2,1,0:T(8,128)(2,1)}, bf16[4,48,1152]{2,1,0:T(8,128)(2,1)S(1)}, u32[]{:S(2)}, u32[]{:S(2)}) collective-permute-start(bf16[4,48,1152]{2,1,0:T(8,128)(2,1)} %get-tuple-element.196), channel_id=1, source_target_pairs={{0,2},{1,3},{2,0},{3,1},{4,6},{5,7},{6,4},{7,5},{8,10},{9,11},{10,... | collective-permute-start | bytes 1327112 | tf_op jit(solution)/shard_map/ppermute | solution.py:805
  253.4 19.0 %collective-permute-start.39 = (bf16[4,48,1152]{2,1,0:T(8,128)(2,1)}, bf16[4,48,1152]{2,1,0:T(8,128)(2,1)}, u32[]{:S(2)}, u32[]{:S(2)}) collective-permute-start(bf16[4,48,1152]{2,1,0:T(8,128)(2,1)} %get-tuple-element.182), channel_id=1, source_target_pairs={{0,2},{1,3},{2,0},{3,1},{4,6},{5,7},{6,4},{7,5},{8,10},{9,11},{10,... | collective-permute-start | bytes 1327112 | tf_op jit(solution)/shard_map/ppermute | solution.py:805
  255.1 17.2 %collective-permute-start.34 = (bf16[48,3456]{1,0:T(8,128)(2,1)}, bf16[48,3456]{1,0:T(8,128)(2,1)}, u32[]{:S(2)}, u32[]{:S(2)}) collective-permute-start(bf16[48,3456]{1,0:T(8,128)(2,1)} %get-tuple-element.189), channel_id=1, source_target_pairs={{0,4},{1,5},{2,6},{3,7},{4,8},{5,9},{6,10},{7,11},{8,12},{9,13},{1... | collective-permute-start | bytes 995336 | tf_op jit(solution)/shard_map/ppermute | solution.py:796
  255.1 17.2 %collective-permute-start.36 = (bf16[48,3456]{1,0:T(8,128)(2,1)}, bf16[48,3456]{1,0:T(8,128)(2,1)}, u32[]{:S(2)}, u32[]{:S(2)}) collective-permute-start(bf16[48,3456]{1,0:T(8,128)(2,1)} %get-tuple-element.191), channel_id=1, source_target_pairs={{0,12},{1,13},{2,14},{3,15},{4,0},{5,1},{6,2},{7,3},{8,4},{9,5},{1... | collective-permute-start | bytes 995336 | tf_op jit(solution)/shard_map/ppermute | solution.py:796
  275.7 18.5 %collective-permute-start.37 = (bf16[4,48,896]{2,1,0:T(8,128)(2,1)S(1)}, bf16[4,48,896]{2,1,0:T(8,128)(2,1)}, u32[]{:S(2)}, u32[]{:S(2)}) collective-permute-start(bf16[4,48,896]{2,1,0:T(8,128)(2,1)S(1)} %copy-done.48), channel_id=1, source_target_pairs={{0,2},{1,3},{2,0},{3,1},{4,6},{5,7},{6,4},{7,5},{8,10},{9,11},{10,... | collective-permute-start | bytes 1032200 | tf_op jit(solution)/shard_map/ppermute | solution.py:805
  277.3 17.0 %collective-permute-start.38 = (bf16[4,48,896]{2,1,0:T(8,128)(2,1)S(1)}, bf16[4,48,896]{2,1,0:T(8,128)(2,1)}, u32[]{:S(2)}, u32[]{:S(2)}) collective-permute-start(bf16[4,48,896]{2,1,0:T(8,128)(2,1)S(1)} %copy-done.47), channel_id=1, source_target_pairs={{0,2},{1,3},{2,0},{3,1},{4,6},{5,7},{6,4},{7,5},{8,10},{9,11},{10,... | collective-permute-start | bytes 1032200 | tf_op jit(solution)/shard_map/ppermute | solution.py:805
  277.8 15.7 %collective-permute-start.35 = (bf16[48,3456]{1,0:T(8,128)(2,1)S(1)}, bf16[48,3456]{1,0:T(8,128)(2,1)S(1)}, u32[]{:S(2)}, u32[]{:S(2)}) collective-permute-start(bf16[48,3456]{1,0:T(8,128)(2,1)S(1)} %copy-done.25), channel_id=1, source_target_pairs={{0,8},{1,9},{2,10},{3,11},{4,12},{5,13},{6,14},{7,15},{8,0},{9,1},... | collective-permute-start | bytes 995336 | tf_op jit(solution)/shard_map/ppermute | solution.py:796
  (87 other events, 862.4 us)

commit v2 on v1

--- a/solution.py
+++ b/solution.py
@@ -574,7 +574,7 @@
         out_shape=[shape, shape],
         scratch_shapes=[pltpu.VMEM((2, UNITS, 48, QKV_HALF), BF), pltpu.SemaphoreType.DMA((2,))],
         cost_estimate=pl.CostEstimate(flops=SLOTS * D * D, bytes_accessed=2**20, transcendentals=0),
-        compiler_params=pltpu.CompilerParams(vmem_limit_bytes=48 * 2**20),
+        compiler_params=pltpu.CompilerParams(vmem_limit_bytes=62 * 2**20),
     )(core, first, g)
 
 
@@ -869,7 +869,7 @@
         ),
         out_shape=[out_shape] * len(counts),
         cost_estimate=pl.CostEstimate(flops=0, bytes_accessed=(200 if apart else 12) * 2**20, transcendentals=0),
-        compiler_params=pltpu.CompilerParams(vmem_limit_bytes=48 * 2**20),
+        compiler_params=pltpu.CompilerParams(vmem_limit_bytes=(62 if block[1] > D * 3 else 48) * 2**20),
     )(places, *operands)
 
 
@@ -890,6 +890,17 @@
         )
         (first,) = column_sums(self.places, self.mine, self.given, [(1, [self.far_came])])
         self.arrived = [along_plane(first, 0), self.second_came]
+        return first
+
+    def send_far_alone(self, sooner):
+        (far,) = column_sums(self.places, self.mine, hold_back(self.given, sooner), [(3, [])])
+        self.far_came = along_plane(far, 1)
+        return far
+
+    def send_neighbours(self, sooner):
+        far_came = hold_back(self.far_came, sooner)
+        first, second = column_sums(self.places, self.mine, self.given, [(1, [far_came]), (2, [])])
+        self.arrived = [along_plane(first, 0), along_plane(second, 1)]
         return first
 
     def send_column(self, sooner=None):
@@ -944,7 +955,7 @@
 
     def send_first(self, sooner):
         far_came, self.second_came = hold_back((self.far_came, self.second_came), sooner)
-        (first,) = arrival_sums(self.places, [self.first, far_came], False)
+        first = (self.first.astype(F32) + far_came.astype(F32)).astype(BF)
         self.first_came = along_plane(first, 0)
         return first
 
@@ -954,17 +965,18 @@
         self.came = [along_z(unit, ahead + 1) for ahead, unit in enumerate(units)]
         return self.own
 
-    def finish(self):
+    def finish(self, sooner):
         total = self.own.astype(F32)
-        for part in self.came:
+        for part in hold_back(self.came, sooner):
             total = total + part.astype(F32)
         own = total.astype(BF)
         return own.astype(F32) + swap_core(own).astype(F32)
 
 
 def sum_small(values):
-    for turn in (1, 2, 4, 8):
-        values = values + lax.ppermute(values, "fsdp", [(chip, chip ^ turn) for chip in range(UNITS)])
+    for turns in ((1, 2, 3), (4, 8, 12)):
+        came = [lax.ppermute(values, "fsdp", [(chip, chip ^ turn) for chip in range(UNITS)]) for turn in turns]
+        values = (values + came[0]) + (came[1] + came[2])
     return values
 
 
@@ -1071,7 +1083,7 @@
 
 
 FORWARD_CALLS = (2, 3, 1)
-BACKWARD_CALLS = (1, 3, 2)
+BACKWARD_CALLS = (1, 2, 3)
 
 
 def on_device(
@@ -1172,9 +1184,9 @@
     if rounds:
         later = Scatter(mine_later, give_later, places)
         backward_part(0, None)
-        sent = later.send_far(state[0])
+        sent = later.send_far_alone(state[0])
         backward_part(1, sent)
-        sent = later.send_first(state[0])
+        sent = later.send_neighbours(state[0])
         backward_part(2, sent)
         qkv_parts = qkv_end(later.arrived)
         sooner = Scatter(*qkv_parts, places)
@@ -1184,14 +1196,14 @@
         small = SmallScatter(*small_parts, places)
         sent = sooner.send_first((grad_in, later.came[0], later.came[2]))
         sent = sooner.send_column(sent)
-        sent = small.send_first((sent, later.came[1]))
+        sent = small.send_first((sent, later.came[1], sooner.came[0]))
         sent = small.send_column((sent, sooner.came))
         later_sums = later.finish(sent)
         (out_new, up_new, down_new), later_table = update_moments(
             update_later_kernel, side, later_sums, of_out + of_up + of_down
         )
         qkv_sums = sooner.finish(later_table)
-        small_sums = small.finish()
+        small_sums = small.finish(later_table)
         (qkv_new, mod_new), sooner_table = update_moments(
             update_sooner_kernel, side, qkv_sums + (small_sums,), of_qkv + tuple(part.T for part in of_mod)
         )

time: 355 us -> 346 us (0.975)
  waiting for transfers between devices: 70.9 us -> 62.1 us
    ppermute x4 -> x6, waiting for transfers between devices: 9.91 us -> 4.97 us  [sum_small(): lax.ppermute(values, 'fsdp', [(chip, chip ^ turn) for chip in range(UNITS)])]
    unnamed x111 -> x109, local copies, waits for them, and re-layouts: 8.52 us -> 5.51 us
    ppermute x4 -> x6, starting transfers between devices: 5.11 us -> 7.89 us  [sum_small(): lax.ppermute(values, 'fsdp', [(chip, chip ^ turn) for chip in range(UNITS)])]
  transfers between devices with their start and end apart: 56 -> 58, of which waited for: 21 -> 22; matrix products, arithmetic and copies ran while one was open for 5% -> 4% of each run, Pallas kernels for 31% -> 32%
where the time goes in v2:
time: 346 us; the launch traced here: 342 us
  Pallas kernels  196 us (57%)
  waiting for transfers between devices  62.1 us (18%)
  starting transfers between devices  57.2 us (17%)
  other arithmetic  14.1 us (4%)
  local copies, waits for them, and re-layouts  10.4 us (3%)
    pallas_call x1, Pallas kernels, middle_part(): pl.pallas_call(functools.partial(middle_kernel, rows), grid=(SLOTS // row...  54.7 us
    pallas_call x3, Pallas kernels, attention_backward(): pl.pallas_call(functools.partial(attention_backward_kernel, block), grid=...  49.5 us
    ppermute x15, waiting for transfers between devices, along_z(): lax.ppermute(values, 'fsdp', [(chip, chip % 4 + 4 * ((chip // 4 + ahead)...  33 us
    pallas_call x3, Pallas kernels, attention_forward(): pl.pallas_call(functools.partial(attention_forward_kernel, block), grid=(...  25.3 us
    ppermute x15, starting transfers between devices, along_z(): lax.ppermute(values, 'fsdp', [(chip, chip % 4 + 4 * ((chip // 4 + ahead)...  25 us
    pallas_call x6, Pallas kernels, column_sums(): pl.pallas_call(functools.partial(column_sums_kernel, counts), grid_spec=p...  21.9 us
    ppermute x19, waiting for transfers between devices, along_plane(): return lax.ppermute(values, ('rep', 'fsdp'), moves)  21.8 us
    ppermute x19, starting transfers between devices, along_plane(): return lax.ppermute(values, ('rep', 'fsdp'), moves)  20.6 us
  transfers between devices with their start and end apart: 58, of which 22 were waited for; matrix products, arithmetic and copies ran while one was open for 4% of the time, Pallas kernels for 32%

profile of v2, /device:TPU:0, one launch (start us, length us, event | category | flops | bytes accessed | tf_op | source)
XLA Modules:
  0.0 341.8 jit_solution(1227091149012031700)
XLA Ops:
  3.4 5.1 %collective-permute-start.2 = (bf16[48,1664]{1,0:T(8,128)(2,1)S(1)}, bf16[48,1664]{1,0:T(8,128)(2,1)S(1)}, u32[]{:S(2)}, u32[]{:S(2)}) collective-permute-start(bf16[48,1664]{1,0:T(8,128)(2,1)S(1)} %maximum_bitcast_fusion), channel_id=1, source_target_pairs={{0,12},{1,13},{2,14},{3,15},{4,0},{5,1},{6,2},{7,3},{8,4},{9,5},{1... | collective-permute-start | bytes 479240 | tf_op jit(solution)/shard_map/ppermute | solution.py:796
  17.3 4.8 %collective-permute-done.1 = bf16[48,1664]{1,0:T(8,128)(2,1)S(1)} collective-permute-done((bf16[48,1664]{1,0:T(8,128)(2,1)S(1)}, bf16[48,1664]{1,0:T(8,128)(2,1)S(1)}, u32[]{:S(2)}, u32[]{:S(2)}) %collective-permute-start.1) | collective-permute-done | bytes 159776 | tf_op jit(solution)/shard_map/ppermute | solution.py:796
  33.3 6.0 %collective-permute-done.4.refs_2_ = bf16[4,48,1664]{2,1,0:T(8,128)(2,1)S(1)} collective-permute-done((bf16[4,48,1664]{2,1,0:T(8,128)(2,1)S(1)}, bf16[4,48,1664]{2,1,0:T(8,128)(2,1)S(1)}, u32[]{:S(2)}, u32[]{:S(2)}) %collective-permute-start.4) | collective-permute-done | bytes 639008 | tf_op jit(solution)/shard_map/ppermute | solution.py:805
  45.1 13.9 %collective-permute-done.10 = bf16[48,3456]{1,0:T(8,128)(2,1)S(1)} collective-permute-done((bf16[48,3456]{1,0:T(8,128)(2,1)S(1)}, bf16[48,3456]{1,0:T(8,128)(2,1)S(1)}, u32[]{:S(2)}, u32[]{:S(2)}) %collective-permute-start.10) | collective-permute-done | bytes 331808 | tf_op jit(solution)/shard_map/ppermute | solution.py:796
  66.2 12.9 %shard_map.409 = (bf16[1024,2304]{1,0:T(8,128)(2,1)}, bf16[1024,768]{1,0:T(8,128)(2,1)}, bf16[768,2304]{1,0:T(8,128)(2,1)}, f32[8,4608]{1,0:T(8,128)}, f32[80,128]{1,0:T(8,128)}) custom-call(s32[32]{0:T(128)} %pad_add_fusion.order_ref, s32[1]{0:T(128)} %bitcast.2.core_ref.side_ref, s32[8]{0:T(128)} %get-tuple-element.260.tiles_ref, ...), custom_call_target="tpu_custom_call" | custom-call | flops 3623878656 | bytes 20971520 | tf_op jit(solution)/shard_map/pallas_call | solution.py:326
  79.1 8.5 %shard_map.410 = (bf16[1024,768]{1,0:T(8,128)(2,1)}, bf16[1024,768]{1,0:T(8,128)(2,1)}) custom-call(bf16[1024,2304]{1,0:T(8,128)(2,1)} %get-tuple-element.146.q_ref.k_ref.v_ref, bf16[1024,2304]{1,0:T(8,128)(2,1)} %get-tuple-element.146.q_ref.k_ref.v_ref, bf16[1024,2304]{1,0:T(8,128)(2,1)} %get-tuple-element.146.q_ref.k_ref.v_ref, ...), custom_call_target="tpu_custom_call" | custom-call | flops 12582912000 | bytes 2621440 | tf_op jit(solution)/shard_map/pallas_call | solution.py:97
  91.7 11.6 %shard_map.411 = (bf16[1024,768]{1,0:T(8,128)(2,1)}, bf16[1024,768]{1,0:T(8,128)(2,1)}) custom-call(bf16[1024,2304]{1,0:T(8,128)(2,1)} %get-tuple-element.146.q_ref.k_ref.v_ref, bf16[1024,2304]{1,0:T(8,128)(2,1)} %get-tuple-element.146.q_ref.k_ref.v_ref, ...), custom_call_target="tpu_custom_call", output_to_operand_aliasing={{0}: (5, {}), {1}: (6, {})} | custom-call | flops 18874368000 | bytes 3932160 | tf_op jit(solution)/shard_map/pallas_call | solution.py:97
  104.6 5.2 %shard_map.412 = (bf16[1024,768]{1,0:T(8,128)(2,1)}, bf16[1024,768]{1,0:T(8,128)(2,1)}) custom-call(bf16[1024,2304]{1,0:T(8,128)(2,1)} %get-tuple-element.146.q_ref.k_ref.v_ref, bf16[1024,2304]{1,0:T(8,128)(2,1)} %get-tuple-element.146.q_ref.k_ref.v_ref, ...), custom_call_target="tpu_custom_call", output_to_operand_aliasing={{0}: (5, {}), {1}: (6, {})} | custom-call | flops 6291456000 | bytes 1310720 | tf_op jit(solution)/shard_map/pallas_call | solution.py:97
  109.8 54.7 %shard_map.413 = (bf16[1024,768]{1,0:T(8,128)(2,1)}, f32[1024,768]{1,0:T(8,128)}, bf16[1024,768]{1,0:T(8,128)(2,1)}, f32[8,8,768]{2,1,0:T(8,128)}, f32[8,3840]{1...) custom-call(s32[32]{0:T(128)} %pad_add_fusion.order_ref, s32[1]{0:T(128)} %bitcast.2.core_ref.side_ref, ...), custom_call_target="tpu_custom_call" | custom-call | flops 32614907904 | bytes 52428800 | tf_op jit(solution)/shard_map/pallas_call | solution.py:521
  166.3 9.5 %shard_map.414.refs_0_ = bf16[3,1024,768]{2,1,0:T(8,128)(2,1)} custom-call(bf16[1024,2304]{1,0:T(8,128)(2,1)} %get-tuple-element.146.q_ref.k_ref.v_ref, bf16[1024,2304]{1,0:T(8,128)(2,1)} %get-tuple-element.146.q_ref.k_ref.v_ref, bf16[1024,2304]{1,0:T(8,128)(2,1)} %get-tuple-element.146.q_ref.k_ref.v_ref, bf16[1024,768]{1,0:T(8,128)(2,1)} %get-tuple-element.165.fo_ref, ...), custom_call_target="tpu_custom_call" | custom-call | flops 4194304000 | bytes 2621440 | tf_op jit(solution)/shard_map/pallas_call | solution.py:175
  175.9 4.5 %shard_map.415 = bf16[4,48,3456]{2,1,0:T(8,128)(2,1)} custom-call(s32[8]{0:T(128)} %fusion.9.places_ref.refs_0_, bf16[4,4,48,3456]{3,2,1,0:T(8,128)(2,1)} %bitcast.92, bf16[4,4,48,3456]{3,2,1,0:T(8,128)(2,1)} %bitcast.38.refs_1_), custom_call_target="tpu_custom_call" | custom-call | bytes 12582912 | tf_op jit(solution)/shard_map/pallas_call | solution.py:862
  181.0 16.5 %shard_map.416.refs_0_ = bf16[3,1024,768]{2,1,0:T(8,128)(2,1)} custom-call(bf16[1024,2304]{1,0:T(8,128)(2,1)} %get-tuple-element.146.q_ref.k_ref.v_ref, bf16[1024,2304]{1,0:T(8,128)(2,1)} %get-tuple-element.146.q_ref.k_ref.v_ref, bf16[1024,2304]{1,0:T(8,128)(2,1)} %get-tuple-element.146.q_ref.k_ref.v_ref, ...), custom_call_target="tpu_custom_call", output_to_operand_aliasing={{}: (9, {})} | custom-call | flops 8388608000 | bytes 5242880 | tf_op jit(solution)/shard_map/pallas_call | solution.py:175
  199.5 5.6 %shard_map.417 = (bf16[4,48,3456]{2,1,0:T(8,128)(2,1)}, bf16[4,48,3456]{2,1,0:T(8,128)(2,1)}) custom-call(s32[8]{0:T(128)} %fusion.9.places_ref.refs_0_, bf16[4,4,48,3456]{3,2,1,0:T(8,128)(2,1)} %bitcast.93, bf16[4,4,48,3456]{3,2,1,0:T(8,128)(2,1)} %bitcast.37.refs_1_.refs_4_.refs_5_.refs_9_.refs_13_, bf16[4,48,3456]{2,1,0:T(8,128)(2,1)} %copy-done.21, ...), custom_call_target="tpu_custom_call" | custom-call | bytes 12582912 | tf_op jit(solution)/shard_map/pallas_call | solution.py:862
  207.3 23.5 %shard_map.418.g_ref = bf16[3,1024,768]{2,1,0:T(8,128)(2,1)} custom-call(bf16[1024,2304]{1,0:T(8,128)(2,1)} %get-tuple-element.146.q_ref.k_ref.v_ref, bf16[1024,2304]{1,0:T(8,128)(2,1)} %get-tuple-element.146.q_ref.k_ref.v_ref, bf16[1024,2304]{1,0:T(8,128)(2,1)} %get-tuple-element.146.q_ref.k_ref.v_ref, ...), custom_call_target="tpu_custom_call", output_to_operand_aliasing={{}: (9, {})} | custom-call | flops 12582912000 | bytes 7864320 | tf_op jit(solution)/shard_map/pallas_call | solution.py:175
  230.8 5.5 %collective-permute-done.32.refs_3_.refs_7_.refs_11_.refs_15_ = bf16[4,48,3456]{2,1,0:T(8,128)(2,1)S(1)} collective-permute-done((bf16[4,48,3456]{2,1,0:T(8,128)(2,1)}, bf16[4,48,3456]{2,1,0:T(8,128)(2,1)S(1)}, u32[]{:S(2)}, u32[]{:S(2)}) %collective-permute-start.32) | collective-permute-done | bytes 1327136 | tf_op jit(solution)/shard_map/ppermute | solution.py:805
  236.3 9.0 %shard_map.419 = (bf16[16,48,1152]{2,1,0:T(8,128)(2,1)}, bf16[16,48,1152]{2,1,0:T(8,128)(2,1)}) custom-call(s32[1]{0:T(128)} %bitcast.2.core_ref.side_ref, bf16[1024,768]{1,0:T(8,128)(2,1)} %get-tuple-element.174.first_ref, bf16[3,1024,768]{2,1,0:T(8,128)(2,1)} %shard_map.418.g_ref), custom_call_target="tpu_custom_call" | custom-call | flops 603979776 | bytes 1048576 | tf_op jit(solution)/shard_map/pallas_call | solution.py:569
  245.5 4.7 %shard_map.420 = (bf16[48,3456]{1,0:T(8,128)(2,1)}, bf16[48,3456]{1,0:T(8,128)(2,1)}, bf16[48,3456]{1,0:T(8,128)(2,1)}, bf16[48,3456]{1,0:T(8,128)(2,1)}) custom-call(s32[8]{0:T(128)} %fusion.9.places_ref.refs_0_, bf16[4,4,48,3456]{3,2,1,0:T(8,128)(2,1)} %bitcast.95, bf16[4,4,48,3456]{3,2,1,0:T(8,128)(2,1)} %bitcast.37.refs_1_.refs_4_.refs_5_.refs_9_.refs_13_, ...), custom_call_target="tpu_custom_call" | custom-call | bytes 209715200 | tf_op jit(solution)/shard_map/pallas_call | solution.py:862
  255.7 3.8 %collective-permute-start.36 = (bf16[48,3456]{1,0:T(8,128)(2,1)}, bf16[48,3456]{1,0:T(8,128)(2,1)}, u32[]{:S(2)}, u32[]{:S(2)}) collective-permute-start(bf16[48,3456]{1,0:T(8,128)(2,1)} %get-tuple-element.192), channel_id=1, source_target_pairs={{0,12},{1,13},{2,14},{3,15},{4,0},{5,1},{6,2},{7,3},{8,4},{9,5},{1... | collective-permute-start | bytes 995336 | tf_op jit(solution)/shard_map/ppermute | solution.py:796
  259.5 13.3 %shard_map.422 = (f32[1024,768]{1,0:T(8,128)}, bf16[4,48,896]{2,1,0:T(8,128)(2,1)}, bf16[4,48,896]{2,1,0:T(8,128)(2,1)}, bf16[4,48,896]{2,1,0:T(8,128)(2,1)}, bf16[4,48,896]{2,1,0:T(8,128)(2,1)}) custom-call(s32[8]{0:T(128)} %fusion.9.places_ref.refs_0_, s32[8]{0:T(128)} %get-tuple-element.260.tiles_ref, f32[8,8]{1,0:T(8,128)} %convert_bitcast_fusion.member_ref, ...), custom_call_target="tpu_custom_call" | custom-call | flops 3623878656 | bytes 31457280 | tf_op jit(solution)/shard_map/pallas_call | solution.py:663
  280.8 7.7 %collective-permute-done.41.refs_2_.refs_6_.refs_10_.refs_14_ = bf16[4,48,1152]{2,1,0:T(8,128)(2,1)S(1)} collective-permute-done((bf16[4,48,1152]{2,1,0:T(8,128)(2,1)S(1)}, bf16[4,48,1152]{2,1,0:T(8,128)(2,1)S(1)}, u32[]{:S(2)}, u32[]{:S(2)}) %collective-permute-start.41) | collective-permute-done | bytes 442400 | tf_op jit(solution)/shard_map/ppermute | solution.py:805
  291.1 4.4 %collective-permute-done.35 = bf16[48,3456]{1,0:T(8,128)(2,1)S(1)} collective-permute-done((bf16[48,3456]{1,0:T(8,128)(2,1)S(1)}, bf16[48,3456]{1,0:T(8,128)(2,1)S(1)}, u32[]{:S(2)}, u32[]{:S(2)}) %collective-permute-start.35) | collective-permute-done | bytes 331808 | tf_op jit(solution)/shard_map/ppermute | solution.py:796
  300.4 5.3 %collective-permute-done.44 = bf16[48,1152]{1,0:T(8,128)(2,1)S(1)} collective-permute-done((bf16[48,1152]{1,0:T(8,128)(2,1)S(1)}, bf16[48,1152]{1,0:T(8,128)(2,1)S(1)}, u32[]{:S(2)}, u32[]{:S(2)}) %collective-permute-start.44) | collective-permute-done | bytes 110624 | tf_op jit(solution)/shard_map/ppermute | solution.py:796
  316.6 3.3 shard_map.426
  319.9 3.0 collective-permute-done.49
  (275 shorter events, 97.5 us)
Async XLA Ops:
  12.0 17.4 %collective-permute-start.6 = (bf16[1,48,3456]{2,1,0:T(8,128)(2,1)S(1)}, bf16[1,48,3456]{2,1,0:T(8,128)(2,1)S(1)}, u32[]{:S(2)}, u32[]{:S(2)}) collective-permute-start(bf16[1,48,3456]{2,1,0:T(8,128)(2,1)S(1)} %get-tuple-element.152.refs_0_), channel_id=1, source_target_pairs={{0,2},{1,3},{2,0},{3,1},{4,6},{5,7},{6,4},{7,5},{8,10},{9,11},{10,... | collective-permute-start | bytes 995336 | tf_op jit(solution)/shard_map/ppermute | solution.py:805
  13.6 17.5 %collective-permute-start.5 = (bf16[1,48,3456]{2,1,0:T(8,128)(2,1)S(1)}, bf16[1,48,3456]{2,1,0:T(8,128)(2,1)}, u32[]{:S(2)}, u32[]{:S(2)}) collective-permute-start(bf16[1,48,3456]{2,1,0:T(8,128)(2,1)S(1)} %get-tuple-element.152.refs_0_), channel_id=1, source_target_pairs={{0,1},{1,0},{2,3},{3,2},{4,5},{5,4},{6,7},{7,6},{8,9},{9,8},{10,11... | collective-permute-start | bytes 995336 | tf_op jit(solution)/shard_map/ppermute | solution.py:805
  22.2 17.1 %collective-permute-start.4 = (bf16[4,48,1664]{2,1,0:T(8,128)(2,1)S(1)}, bf16[4,48,1664]{2,1,0:T(8,128)(2,1)S(1)}, u32[]{:S(2)}, u32[]{:S(2)}) collective-permute-start(bf16[4,48,1664]{2,1,0:T(8,128)(2,1)S(1)} %pad_maximum_fusion.1.refs_0_), channel_id=1, source_target_pairs={{0,2},{1,3},{2,0},{3,1},{4,6},{5,7},{6,4},{7,5},{8,10},{9,11},{10,... | collective-permute-start | bytes 1916936 | tf_op jit(solution)/shard_map/ppermute | solution.py:805
  23.7 16.4 %collective-permute-start.3 = (bf16[4,48,1664]{2,1,0:T(8,128)(2,1)S(1)}, bf16[4,48,1664]{2,1,0:T(8,128)(2,1)S(1)}, u32[]{:S(2)}, u32[]{:S(2)}) collective-permute-start(bf16[4,48,1664]{2,1,0:T(8,128)(2,1)S(1)} %pad_maximum_fusion.1.refs_0_), channel_id=1, source_target_pairs={{0,1},{1,0},{2,3},{3,2},{4,5},{5,4},{6,7},{7,6},{8,9},{9,8},{10,11... | collective-permute-start | bytes 1916936 | tf_op jit(solution)/shard_map/ppermute | solution.py:805
  28.2 14.7 %collective-permute-start.11 = (bf16[48,3456]{1,0:T(8,128)(2,1)S(1)}, bf16[48,3456]{1,0:T(8,128)(2,1)S(1)}, u32[]{:S(2)}, u32[]{:S(2)}) collective-permute-start(bf16[48,3456]{1,0:T(8,128)(2,1)S(1)} %get-tuple-element.135), channel_id=1, source_target_pairs={{0,12},{1,13},{2,14},{3,15},{4,0},{5,1},{6,2},{7,3},{8,4},{9,5},{1... | collective-permute-start | bytes 995336 | tf_op jit(solution)/shard_map/ppermute | solution.py:796
  29.4 29.6 %collective-permute-start.10 = (bf16[48,3456]{1,0:T(8,128)(2,1)S(1)}, bf16[48,3456]{1,0:T(8,128)(2,1)S(1)}, u32[]{:S(2)}, u32[]{:S(2)}) collective-permute-start(bf16[48,3456]{1,0:T(8,128)(2,1)S(1)} %get-tuple-element.135), channel_id=1, source_target_pairs={{0,8},{1,9},{2,10},{3,11},{4,12},{5,13},{6,14},{7,15},{8,0},{9,1},... | collective-permute-start | bytes 995336 | tf_op jit(solution)/shard_map/ppermute | solution.py:796
  31.2 27.9 %collective-permute-start.9 = (bf16[48,3456]{1,0:T(8,128)(2,1)S(1)}, bf16[48,3456]{1,0:T(8,128)(2,1)S(1)}, u32[]{:S(2)}, u32[]{:S(2)}) collective-permute-start(bf16[48,3456]{1,0:T(8,128)(2,1)S(1)} %get-tuple-element.135), channel_id=1, source_target_pairs={{0,4},{1,5},{2,6},{3,7},{4,8},{5,9},{6,10},{7,11},{8,12},{9,13},{1... | collective-permute-start | bytes 995336 | tf_op jit(solution)/shard_map/ppermute | solution.py:796
  40.2 18.9 %collective-permute-start.8 = (bf16[2,48,1664]{2,1,0:T(8,128)(2,1)S(1)}, bf16[2,48,1664]{2,1,0:T(8,128)(2,1)S(1)}, u32[]{:S(2)}, u32[]{:S(2)}) collective-permute-start(bf16[2,48,1664]{2,1,0:T(8,128)(2,1)S(1)} %get-tuple-element.250), channel_id=1, source_target_pairs={{0,2},{1,3},{2,0},{3,1},{4,6},{5,7},{6,4},{7,5},{8,10},{9,11},{10,... | collective-permute-start | bytes 958472 | tf_op jit(solution)/shard_map/ppermute | solution.py:805
  41.7 17.3 %collective-permute-start.7 = (bf16[2,48,1664]{2,1,0:T(8,128)(2,1)S(1)}, bf16[2,48,1664]{2,1,0:T(8,128)(2,1)S(1)}, u32[]{:S(2)}, u32[]{:S(2)}) collective-permute-start(bf16[2,48,1664]{2,1,0:T(8,128)(2,1)S(1)} %get-tuple-element.251), channel_id=1, source_target_pairs={{0,2},{1,3},{2,0},{3,1},{4,6},{5,7},{6,4},{7,5},{8,10},{9,11},{10,... | collective-permute-start | bytes 958472 | tf_op jit(solution)/shard_map/ppermute | solution.py:805
  42.9 19.7 %collective-permute-start.14 = (bf16[1,48,3456]{2,1,0:T(8,128)(2,1)}, bf16[1,48,3456]{2,1,0:T(8,128)(2,1)}, u32[]{:S(2)}, u32[]{:S(2)}) collective-permute-start(bf16[1,48,3456]{2,1,0:T(8,128)(2,1)} %collective-permute-done.5.refs_2_), channel_id=1, source_target_pairs={{0,2},{1,3},{2,0},{3,1},{4,6},{5,7},{6,4},{7,5},{8,10},{9,11},{10,... | collective-permute-start | bytes 995336 | tf_op jit(solution)/shard_map/ppermute | solution.py:805
  63.9 24.9 %collective-permute-start.13 = (bf16[3,48,3456]{2,1,0:T(8,128)(2,1)S(1)}, bf16[3,48,3456]{2,1,0:T(8,128)(2,1)}, u32[]{:S(2)}, u32[]{:S(2)}) collective-permute-start(bf16[3,48,3456]{2,1,0:T(8,128)(2,1)S(1)} %pad_maximum_fusion.refs_1_), channel_id=1, source_target_pairs={{0,2},{1,3},{2,0},{3,1},{4,6},{5,7},{6,4},{7,5},{8,10},{9,11},{10,... | collective-permute-start | bytes 2985992 | tf_op jit(solution)/shard_map/ppermute | solution.py:805
  64.4 24.3 %collective-permute-start.12 = (bf16[3,48,3456]{2,1,0:T(8,128)(2,1)S(1)}, bf16[3,48,3456]{2,1,0:T(8,128)(2,1)}, u32[]{:S(2)}, u32[]{:S(2)}) collective-permute-start(bf16[3,48,3456]{2,1,0:T(8,128)(2,1)S(1)} %pad_maximum_fusion.refs_1_), channel_id=1, source_target_pairs={{0,1},{1,0},{2,3},{3,2},{4,5},{5,4},{6,7},{7,6},{8,9},{9,8},{10,11... | collective-permute-start | bytes 2985992 | tf_op jit(solution)/shard_map/ppermute | solution.py:805
  64.9 25.1 %collective-permute-start.27 = (bf16[1,48,3456]{2,1,0:T(8,128)(2,1)}, bf16[1,48,3456]{2,1,0:T(8,128)(2,1)}, u32[]{:S(2)}, u32[]{:S(2)}) collective-permute-start(bf16[1,48,3456]{2,1,0:T(8,128)(2,1)} %collective-permute-done.14.refs_6_), channel_id=1, source_target_pairs={{0,16},{16,0},{1,17},{17,1},{2,18},{18,2},{3,19},{19,3},{4,20},{20... | collective-permute-start | bytes 995336 | tf_op jit(solution)/shard_map/ppermute | solution.py:809
  89.4 14.5 %collective-permute-start.20 = (bf16[3,48,3456]{2,1,0:T(8,128)(2,1)}, bf16[3,48,3456]{2,1,0:T(8,128)(2,1)}, u32[]{:S(2)}, u32[]{:S(2)}) collective-permute-start(bf16[3,48,3456]{2,1,0:T(8,128)(2,1)} %collective-permute-done.12.refs_3_), channel_id=1, source_target_pairs={{0,2},{1,3},{2,0},{3,1},{4,6},{5,7},{6,4},{7,5},{8,10},{9,11},{10,... | collective-permute-start | bytes 2985992 | tf_op jit(solution)/shard_map/ppermute | solution.py:805
  180.4 18.0 %collective-permute-start.30 = (bf16[4,48,3456]{2,1,0:T(8,128)(2,1)}, bf16[4,48,3456]{2,1,0:T(8,128)(2,1)S(1)}, u32[]{:S(2)}, u32[]{:S(2)}) collective-permute-start(bf16[4,48,3456]{2,1,0:T(8,128)(2,1)} %shard_map.415), channel_id=1, source_target_pairs={{0,2},{1,3},{2,0},{3,1},{4,6},{5,7},{6,4},{7,5},{8,10},{9,11},{10,... | collective-permute-start | bytes 3981320 | tf_op jit(solution)/shard_map/ppermute | solution.py:805
  205.1 31.2 %collective-permute-start.32 = (bf16[4,48,3456]{2,1,0:T(8,128)(2,1)}, bf16[4,48,3456]{2,1,0:T(8,128)(2,1)S(1)}, u32[]{:S(2)}, u32[]{:S(2)}) collective-permute-start(bf16[4,48,3456]{2,1,0:T(8,128)(2,1)} %get-tuple-element.175), channel_id=1, source_target_pairs={{0,2},{1,3},{2,0},{3,1},{4,6},{5,7},{6,4},{7,5},{8,10},{9,11},{10,... | collective-permute-start | bytes 3981320 | tf_op jit(solution)/shard_map/ppermute | solution.py:805
  205.8 30.6 %collective-permute-start.31 = (bf16[4,48,3456]{2,1,0:T(8,128)(2,1)}, bf16[4,48,3456]{2,1,0:T(8,128)(2,1)}, u32[]{:S(2)}, u32[]{:S(2)}) collective-permute-start(bf16[4,48,3456]{2,1,0:T(8,128)(2,1)} %get-tuple-element.172), channel_id=1, source_target_pairs={{0,1},{1,0},{2,3},{3,2},{4,5},{5,4},{6,7},{7,6},{8,9},{9,8},{10,11... | collective-permute-start | bytes 3981320 | tf_op jit(solution)/shard_map/ppermute | solution.py:805
  252.9 20.0 %collective-permute-start.40 = (bf16[4,48,1152]{2,1,0:T(8,128)(2,1)S(1)}, bf16[4,48,1152]{2,1,0:T(8,128)(2,1)S(1)}, u32[]{:S(2)}, u32[]{:S(2)}) collective-permute-start(bf16[4,48,1152]{2,1,0:T(8,128)(2,1)S(1)} %get-tuple-element.197), channel_id=1, source_target_pairs={{0,2},{1,3},{2,0},{3,1},{4,6},{5,7},{6,4},{7,5},{8,10},{9,11},{10,... | collective-permute-start | bytes 1327112 | tf_op jit(solution)/shard_map/ppermute | solution.py:805
  254.1 18.8 %collective-permute-start.39 = (bf16[4,48,1152]{2,1,0:T(8,128)(2,1)S(1)}, bf16[4,48,1152]{2,1,0:T(8,128)(2,1)S(1)}, u32[]{:S(2)}, u32[]{:S(2)}) collective-permute-start(bf16[4,48,1152]{2,1,0:T(8,128)(2,1)S(1)} %get-tuple-element.183), channel_id=1, source_target_pairs={{0,2},{1,3},{2,0},{3,1},{4,6},{5,7},{6,4},{7,5},{8,10},{9,11},{10,... | collective-permute-start | bytes 1327112 | tf_op jit(solution)/shard_map/ppermute | solution.py:805
  255.7 17.2 %collective-permute-start.34 = (bf16[48,3456]{1,0:T(8,128)(2,1)}, bf16[48,3456]{1,0:T(8,128)(2,1)}, u32[]{:S(2)}, u32[]{:S(2)}) collective-permute-start(bf16[48,3456]{1,0:T(8,128)(2,1)} %get-tuple-element.190), channel_id=1, source_target_pairs={{0,4},{1,5},{2,6},{3,7},{4,8},{5,9},{6,10},{7,11},{8,12},{9,13},{1... | collective-permute-start | bytes 995336 | tf_op jit(solution)/shard_map/ppermute | solution.py:796
  255.7 17.2 %collective-permute-start.36 = (bf16[48,3456]{1,0:T(8,128)(2,1)}, bf16[48,3456]{1,0:T(8,128)(2,1)}, u32[]{:S(2)}, u32[]{:S(2)}) collective-permute-start(bf16[48,3456]{1,0:T(8,128)(2,1)} %get-tuple-element.192), channel_id=1, source_target_pairs={{0,12},{1,13},{2,14},{3,15},{4,0},{5,1},{6,2},{7,3},{8,4},{9,5},{1... | collective-permute-start | bytes 995336 | tf_op jit(solution)/shard_map/ppermute | solution.py:796
  276.6 18.9 %collective-permute-start.37 = (bf16[4,48,896]{2,1,0:T(8,128)(2,1)S(1)}, bf16[4,48,896]{2,1,0:T(8,128)(2,1)S(1)}, u32[]{:S(2)}, u32[]{:S(2)}) collective-permute-start(bf16[4,48,896]{2,1,0:T(8,128)(2,1)S(1)} %copy-done.42), channel_id=1, source_target_pairs={{0,2},{1,3},{2,0},{3,1},{4,6},{5,7},{6,4},{7,5},{8,10},{9,11},{10,... | collective-permute-start | bytes 1032200 | tf_op jit(solution)/shard_map/ppermute | solution.py:805
  277.7 17.8 %collective-permute-start.38 = (bf16[4,48,896]{2,1,0:T(8,128)(2,1)S(1)}, bf16[4,48,896]{2,1,0:T(8,128)(2,1)S(1)}, u32[]{:S(2)}, u32[]{:S(2)}) collective-permute-start(bf16[4,48,896]{2,1,0:T(8,128)(2,1)S(1)} %copy-done.41), channel_id=1, source_target_pairs={{0,2},{1,3},{2,0},{3,1},{4,6},{5,7},{6,4},{7,5},{8,10},{9,11},{10,... | collective-permute-start | bytes 1032200 | tf_op jit(solution)/shard_map/ppermute | solution.py:805
  278.6 16.9 %collective-permute-start.35 = (bf16[48,3456]{1,0:T(8,128)(2,1)S(1)}, bf16[48,3456]{1,0:T(8,128)(2,1)S(1)}, u32[]{:S(2)}, u32[]{:S(2)}) collective-permute-start(bf16[48,3456]{1,0:T(8,128)(2,1)S(1)} %copy-done.44), channel_id=1, source_target_pairs={{0,8},{1,9},{2,10},{3,11},{4,12},{5,13},{6,14},{7,15},{8,0},{9,1},... | collective-permute-start | bytes 995336 | tf_op jit(solution)/shard_map/ppermute | solution.py:796
  (88 other events, 777.9 us)

commit v3 on v2

--- a/solution.py
+++ b/solution.py
@@ -37,6 +37,13 @@
 
 def mm(a, b, dims=NN):
     return lax.dot_general(a, b, dims, preferred_element_type=F32)
+
+
+def in_parts(values):
+    high = values.astype(BF)
+    rest = values - high.astype(F32)
+    middle = rest.astype(BF)
+    return jnp.concatenate([high, middle, (rest - middle.astype(F32)).astype(BF)], axis=0)
 
 
 def swap_halves(v):
@@ -266,18 +273,18 @@
     x_ref, cond_ref, cos_ref, sin_ref, qkv_ref, first_ref, w_ref, mod_ref, flat_ref, modt, vecs, sems = refs[10:]
     step = pl.program_id(0)
 
+    small = unit_copies(units, order_ref, core_ref[0], sems, (
+        (vecs, 16, QKV_HALF + 3 * COND, 128, 16, 0, 0, 0, False),
+        (modt, 48, QKV_HALF, 128, 288, 144, 0, 0, True),
+        (modt, 48, QKV_HALF + 128, 128, 288, 144, 48, 0, True),
+        (modt, 48, QKV_HALF + 256, 128, 288, 144, 96, 0, True),
+    ), 0)
+    large = unit_copies(units, order_ref, core_ref[0], sems, (
+        (w_ref, 48, 0, QKV_HALF, 48, 0, 0, QKV_HALF, True),
+    ), len(small))
+
     @pl.when(step == 0)
     def _():
-        core = core_ref[0]
-        small = unit_copies(units, order_ref, core, sems, (
-            (vecs, 16, QKV_HALF + 3 * COND, 128, 16, 0, 0, 0, False),
-            (modt, 48, QKV_HALF, 128, 288, 144, 0, 0, True),
-            (modt, 48, QKV_HALF + 128, 128, 288, 144, 48, 0, True),
-            (modt, 48, QKV_HALF + 256, 128, 288, 144, 96, 0, True),
-        ), 0)
-        large = unit_copies(units, order_ref, core, sems, (
-            (w_ref, 48, 0, QKV_HALF, 48, 0, 0, QKV_HALF, True),
-        ), len(small))
         for copy in small + large:
             copy.start()
         for copy in small:
@@ -293,8 +300,6 @@
                 piece = jnp.where(lane >= turn, piece, 0.0)
             flat_ref[row : row + 5, :] += piece[:5]
         mod_ref[...] = mm(cond_ref[...], modt[...], NT) + line(flat_ref, (3 * D + FF) // 128, 6 * D // 128)
-        for copy in large:
-            copy.wait()
 
     gain = line(flat_ref, 0, D // 128)
     for part in range(rows // TILE):
@@ -306,6 +311,12 @@
         first_ref[at, :] = (normal * (gain * (1.0 + scale)) + shift).astype(BF)
     first = first_ref[...]
     cos, sin = cos_ref[...], sin_ref[...]
+
+    @pl.when(step == 0)
+    def _():
+        for copy in large:
+            copy.wait()
+
     for kind in range(3):
         mixed = mm(first, w_ref[:, kind * D : (kind + 1) * D])
         if kind < 2:
@@ -609,17 +620,16 @@
             sums[at, 3 * D : 4 * D] = sums_in[tile, 1:2, :]
             sums[at, 4 * D : 5 * D] = sums_in[tile, 2:3, :]
             sums[at, 5 * D : 6 * D] = sums_in[tile, 3:4, :]
-        member = member_ref[...]
-        scale_one = lax.dot_general(member, mod_ref[:, D : 2 * D], NN, precision=lax.Precision.HIGHEST, preferred_element_type=F32)
-        scale_two = lax.dot_general(member, mod_ref[:, 4 * D : 5 * D], NN, precision=lax.Precision.HIGHEST, preferred_element_type=F32)
+        member = member_ref[...].astype(BF)
+        scales = [mod_ref[pl.ds(tiles_ref[tile], 1), :] for tile in range(BLOCKS)]
+        scale_one = jnp.concatenate([scale[:, D : 2 * D] for scale in scales], axis=0)
+        scale_two = jnp.concatenate([scale[:, 4 * D : 5 * D] for scale in scales], axis=0)
         grad_gain_one = jnp.sum(sums[:, D : 2 * D] * (1.0 + scale_one), axis=0, keepdims=True)
         grad_gain_two = jnp.sum(sums[:, 4 * D : 5 * D] * (1.0 + scale_two), axis=0, keepdims=True)
         sums[:, D : 2 * D] = sums[:, D : 2 * D] * gain
         sums[:, 4 * D : 5 * D] = sums[:, 4 * D : 5 * D] * gain_two
-        by_segment = lax.dot_general(member, sums[...], TN, precision=lax.Precision.HIGHEST, preferred_element_type=F32)
-        grad_mod = lax.dot_general(
-            by_segment, cond_ref[...].astype(F32), TN, precision=lax.Precision.HIGHEST, preferred_element_type=F32
-        ).astype(BF).reshape(4, 4, 6, 48, COND)
+        by_segment = mm(jnp.concatenate([member] * 3, axis=0), in_parts(sums[...]), TN)
+        grad_mod = mm(in_parts(by_segment), jnp.concatenate([cond_ref[...]] * 3, axis=0), TN).astype(BF).reshape(4, 4, 6, 48, COND)
         for block in range(6):
             units[:, :, :, block * COND : (block + 1) * COND] = grad_mod[:, :, block]
         row = jnp.concatenate(
@@ -1102,6 +1112,7 @@
     if rounds:
         order = jnp.concatenate([jnp.asarray(ORIGIN)[core, chip], jnp.asarray(ORIGIN)[1 - core, chip]])
         places = jnp.asarray(PLACES)[core, chip]
+        order, places = lax.optimization_barrier((order, places))
         side = core[None].astype(jnp.int32)
         unit_first = pack_first(qkv_low, mod_low.T, vector_low[None], core)[0]
         unit_second = pack_second(out_low, up_low, down_low, core)[0]
@@ -1197,7 +1208,7 @@
         sent = sooner.send_first((grad_in, later.came[0], later.came[2]))
         sent = sooner.send_column(sent)
         sent = small.send_first((sent, later.came[1], sooner.came[0]))
-        sent = small.send_column((sent, sooner.came))
+        sent = small.send_column((sent, sooner.came[:2]))
         later_sums = later.finish(sent)
         (out_new, up_new, down_new), later_table = update_moments(
             update_later_kernel, side, later_sums, of_out + of_up + of_down

time: 346 us -> 345 us (level)
  no operation moved by 1% of the time
where the time goes in v3:
time: 345 us; the launch traced here: 340 us
  Pallas kernels  194 us (56%)
  waiting for transfers between devices  64.1 us (19%)
  starting transfers between devices  57.8 us (17%)
  other arithmetic  14.1 us (4%)
  local copies, waits for them, and re-layouts  8.94 us (3%)
    pallas_call x1, Pallas kernels, middle_part(): pl.pallas_call(functools.partial(middle_kernel, rows), grid=(SLOTS // row...  54.8 us
    pallas_call x3, Pallas kernels, attention_backward(): pl.pallas_call(functools.partial(attention_backward_kernel, block), grid=...  49.3 us
    ppermute x15, waiting for transfers between devices, along_z(): lax.ppermute(values, 'fsdp', [(chip, chip % 4 + 4 * ((chip // 4 + ahead)...  33.7 us
    ppermute x15, starting transfers between devices, along_z(): lax.ppermute(values, 'fsdp', [(chip, chip % 4 + 4 * ((chip // 4 + ahead)...  26.6 us
    pallas_call x3, Pallas kernels, attention_forward(): pl.pallas_call(functools.partial(attention_forward_kernel, block), grid=(...  25.3 us
    ppermute x19, waiting for transfers between devices, along_plane(): return lax.ppermute(values, ('rep', 'fsdp'), moves)  23 us
    pallas_call x6, Pallas kernels, column_sums(): pl.pallas_call(functools.partial(column_sums_kernel, counts), grid_spec=p...  21.9 us
    ppermute x19, starting transfers between devices, along_plane(): return lax.ppermute(values, ('rep', 'fsdp'), moves)  19.5 us
  transfers between devices with their start and end apart: 58, of which 22 were waited for; matrix products, arithmetic and copies ran while one was open for 4% of the time, Pallas kernels for 32%

profile of v3, /device:TPU:0, one launch (start us, length us, event | category | flops | bytes accessed | tf_op | source)
XLA Modules:
  0.0 340.2 jit_solution(2817129661479173312)
XLA Ops:
  3.4 5.1 %collective-permute-start.2 = (bf16[48,1664]{1,0:T(8,128)(2,1)S(1)}, bf16[48,1664]{1,0:T(8,128)(2,1)S(1)}, u32[]{:S(2)}, u32[]{:S(2)}) collective-permute-start(bf16[48,1664]{1,0:T(8,128)(2,1)S(1)} %maximum_bitcast_fusion), channel_id=1, source_target_pairs={{0,12},{1,13},{2,14},{3,15},{4,0},{5,1},{6,2},{7,3},{8,4},{9,5},{1... | collective-permute-start | bytes 479240 | tf_op jit(solution)/shard_map/ppermute | solution.py:806
  18.0 4.1 %collective-permute-done.1 = bf16[48,1664]{1,0:T(8,128)(2,1)S(1)} collective-permute-done((bf16[48,1664]{1,0:T(8,128)(2,1)S(1)}, bf16[48,1664]{1,0:T(8,128)(2,1)S(1)}, u32[]{:S(2)}, u32[]{:S(2)}) %collective-permute-start.1) | collective-permute-done | bytes 159776 | tf_op jit(solution)/shard_map/ppermute | solution.py:806
  33.6 5.6 %collective-permute-done.4.refs_2_ = bf16[4,48,1664]{2,1,0:T(8,128)(2,1)S(1)} collective-permute-done((bf16[4,48,1664]{2,1,0:T(8,128)(2,1)S(1)}, bf16[4,48,1664]{2,1,0:T(8,128)(2,1)S(1)}, u32[]{:S(2)}, u32[]{:S(2)}) %collective-permute-start.4) | collective-permute-done | bytes 639008 | tf_op jit(solution)/shard_map/ppermute | solution.py:815
  44.8 14.3 %collective-permute-done.10 = bf16[48,3456]{1,0:T(8,128)(2,1)S(1)} collective-permute-done((bf16[48,3456]{1,0:T(8,128)(2,1)S(1)}, bf16[48,3456]{1,0:T(8,128)(2,1)S(1)}, u32[]{:S(2)}, u32[]{:S(2)}) %collective-permute-start.10) | collective-permute-done | bytes 331808 | tf_op jit(solution)/shard_map/ppermute | solution.py:806
  66.2 12.3 %shard_map.409 = (bf16[1024,2304]{1,0:T(8,128)(2,1)}, bf16[1024,768]{1,0:T(8,128)(2,1)}, bf16[768,2304]{1,0:T(8,128)(2,1)}, f32[8,4608]{1,0:T(8,128)}, f32[80,128]{1,0:T(8,128)}) custom-call(s32[32]{0:T(128)} %pad_add_fusion.order_ref, s32[1]{0:T(128)} %bitcast.3.core_ref.side_ref, s32[8]{0:T(128)} %get-tuple-element.264.tiles_ref, ...), custom_call_target="tpu_custom_call" | custom-call | flops 3623878656 | bytes 20971520 | tf_op jit(solution)/shard_map/pallas_call | solution.py:337
  78.6 8.5 %shard_map.410 = (bf16[1024,768]{1,0:T(8,128)(2,1)}, bf16[1024,768]{1,0:T(8,128)(2,1)}) custom-call(bf16[1024,2304]{1,0:T(8,128)(2,1)} %get-tuple-element.149.q_ref.k_ref.v_ref, bf16[1024,2304]{1,0:T(8,128)(2,1)} %get-tuple-element.149.q_ref.k_ref.v_ref, bf16[1024,2304]{1,0:T(8,128)(2,1)} %get-tuple-element.149.q_ref.k_ref.v_ref, ...), custom_call_target="tpu_custom_call" | custom-call | flops 12582912000 | bytes 2621440 | tf_op jit(solution)/shard_map/pallas_call | solution.py:104
  91.7 11.6 %shard_map.411 = (bf16[1024,768]{1,0:T(8,128)(2,1)}, bf16[1024,768]{1,0:T(8,128)(2,1)}) custom-call(bf16[1024,2304]{1,0:T(8,128)(2,1)} %get-tuple-element.149.q_ref.k_ref.v_ref, bf16[1024,2304]{1,0:T(8,128)(2,1)} %get-tuple-element.149.q_ref.k_ref.v_ref, ...), custom_call_target="tpu_custom_call", output_to_operand_aliasing={{0}: (5, {}), {1}: (6, {})} | custom-call | flops 18874368000 | bytes 3932160 | tf_op jit(solution)/shard_map/pallas_call | solution.py:104
  104.7 5.2 %shard_map.412 = (bf16[1024,768]{1,0:T(8,128)(2,1)}, bf16[1024,768]{1,0:T(8,128)(2,1)}) custom-call(bf16[1024,2304]{1,0:T(8,128)(2,1)} %get-tuple-element.149.q_ref.k_ref.v_ref, bf16[1024,2304]{1,0:T(8,128)(2,1)} %get-tuple-element.149.q_ref.k_ref.v_ref, ...), custom_call_target="tpu_custom_call", output_to_operand_aliasing={{0}: (5, {}), {1}: (6, {})} | custom-call | flops 6291456000 | bytes 1310720 | tf_op jit(solution)/shard_map/pallas_call | solution.py:104
  109.9 54.8 %shard_map.413 = (bf16[1024,768]{1,0:T(8,128)(2,1)}, f32[1024,768]{1,0:T(8,128)}, bf16[1024,768]{1,0:T(8,128)(2,1)}, f32[8,8,768]{2,1,0:T(8,128)}, f32[8,3840]{1...) custom-call(s32[32]{0:T(128)} %pad_add_fusion.order_ref, s32[1]{0:T(128)} %bitcast.3.core_ref.side_ref, ...), custom_call_target="tpu_custom_call" | custom-call | flops 32614907904 | bytes 52428800 | tf_op jit(solution)/shard_map/pallas_call | solution.py:532
  165.2 9.5 %shard_map.414.refs_0_ = bf16[3,1024,768]{2,1,0:T(8,128)(2,1)} custom-call(bf16[1024,2304]{1,0:T(8,128)(2,1)} %get-tuple-element.149.q_ref.k_ref.v_ref, bf16[1024,2304]{1,0:T(8,128)(2,1)} %get-tuple-element.149.q_ref.k_ref.v_ref, bf16[1024,2304]{1,0:T(8,128)(2,1)} %get-tuple-element.149.q_ref.k_ref.v_ref, bf16[1024,768]{1,0:T(8,128)(2,1)} %get-tuple-element.169.fo_ref, ...), custom_call_target="tpu_custom_call" | custom-call | flops 4194304000 | bytes 2621440 | tf_op jit(solution)/shard_map/pallas_call | solution.py:182
  174.7 4.5 %shard_map.415 = bf16[4,48,3456]{2,1,0:T(8,128)(2,1)} custom-call(s32[8]{0:T(128)} %fusion.9.places_ref.refs_0_, bf16[4,4,48,3456]{3,2,1,0:T(8,128)(2,1)} %bitcast.92, bf16[4,4,48,3456]{3,2,1,0:T(8,128)(2,1)} %bitcast.38.refs_1_), custom_call_target="tpu_custom_call" | custom-call | bytes 12582912 | tf_op jit(solution)/shard_map/pallas_call | solution.py:872
  179.7 16.4 %shard_map.416.refs_0_ = bf16[3,1024,768]{2,1,0:T(8,128)(2,1)} custom-call(bf16[1024,2304]{1,0:T(8,128)(2,1)} %get-tuple-element.149.q_ref.k_ref.v_ref, bf16[1024,2304]{1,0:T(8,128)(2,1)} %get-tuple-element.149.q_ref.k_ref.v_ref, bf16[1024,2304]{1,0:T(8,128)(2,1)} %get-tuple-element.149.q_ref.k_ref.v_ref, ...), custom_call_target="tpu_custom_call", output_to_operand_aliasing={{}: (9, {})} | custom-call | flops 8388608000 | bytes 5242880 | tf_op jit(solution)/shard_map/pallas_call | solution.py:182
  198.2 5.6 %shard_map.417 = (bf16[4,48,3456]{2,1,0:T(8,128)(2,1)}, bf16[4,48,3456]{2,1,0:T(8,128)(2,1)}) custom-call(s32[8]{0:T(128)} %fusion.9.places_ref.refs_0_, bf16[4,4,48,3456]{3,2,1,0:T(8,128)(2,1)} %bitcast.93, bf16[4,4,48,3456]{3,2,1,0:T(8,128)(2,1)} %bitcast.37.refs_1_.refs_4_.refs_5_.refs_9_.refs_13_, bf16[4,48,3456]{2,1,0:T(8,128)(2,1)} %copy-done.23, ...), custom_call_target="tpu_custom_call" | custom-call | bytes 12582912 | tf_op jit(solution)/shard_map/pallas_call | solution.py:872
  205.4 23.4 %shard_map.418.g_ref = bf16[3,1024,768]{2,1,0:T(8,128)(2,1)} custom-call(bf16[1024,2304]{1,0:T(8,128)(2,1)} %get-tuple-element.149.q_ref.k_ref.v_ref, bf16[1024,2304]{1,0:T(8,128)(2,1)} %get-tuple-element.149.q_ref.k_ref.v_ref, bf16[1024,2304]{1,0:T(8,128)(2,1)} %get-tuple-element.149.q_ref.k_ref.v_ref, ...), custom_call_target="tpu_custom_call", output_to_operand_aliasing={{}: (9, {})} | custom-call | flops 12582912000 | bytes 7864320 | tf_op jit(solution)/shard_map/pallas_call | solution.py:182
  228.8 6.3 %collective-permute-done.32.refs_3_.refs_7_.refs_11_.refs_15_ = bf16[4,48,3456]{2,1,0:T(8,128)(2,1)S(1)} collective-permute-done((bf16[4,48,3456]{2,1,0:T(8,128)(2,1)}, bf16[4,48,3456]{2,1,0:T(8,128)(2,1)S(1)}, u32[]{:S(2)}, u32[]{:S(2)}) %collective-permute-start.32) | collective-permute-done | bytes 1327136 | tf_op jit(solution)/shard_map/ppermute | solution.py:815
  235.1 8.9 %shard_map.419 = (bf16[16,48,1152]{2,1,0:T(8,128)(2,1)}, bf16[16,48,1152]{2,1,0:T(8,128)(2,1)}) custom-call(s32[1]{0:T(128)} %bitcast.3.core_ref.side_ref, bf16[1024,768]{1,0:T(8,128)(2,1)} %get-tuple-element.178.first_ref, bf16[3,1024,768]{2,1,0:T(8,128)(2,1)} %shard_map.418.g_ref), custom_call_target="tpu_custom_call" | custom-call | flops 603979776 | bytes 1048576 | tf_op jit(solution)/shard_map/pallas_call | solution.py:580
  244.1 4.7 %shard_map.420 = (bf16[48,3456]{1,0:T(8,128)(2,1)}, bf16[48,3456]{1,0:T(8,128)(2,1)}, bf16[48,3456]{1,0:T(8,128)(2,1)}, bf16[48,3456]{1,0:T(8,128)(2,1)}) custom-call(s32[8]{0:T(128)} %fusion.9.places_ref.refs_0_, bf16[4,4,48,3456]{3,2,1,0:T(8,128)(2,1)} %bitcast.95, bf16[4,4,48,3456]{3,2,1,0:T(8,128)(2,1)} %bitcast.37.refs_1_.refs_4_.refs_5_.refs_9_.refs_13_, ...), custom_call_target="tpu_custom_call" | custom-call | bytes 209715200 | tf_op jit(solution)/shard_map/pallas_call | solution.py:872
  254.3 3.8 %collective-permute-start.36 = (bf16[48,3456]{1,0:T(8,128)(2,1)}, bf16[48,3456]{1,0:T(8,128)(2,1)}, u32[]{:S(2)}, u32[]{:S(2)}) collective-permute-start(bf16[48,3456]{1,0:T(8,128)(2,1)} %get-tuple-element.196), channel_id=1, source_target_pairs={{0,12},{1,13},{2,14},{3,15},{4,0},{5,1},{6,2},{7,3},{8,4},{9,5},{1... | collective-permute-start | bytes 995336 | tf_op jit(solution)/shard_map/ppermute | solution.py:806
  258.1 11.7 %shard_map.422 = (f32[1024,768]{1,0:T(8,128)}, bf16[4,48,896]{2,1,0:T(8,128)(2,1)}, bf16[4,48,896]{2,1,0:T(8,128)(2,1)}, bf16[4,48,896]{2,1,0:T(8,128)(2,1)}, bf16[4,48,896]{2,1,0:T(8,128)(2,1)}) custom-call(s32[8]{0:T(128)} %fusion.9.places_ref.refs_0_, s32[8]{0:T(128)} %get-tuple-element.264.tiles_ref, f32[8,8]{1,0:T(8,128)} %convert_bitcast_fusion.member_ref, ...), custom_call_target="tpu_custom_call" | custom-call | flops 3623878656 | bytes 31457280 | tf_op jit(solution)/shard_map/pallas_call | solution.py:673
  279.4 7.7 %collective-permute-done.41.refs_2_.refs_6_.refs_10_.refs_14_ = bf16[4,48,1152]{2,1,0:T(8,128)(2,1)S(1)} collective-permute-done((bf16[4,48,1152]{2,1,0:T(8,128)(2,1)S(1)}, bf16[4,48,1152]{2,1,0:T(8,128)(2,1)S(1)}, u32[]{:S(2)}, u32[]{:S(2)}) %collective-permute-start.41) | collective-permute-done | bytes 442400 | tf_op jit(solution)/shard_map/ppermute | solution.py:815
  289.7 4.2 %collective-permute-done.35 = bf16[48,3456]{1,0:T(8,128)(2,1)S(1)} collective-permute-done((bf16[48,3456]{1,0:T(8,128)(2,1)S(1)}, bf16[48,3456]{1,0:T(8,128)(2,1)S(1)}, u32[]{:S(2)}, u32[]{:S(2)}) %collective-permute-start.35) | collective-permute-done | bytes 331808 | tf_op jit(solution)/shard_map/ppermute | solution.py:806
  297.9 5.3 %collective-permute-done.44 = bf16[48,1152]{1,0:T(8,128)(2,1)S(1)} collective-permute-done((bf16[48,1152]{1,0:T(8,128)(2,1)S(1)}, bf16[48,1152]{1,0:T(8,128)(2,1)S(1)}, u32[]{:S(2)}, u32[]{:S(2)}) %collective-permute-start.44) | collective-permute-done | bytes 110624 | tf_op jit(solution)/shard_map/ppermute | solution.py:806
  311.9 3.5 %collective-permute-start.50 = (bf16[48,896]{1,0:T(8,128)(2,1)}, bf16[48,896]{1,0:T(8,128)(2,1)S(1)}, u32[]{:S(2)}, u32[]{:S(2)}) collective-permute-start(bf16[48,896]{1,0:T(8,128)(2,1)} %get-tuple-element.223), channel_id=1, source_target_pairs={{0,12},{1,13},{2,14},{3,15},{4,0},{5,1},{6,2},{7,3},{8,4},{9,5},{1... | collective-permute-start | bytes 258056 | tf_op jit(solution)/shard_map/ppermute | solution.py:806
  315.4 3.3 shard_map.426
  (273 shorter events, 98.3 us)
Async XLA Ops:
  3.4 14.5 %collective-permute-start.2 = (bf16[48,1664]{1,0:T(8,128)(2,1)S(1)}, bf16[48,1664]{1,0:T(8,128)(2,1)S(1)}, u32[]{:S(2)}, u32[]{:S(2)}) collective-permute-start(bf16[48,1664]{1,0:T(8,128)(2,1)S(1)} %maximum_bitcast_fusion), channel_id=1, source_target_pairs={{0,12},{1,13},{2,14},{3,15},{4,0},{5,1},{6,2},{7,3},{8,4},{9,5},{1... | collective-permute-start | bytes 479240 | tf_op jit(solution)/shard_map/ppermute | solution.py:806
  12.0 17.4 %collective-permute-start.6 = (bf16[1,48,3456]{2,1,0:T(8,128)(2,1)S(1)}, bf16[1,48,3456]{2,1,0:T(8,128)(2,1)S(1)}, u32[]{:S(2)}, u32[]{:S(2)}) collective-permute-start(bf16[1,48,3456]{2,1,0:T(8,128)(2,1)S(1)} %get-tuple-element.155.refs_0_), channel_id=1, source_target_pairs={{0,2},{1,3},{2,0},{3,1},{4,6},{5,7},{6,4},{7,5},{8,10},{9,11},{10,... | collective-permute-start | bytes 995336 | tf_op jit(solution)/shard_map/ppermute | solution.py:815
  13.6 17.5 %collective-permute-start.5 = (bf16[1,48,3456]{2,1,0:T(8,128)(2,1)S(1)}, bf16[1,48,3456]{2,1,0:T(8,128)(2,1)S(1)}, u32[]{:S(2)}, u32[]{:S(2)}) collective-permute-start(bf16[1,48,3456]{2,1,0:T(8,128)(2,1)S(1)} %get-tuple-element.155.refs_0_), channel_id=1, source_target_pairs={{0,1},{1,0},{2,3},{3,2},{4,5},{5,4},{6,7},{7,6},{8,9},{9,8},{10,11... | collective-permute-start | bytes 995336 | tf_op jit(solution)/shard_map/ppermute | solution.py:815
  22.2 17.1 %collective-permute-start.4 = (bf16[4,48,1664]{2,1,0:T(8,128)(2,1)S(1)}, bf16[4,48,1664]{2,1,0:T(8,128)(2,1)S(1)}, u32[]{:S(2)}, u32[]{:S(2)}) collective-permute-start(bf16[4,48,1664]{2,1,0:T(8,128)(2,1)S(1)} %pad_maximum_fusion.1.refs_0_), channel_id=1, source_target_pairs={{0,2},{1,3},{2,0},{3,1},{4,6},{5,7},{6,4},{7,5},{8,10},{9,11},{10,... | collective-permute-start | bytes 1916936 | tf_op jit(solution)/shard_map/ppermute | solution.py:815
  23.7 15.5 %collective-permute-start.3 = (bf16[4,48,1664]{2,1,0:T(8,128)(2,1)S(1)}, bf16[4,48,1664]{2,1,0:T(8,128)(2,1)S(1)}, u32[]{:S(2)}, u32[]{:S(2)}) collective-permute-start(bf16[4,48,1664]{2,1,0:T(8,128)(2,1)S(1)} %pad_maximum_fusion.1.refs_0_), channel_id=1, source_target_pairs={{0,1},{1,0},{2,3},{3,2},{4,5},{5,4},{6,7},{7,6},{8,9},{9,8},{10,11... | collective-permute-start | bytes 1916936 | tf_op jit(solution)/shard_map/ppermute | solution.py:815
  29.4 29.6 %collective-permute-start.10 = (bf16[48,3456]{1,0:T(8,128)(2,1)S(1)}, bf16[48,3456]{1,0:T(8,128)(2,1)S(1)}, u32[]{:S(2)}, u32[]{:S(2)}) collective-permute-start(bf16[48,3456]{1,0:T(8,128)(2,1)S(1)} %get-tuple-element.138), channel_id=1, source_target_pairs={{0,8},{1,9},{2,10},{3,11},{4,12},{5,13},{6,14},{7,15},{8,0},{9,1},... | collective-permute-start | bytes 995336 | tf_op jit(solution)/shard_map/ppermute | solution.py:806
  31.2 27.9 %collective-permute-start.9 = (bf16[48,3456]{1,0:T(8,128)(2,1)S(1)}, bf16[48,3456]{1,0:T(8,128)(2,1)S(1)}, u32[]{:S(2)}, u32[]{:S(2)}) collective-permute-start(bf16[48,3456]{1,0:T(8,128)(2,1)S(1)} %get-tuple-element.138), channel_id=1, source_target_pairs={{0,4},{1,5},{2,6},{3,7},{4,8},{5,9},{6,10},{7,11},{8,12},{9,13},{1... | collective-permute-start | bytes 995336 | tf_op jit(solution)/shard_map/ppermute | solution.py:806
  39.3 19.7 %collective-permute-start.8 = (bf16[2,48,1664]{2,1,0:T(8,128)(2,1)S(1)}, bf16[2,48,1664]{2,1,0:T(8,128)(2,1)S(1)}, u32[]{:S(2)}, u32[]{:S(2)}) collective-permute-start(bf16[2,48,1664]{2,1,0:T(8,128)(2,1)S(1)} %get-tuple-element.254), channel_id=1, source_target_pairs={{0,2},{1,3},{2,0},{3,1},{4,6},{5,7},{6,4},{7,5},{8,10},{9,11},{10,... | collective-permute-start | bytes 958472 | tf_op jit(solution)/shard_map/ppermute | solution.py:815
  40.9 18.1 %collective-permute-start.7 = (bf16[2,48,1664]{2,1,0:T(8,128)(2,1)S(1)}, bf16[2,48,1664]{2,1,0:T(8,128)(2,1)S(1)}, u32[]{:S(2)}, u32[]{:S(2)}) collective-permute-start(bf16[2,48,1664]{2,1,0:T(8,128)(2,1)S(1)} %get-tuple-element.255), channel_id=1, source_target_pairs={{0,2},{1,3},{2,0},{3,1},{4,6},{5,7},{6,4},{7,5},{8,10},{9,11},{10,... | collective-permute-start | bytes 958472 | tf_op jit(solution)/shard_map/ppermute | solution.py:815
  42.0 20.6 %collective-permute-start.14 = (bf16[1,48,3456]{2,1,0:T(8,128)(2,1)S(1)}, bf16[1,48,3456]{2,1,0:T(8,128)(2,1)}, u32[]{:S(2)}, u32[]{:S(2)}) collective-permute-start(bf16[1,48,3456]{2,1,0:T(8,128)(2,1)S(1)} %collective-permute-done.5.refs_2_), channel_id=1, source_target_pairs={{0,2},{1,3},{2,0},{3,1},{4,6},{5,7},{6,4},{7,5},{8,10},{9,11},{10,... | collective-permute-start | bytes 995336 | tf_op jit(solution)/shard_map/ppermute | solution.py:815
  63.9 24.9 %collective-permute-start.13 = (bf16[3,48,3456]{2,1,0:T(8,128)(2,1)S(1)}, bf16[3,48,3456]{2,1,0:T(8,128)(2,1)}, u32[]{:S(2)}, u32[]{:S(2)}) collective-permute-start(bf16[3,48,3456]{2,1,0:T(8,128)(2,1)S(1)} %pad_maximum_fusion.refs_1_), channel_id=1, source_target_pairs={{0,2},{1,3},{2,0},{3,1},{4,6},{5,7},{6,4},{7,5},{8,10},{9,11},{10,... | collective-permute-start | bytes 2985992 | tf_op jit(solution)/shard_map/ppermute | solution.py:815
  64.4 24.3 %collective-permute-start.12 = (bf16[3,48,3456]{2,1,0:T(8,128)(2,1)S(1)}, bf16[3,48,3456]{2,1,0:T(8,128)(2,1)}, u32[]{:S(2)}, u32[]{:S(2)}) collective-permute-start(bf16[3,48,3456]{2,1,0:T(8,128)(2,1)S(1)} %pad_maximum_fusion.refs_1_), channel_id=1, source_target_pairs={{0,1},{1,0},{2,3},{3,2},{4,5},{5,4},{6,7},{7,6},{8,9},{9,8},{10,11... | collective-permute-start | bytes 2985992 | tf_op jit(solution)/shard_map/ppermute | solution.py:815
  65.0 25.0 %collective-permute-start.27 = (bf16[1,48,3456]{2,1,0:T(8,128)(2,1)}, bf16[1,48,3456]{2,1,0:T(8,128)(2,1)}, u32[]{:S(2)}, u32[]{:S(2)}) collective-permute-start(bf16[1,48,3456]{2,1,0:T(8,128)(2,1)} %collective-permute-done.14.refs_6_), channel_id=1, source_target_pairs={{0,16},{16,0},{1,17},{17,1},{2,18},{18,2},{3,19},{19,3},{4,20},{20... | collective-permute-start | bytes 995336 | tf_op jit(solution)/shard_map/ppermute | solution.py:819
  89.4 14.5 %collective-permute-start.20 = (bf16[3,48,3456]{2,1,0:T(8,128)(2,1)}, bf16[3,48,3456]{2,1,0:T(8,128)(2,1)}, u32[]{:S(2)}, u32[]{:S(2)}) collective-permute-start(bf16[3,48,3456]{2,1,0:T(8,128)(2,1)} %collective-permute-done.12.refs_3_), channel_id=1, source_target_pairs={{0,2},{1,3},{2,0},{3,1},{4,6},{5,7},{6,4},{7,5},{8,10},{9,11},{10,... | collective-permute-start | bytes 2985992 | tf_op jit(solution)/shard_map/ppermute | solution.py:815
  179.1 18.0 %collective-permute-start.30 = (bf16[4,48,3456]{2,1,0:T(8,128)(2,1)}, bf16[4,48,3456]{2,1,0:T(8,128)(2,1)S(1)}, u32[]{:S(2)}, u32[]{:S(2)}) collective-permute-start(bf16[4,48,3456]{2,1,0:T(8,128)(2,1)} %shard_map.415), channel_id=1, source_target_pairs={{0,2},{1,3},{2,0},{3,1},{4,6},{5,7},{6,4},{7,5},{8,10},{9,11},{10,... | collective-permute-start | bytes 3981320 | tf_op jit(solution)/shard_map/ppermute | solution.py:815
  203.8 31.2 %collective-permute-start.32 = (bf16[4,48,3456]{2,1,0:T(8,128)(2,1)}, bf16[4,48,3456]{2,1,0:T(8,128)(2,1)S(1)}, u32[]{:S(2)}, u32[]{:S(2)}) collective-permute-start(bf16[4,48,3456]{2,1,0:T(8,128)(2,1)} %get-tuple-element.179), channel_id=1, source_target_pairs={{0,2},{1,3},{2,0},{3,1},{4,6},{5,7},{6,4},{7,5},{8,10},{9,11},{10,... | collective-permute-start | bytes 3981320 | tf_op jit(solution)/shard_map/ppermute | solution.py:815
  204.4 30.7 %collective-permute-start.31 = (bf16[4,48,3456]{2,1,0:T(8,128)(2,1)}, bf16[4,48,3456]{2,1,0:T(8,128)(2,1)}, u32[]{:S(2)}, u32[]{:S(2)}) collective-permute-start(bf16[4,48,3456]{2,1,0:T(8,128)(2,1)} %get-tuple-element.176), channel_id=1, source_target_pairs={{0,1},{1,0},{2,3},{3,2},{4,5},{5,4},{6,7},{7,6},{8,9},{9,8},{10,11... | collective-permute-start | bytes 3981320 | tf_op jit(solution)/shard_map/ppermute | solution.py:815
  251.5 19.8 %collective-permute-start.40 = (bf16[4,48,1152]{2,1,0:T(8,128)(2,1)S(1)}, bf16[4,48,1152]{2,1,0:T(8,128)(2,1)S(1)}, u32[]{:S(2)}, u32[]{:S(2)}) collective-permute-start(bf16[4,48,1152]{2,1,0:T(8,128)(2,1)S(1)} %get-tuple-element.201), channel_id=1, source_target_pairs={{0,2},{1,3},{2,0},{3,1},{4,6},{5,7},{6,4},{7,5},{8,10},{9,11},{10,... | collective-permute-start | bytes 1327112 | tf_op jit(solution)/shard_map/ppermute | solution.py:815
  252.5 18.9 %collective-permute-start.39 = (bf16[4,48,1152]{2,1,0:T(8,128)(2,1)S(1)}, bf16[4,48,1152]{2,1,0:T(8,128)(2,1)S(1)}, u32[]{:S(2)}, u32[]{:S(2)}) collective-permute-start(bf16[4,48,1152]{2,1,0:T(8,128)(2,1)S(1)} %get-tuple-element.187), channel_id=1, source_target_pairs={{0,2},{1,3},{2,0},{3,1},{4,6},{5,7},{6,4},{7,5},{8,10},{9,11},{10,... | collective-permute-start | bytes 1327112 | tf_op jit(solution)/shard_map/ppermute | solution.py:815
  254.3 15.6 %collective-permute-start.34 = (bf16[48,3456]{1,0:T(8,128)(2,1)}, bf16[48,3456]{1,0:T(8,128)(2,1)}, u32[]{:S(2)}, u32[]{:S(2)}) collective-permute-start(bf16[48,3456]{1,0:T(8,128)(2,1)} %get-tuple-element.194), channel_id=1, source_target_pairs={{0,4},{1,5},{2,6},{3,7},{4,8},{5,9},{6,10},{7,11},{8,12},{9,13},{1... | collective-permute-start | bytes 995336 | tf_op jit(solution)/shard_map/ppermute | solution.py:806
  254.3 17.1 %collective-permute-start.36 = (bf16[48,3456]{1,0:T(8,128)(2,1)}, bf16[48,3456]{1,0:T(8,128)(2,1)}, u32[]{:S(2)}, u32[]{:S(2)}) collective-permute-start(bf16[48,3456]{1,0:T(8,128)(2,1)} %get-tuple-element.196), channel_id=1, source_target_pairs={{0,12},{1,13},{2,14},{3,15},{4,0},{5,1},{6,2},{7,3},{8,4},{9,5},{1... | collective-permute-start | bytes 995336 | tf_op jit(solution)/shard_map/ppermute | solution.py:806
  275.0 18.9 %collective-permute-start.37 = (bf16[4,48,896]{2,1,0:T(8,128)(2,1)S(1)}, bf16[4,48,896]{2,1,0:T(8,128)(2,1)S(1)}, u32[]{:S(2)}, u32[]{:S(2)}) collective-permute-start(bf16[4,48,896]{2,1,0:T(8,128)(2,1)S(1)} %copy-done.42), channel_id=1, source_target_pairs={{0,2},{1,3},{2,0},{3,1},{4,6},{5,7},{6,4},{7,5},{8,10},{9,11},{10,... | collective-permute-start | bytes 1032200 | tf_op jit(solution)/shard_map/ppermute | solution.py:815
  275.9 18.0 %collective-permute-start.38 = (bf16[4,48,896]{2,1,0:T(8,128)(2,1)S(1)}, bf16[4,48,896]{2,1,0:T(8,128)(2,1)S(1)}, u32[]{:S(2)}, u32[]{:S(2)}) collective-permute-start(bf16[4,48,896]{2,1,0:T(8,128)(2,1)S(1)} %copy-done.41), channel_id=1, source_target_pairs={{0,2},{1,3},{2,0},{3,1},{4,6},{5,7},{6,4},{7,5},{8,10},{9,11},{10,... | collective-permute-start | bytes 1032200 | tf_op jit(solution)/shard_map/ppermute | solution.py:815
  277.0 16.9 %collective-permute-start.35 = (bf16[48,3456]{1,0:T(8,128)(2,1)S(1)}, bf16[48,3456]{1,0:T(8,128)(2,1)S(1)}, u32[]{:S(2)}, u32[]{:S(2)}) collective-permute-start(bf16[48,3456]{1,0:T(8,128)(2,1)S(1)} %copy-done.45), channel_id=1, source_target_pairs={{0,8},{1,9},{2,10},{3,11},{4,12},{5,13},{6,14},{7,15},{8,0},{9,1},... | collective-permute-start | bytes 995336 | tf_op jit(solution)/shard_map/ppermute | solution.py:806
  (87 other events, 864.8 us)
